TPU v7x, 128 devices: a whole 4x4x4 slice. The times are simulated.
128 devices in a mesh: dp: 16 (over z, y_hi, core), layer: 8 (over x, y_lo).
Axes of the slice: x: 4, y: 4 (y_hi: 2, y_lo: 2; y = y_hi * 2 + y_lo), z: 4, core: 2. Of those that a mesh axis runs over, the one named last changes fastest.
Arguments:
- grads_proj: bfloat16 [8, 4096, 64, 256], P('layer', 'dp'), may hold values from -6 to 6
- inputs_proj: bfloat16 [8, 4096, 64, 256], P('layer', 'dp'), may hold values from -6 to 6
Outputs:
- gram: float32 [4096, 4096], P('dp', 'layer')
All inputs are finite; a program needn't handle non-finite values.
Results may differ from a plain program's by a relative error of at most 0.002.
Values may be sent and summed in bfloat16 or wider, within the bound.
No kernel may reach another device: no remote copies, remote signals or barrier semaphores. Data moves between devices by JAX's collectives and lax.ppermute only.
A program may use at most 128 MiB of HBM per device.

v0:
```python
import jax
import jax.numpy as jnp
from jax import lax
from jax.sharding import PartitionSpec as P


def contract(left, right):
    return lax.dot_general(
        left, right, (((1,), (1,)), ((), ())), preferred_element_type=jnp.float32
    )


def body(grads_proj, inputs_proj):
    local_layers = grads_proj.shape[0]
    examples = grads_proj.shape[1]
    tokens = grads_proj.shape[3]
    rank_width = grads_proj.shape[2]
    all_layers = local_layers * lax.axis_size("layer")
    prod = jnp.einsum(
        "leot,leit->eloi", grads_proj, inputs_proj, preferred_element_type=jnp.float32
    )
    prod = prod * (1.0 / jnp.sqrt(jnp.float32(tokens)))
    features = prod.astype(jnp.bfloat16).reshape(examples, local_layers * rank_width * rank_width)
    partial_gram = contract(features, lax.all_gather(features, "dp", axis=0, tiled=True))
    summed = lax.psum_scatter(partial_gram, "layer", scatter_dimension=1, tiled=True)
    return summed * (1.0 / jnp.sqrt(jnp.float32(all_layers * rank_width * rank_width)))


def solution(mesh):
    return jax.shard_map(
        body,
        mesh=mesh,
        in_specs=(P("layer", "dp", None, None), P("layer", "dp", None, None)),
        out_specs=P("dp", "layer"),
        check_vma=False,
    )
```

profile of v0, /device:TPU:104, one launch (start us, length us, event | category | flops | bytes accessed | tf_op | source)
XLA Modules:
  0.0 339.6 jit_solution(12346431570289781996)
XLA Ops:
  6.5 0.0 all-gather.2.cloned.1.call-start
  6.5 10.0 %multiply_convert_fusion = bf16[256,64,64]{2,1,0:T(8,128)(2,1)} fusion(bf16[1,256,64,256]{3,2,1,0:T(8,128)(2,1)} %param.3, bf16[1,256,64,256]{3,2,1,0:T(8,128)(2,1)} %param.2), kind=kOutput, calls=%fused_computation.3 | convolution fusion | flops 538968064 | bytes 18874368 | tf_op jit(solution)/shard_map/leot,leit->eloi/dot_general | solution.py:19
  16.6 5.9 %copy.3 = bf16[256,64,64]{0,2,1:T(8,128)(2,1)} copy(bf16[256,64,64]{2,1,0:T(8,128)(2,1)} %multiply_convert_fusion) | data formatting | bytes 4194304 | tf_op jit(solution)/shard_map/convert_element_type | solution.py:23
  22.5 0.0 all-gather.2.cloned.1.call-update
  22.5 0.0 reduce-scatter.2.cloned.1.call-start
  22.5 201.7 %all-gather.2.cloned.1.call-done = bf16[4096,4096]{0,1:T(8,128)(2,1)} async-done(((bf16[256,4096]{0,1:T(8,128)(2,1)}), bf16[4096,4096]{0,1:T(8,128)(2,1)}) %all-gather.2.cloned.1.call-update) | async-done | bytes 33554448 | tf_op jit(solution)/shard_map/all_gather | solution.py:24
  224.3 17.0 %fusion.7 = f32[256,4096]{1,0:T(8,128)} fusion(bf16[256,4096]{0,1:T(8,128)(2,1)} %bitcast.14, bf16[4096,4096]{0,1:T(8,128)(2,1)} %all-gather.2.cloned.1.call-done), kind=kOutput, calls=%fused_computation.5 | convolution fusion | flops 8589934592 | bytes 39845888 | tf_op jit(solution)/shard_map/dot_general | solution.py:8
  241.3 0.0 reduce-scatter.2.cloned.1.call-update
  241.3 89.5 %reduce-scatter.2.cloned.1.call-done = f32[256,512]{1,0:T(8,128)} async-done(((f32[256,4096]{1,0:T(8,128)}), f32[256,512]{1,0:T(8,128)}) %reduce-scatter.2.cloned.1.call-update) | async-done | bytes 524304 | tf_op jit(solution)/shard_map/reduce_scatter | solution.py:25
  330.8 1.9 broadcast_multiply_fusion
Async XLA Ops:
  6.5 217.7 %all-gather.2.cloned.1.call-start = ((), (), s32[]{:S(2)}) async-start(), calls=%async_computation.1 | async-start | bytes 35651584 | tf_op jit(solution)/shard_map/all_gather | solution.py:24
  22.5 308.3 %reduce-scatter.2.cloned.1.call-start = ((), (), s32[]{:S(2)}) async-start(), calls=%async_computation.2 | async-start | bytes 4718592 | tf_op jit(solution)/shard_map/reduce_scatter | solution.py:25
Sparse Core Ops, SparseCore 0:
  22.6 201.6 all-gather.1
  241.4 89.3 reduce-scatter.1
where the time goes:
time: 343 us; the launch traced here: 340 us
  waiting for transfers between devices  291 us (85%)
  matrix products  27 us (8%)
  between operations  13.4 us (4%)
  local copies, waits for them, and re-layouts  5.88 us (2%)
    all_gather x1, waiting for transfers between devices, body(): lax.all_gather(features, 'dp', axis=0, tiled=True)  202 us
    reduce_scatter x1, waiting for transfers between devices, body(): lax.psum_scatter(partial_gram, 'layer', scatter_dimension=1, tiled=True)  89.5 us
    dot_general x1, matrix products, contract(): lax.dot_general(left, right, (((1,), (1,)), ((), ())), preferred_element_...  17 us
    dot_general x1, matrix products, body(): jnp.einsum('leot,leit->eloi', grads_proj, inputs_proj, preferred_element_...  10 us
  transfers between devices with their start and end apart: 2, of which 2 were waited for; matrix products, arithmetic and copies ran while one was open for 0% of the time, Pallas kernels for 0%

commit v1 on v0

v1 whole, which is shorter than its diff:
```python
import functools
import jax
import jax.numpy as jnp
from jax import lax
from jax.experimental import pallas as pl
from jax.experimental.pallas import tpu as pltpu
from jax.sharding import PartitionSpec as P

NT = (((1,), (1,)), ((), ()))

def feat_kernel(core_ref, g_ref, i_ref, fc_ref, fo_ref, prod, *, group, mode):
    n = g_ref.shape[1]
    c = core_ref[0]
    scale = 1.0 / 16.0
    if mode == "dup":
        for e in range(n):
            right = jnp.concatenate([i_ref[0, e], i_ref[0, e]], axis=0)
            prod[pl.ds(e * 64, 64), :] = lax.dot_general(g_ref[0, e], right, NT, preferred_element_type=jnp.float32)
    elif mode == "pair":
        for e in range(0, n, 2):
            right = jnp.concatenate([i_ref[0, e], i_ref[0, e], i_ref[0, e + 1], i_ref[0, e + 1]], axis=0)
            left = jnp.concatenate([g_ref[0, e], g_ref[0, e + 1]], axis=0)
            r = lax.dot_general(left, right, NT, preferred_element_type=jnp.float32)
            prod[pl.ds(e * 64, 64), :] = r[:64, :128]
            prod[pl.ds(e * 64 + 64, 64), :] = r[64:, 128:]
    lane = lax.broadcasted_iota(jnp.int32, (n, 128), 1) < 64
    for half, out in ((c, fc_ref), (1 - c, fo_ref)):
        for t in range(16):
            lo = prod[pl.ds(half * 32 + 2 * t, n, stride=64), :]
            hi = prod[pl.ds(half * 32 + 2 * t + 1, n, stride=64), :]
            out[t] = (jnp.where(lane, lo, hi) * scale).astype(jnp.bfloat16)

def features(core, g, i, n=32, mode="dup"):
    ex = g.shape[1]
    return pl.pallas_call(
        functools.partial(feat_kernel, group=1, mode=mode),
        grid_spec=pltpu.PrefetchScalarGridSpec(
            num_scalar_prefetch=1, grid=(ex // n,),
            in_specs=[pl.BlockSpec((1, n, 64, 256), lambda s, c: (0, s, 0, 0))] * 2,
            out_specs=[pl.BlockSpec((16, n, 128), lambda s, c: (0, s, 0))] * 2,
            scratch_shapes=[pltpu.VMEM((n * 64, 128), jnp.float32)]),
        out_shape=[jax.ShapeDtypeStruct((16, ex, 128), jnp.bfloat16)] * 2,
        compiler_params=pltpu.CompilerParams(vmem_limit_bytes=48 << 20),
        cost_estimate=pl.CostEstimate(flops=2 * ex * 64 * 64 * 256, bytes_accessed=18 << 20, transcendentals=0),
        name="features",
    )(core, g, i)

def cat(ref, lo, n):
    return jnp.concatenate([ref[lo + t] for t in range(n)], axis=1)

def gram_kernel(s_ref, ac, ao, fc, fo, gc, go, xsa, xsb, xoa, xob, x2s, x2o, p0, p1, p2, p3):
    f32 = jnp.float32
    dot = lambda a, b: lax.dot_general(a, b, NT, preferred_element_type=f32)
    outs = (p0, p1, p2, p3)
    def put(which, col, val):
        for d in range(4):
            @pl.when(s_ref[which] == d)
            def _():
                outs[d][:, col * 256:(col + 1) * 256] = val.astype(outs[d].dtype)
    a, b = cat(ac, 0, 16), cat(ao, 0, 16)
    put(0, 0, dot(a, cat(fc, 0, 16)) + dot(b, cat(fo, 0, 16)))
    put(0, 1, dot(a, cat(gc, 0, 16)) + dot(b, cat(go, 0, 16)))
    put(1, 0, dot(a, cat(xsa, 0, 16)))
    put(1, 1, dot(a, cat(xsb, 0, 16)))
    put(2, 0, dot(b, cat(xob, 0, 16)))
    put(2, 1, dot(b, cat(xoa, 0, 16)))
    h = s_ref[4] * 8
    a, b = cat(ac, h, 8), cat(ao, h, 8)
    put(3, 0, dot(a, cat(x2s.at[0], 0, 8)) + dot(b, cat(x2o.at[1], 0, 8)))
    put(3, 1, dot(a, cat(x2s.at[1], 0, 8)) + dot(b, cat(x2o.at[0], 0, 8)))

def gram(slots, *ops):
    rows = ops[0].shape[1]
    v = pl.BlockSpec(memory_space=pltpu.VMEM)
    return pl.pallas_call(
        gram_kernel,
        in_specs=[pl.BlockSpec(memory_space=pltpu.SMEM)] + [v] * len(ops),
        out_specs=[v] * 4,
        out_shape=[jax.ShapeDtypeStruct((rows, 512), jnp.float32)] + [jax.ShapeDtypeStruct((rows, 512), jnp.bfloat16)] * 3,
        compiler_params=pltpu.CompilerParams(vmem_limit_bytes=48 << 20),
        cost_estimate=pl.CostEstimate(flops=2 * rows * 512 * 10240, bytes_accessed=12 << 20, transcendentals=0),
        name="gram",
    )(slots, *ops)


AXES = ("dp", "layer")


def device(x, y, z, c):
    x, y, z = x % 4, y % 4, z % 4
    return ((z * 2 + y // 2) * 2 + c) * 8 + x * 2 + y % 2


def shift(array, move):
    pairs = []
    for x in range(4):
        for y in range(4):
            for z in range(4):
                for c in range(2):
                    place = move(x, y, z, c)
                    if place is not None:
                        pairs.append((device(x, y, z, c), device(*place)))
    return lax.ppermute(array, AXES, pairs)


def other_core(x, y, z, c):
    return x, y, z, 1 - c


def other_half(x, y, z, c):
    return x, y + 2, z, c


def along_z(x, y, z, c):
    return x, y, z - 1 + 2 * c, c


def body(grads_proj, inputs_proj):
    dp = lax.axis_index("dp").astype(jnp.int32)
    layer = lax.axis_index("layer").astype(jnp.int32)
    core = dp % 2
    z = dp // 4
    y = (dp // 2) % 2 * 2 + layer % 2
    x = layer // 2

    own_c, own_o = features(core.reshape(1), grads_proj, inputs_proj)
    far_c, far_o = shift(own_c, other_half), shift(own_o, other_half)
    mate_c = shift(own_o, other_core)
    side_a = shift(own_c, along_z)
    side_b = shift(mate_c, along_z)
    mate_o = shift(own_c, other_core)
    to_z = (z - 1 + 2 * core) % 4
    start = to_z // 2 * 8
    part = jnp.stack([lax.dynamic_slice_in_dim(side_a, start, 8, 0), lax.dynamic_slice_in_dim(side_b, start, 8, 0)])
    two = shift(part, along_z)
    back_a, back_b = shift(side_a, other_core), shift(side_b, other_core)
    two_back = shift(two, other_core)

    near = jnp.where(core == 0, 1, 3)
    slots = jnp.stack([z - x, z + near - x, z + 4 - near - x, z + 2 - x]) % 4
    slots = jnp.concatenate([slots, (z // 2).reshape(1)]).astype(jnp.int32)
    columns = (own_c, own_o, mate_c, mate_o, side_a, side_b, back_a, back_b, two, two_back)

    def over_x(rows_c, rows_o):
        keep, up, two_up, down = gram(slots, rows_c, rows_o, *columns)
        up = shift(up, lambda x, y, z, c: (x + 1, y, z, c))
        down = shift(down, lambda x, y, z, c: (x - 1, y, z, c))
        two_up = shift(two_up, lambda x, y, z, c: (x + 2, y, z, c))
        f32 = jnp.float32
        return (keep + up.astype(f32)) + (down.astype(f32) + two_up.astype(f32))

    near_sum = over_x(own_c, own_o)
    far_sum = over_x(far_c, far_o)
    edge = (y == 0) | (y == 3)
    give = jnp.where(edge, far_sum, near_sum).astype(jnp.bfloat16)
    keep = jnp.where(edge, near_sum, far_sum)
    total = keep + shift(give, lambda x, y, z, c: (x, y ^ 1, z, c)).astype(jnp.float32)
    sent = total.astype(jnp.bfloat16)
    direct = shift(sent, lambda x, y, z, c: (x, 3 - y, z, c) if y in (1, 2) else None).astype(jnp.float32)
    direct = jnp.where(edge, total, direct)
    turn_a = shift(sent[:, :256], lambda x, y, z, c: (z, y, x, c) if x != z else None)
    turn_b = shift(sent[:, 256:], lambda x, y, z, c: (z, y, x, 1 - c) if x != z else None)
    turned = jnp.concatenate([turn_a.T, turn_b.T], axis=1).astype(jnp.float32)
    out = direct + turned
    out = jnp.where(core == 0, out, jnp.concatenate([out[:, 256:], out[:, :256]], axis=1))
    return out * (1.0 / jnp.sqrt(jnp.float32(8 * 4096)))


def solution(mesh):
    return jax.shard_map(
        body,
        mesh=mesh,
        in_specs=(P("layer", "dp", None, None), P("layer", "dp", None, None)),
        out_specs=P("dp", "layer"),
        check_vma=False,
    )
```

time: 343 us -> 144 us (0.42)
  waiting for transfers between devices: 291 us -> 73.6 us
  Pallas kernels: 0 us -> 36.3 us
  matrix products: 27 us -> 0 us
  starting transfers between devices: 0.04 us -> 23.5 us
  between operations: 13.4 us -> 0.15 us
    all_gather x1 -> x0, waiting for transfers between devices: 202 us -> none  [body(): lax.all_gather(features, 'dp', axis=0, tiled=True)]
    reduce_scatter x1 -> x0, waiting for transfers between devices: 89.5 us -> none  [body(): lax.psum_scatter(partial_gram, 'layer', scatter_dimension=1, tiled=True)]
    ppermute x0 -> x20, waiting for transfers between devices: none -> 73.6 us  [shift(): return lax.ppermute(array, AXES, pairs)]
    pallas_call x0 -> x3, Pallas kernels: none -> 36.3 us  [the longest x2 22.8 us: gram(): pl.pallas_call(gram_kernel, in_specs=[pl.BlockSpec(memory_space=pltpu.SME...]
    dot_general x2 -> x0, matrix products: 27 us -> none  [the longest x1 17 us: contract(): lax.dot_general(left, right, (((1,), (1,)), ((), ())), preferred_element_...]
    ppermute x0 -> x20, starting transfers between devices: none -> 23.5 us  [shift(): return lax.ppermute(array, AXES, pairs)]
    convert_element_type x1, local copies, waits for them, and re-layouts: 5.88 us -> 0.14 us  [body(): shift(sent, lambda x, y, z, c: (x, 3 - y, z, c) if y in (1, 2) else None)]
  transfers between devices with their start and end apart: 2 -> 20, of which waited for: 2 -> 10; matrix products, arithmetic and copies ran while one was open for 0% -> 2% of each run, Pallas kernels for 0% -> 8%
where the time goes in v1:
time: 144 us; the launch traced here: 143 us
  waiting for transfers between devices  73.6 us (51%)
  Pallas kernels  36.3 us (25%)
  starting transfers between devices  23.5 us (16%)
  local copies, waits for them, and re-layouts  5.23 us (4%)
  other arithmetic  4.06 us (3%)
    ppermute x20, waiting for transfers between devices, shift(): return lax.ppermute(array, AXES, pairs)  73.6 us
    ppermute x20, starting transfers between devices, shift(): return lax.ppermute(array, AXES, pairs)  23.5 us
    pallas_call x2, Pallas kernels, gram(): pl.pallas_call(gram_kernel, in_specs=[pl.BlockSpec(memory_space=pltpu.SME...  22.8 us
    pallas_call x1, Pallas kernels, features(): pl.pallas_call(functools.partial(feat_kernel, group=1, mode=mode), grid_s...  13.5 us
  transfers between devices with their start and end apart: 20, of which 10 were waited for; matrix products, arithmetic and copies ran while one was open for 2% of the time, Pallas kernels for 8%

profile of v1, /device:TPU:104, one launch (start us, length us, event | category | flops | bytes accessed | tf_op | source)
XLA Modules:
  0.0 142.9 jit_solution(12226992305025503152)
XLA Ops:
  0.0 13.5 %features.1 = (bf16[16,256,128]{2,1,0:T(8,128)(2,1)S(1)}, bf16[16,256,128]{2,1,0:T(8,128)(2,1)S(1)}) custom-call(s32[1]{0:T(128)} %bitcast.5.core_ref, bf16[1,256,64,256]{3,2,1,0:T(8,128)(2,1)} %g_ref.1, bf16[1,256,64,256]{3,2,1,0:T(8,128)(2,1)} %i_ref.1), custom_call_target="tpu_custom_call" | custom-call | flops 536870912 | bytes 18874368 | tf_op jit(solution)/shard_map/features/pallas_call | solution.py:35
  13.5 0.1 collective-permute-start
  13.6 0.4 collective-permute-start.2
  14.0 2.2 %collective-permute-done.gc = bf16[16,256,128]{2,1,0:T(8,128)(2,1)S(1)} collective-permute-done((bf16[16,256,128]{2,1,0:T(8,128)(2,1)S(1)}, bf16[16,256,128]{2,1,0:T(8,128)(2,1)S(1)}, u32[]{:S(2)}, u32[]{:S(2)}) %collective-permute-start) | collective-permute-done | bytes 1048608 | tf_op jit(solution)/shard_map/ppermute | solution.py:103
  16.2 0.4 collective-permute-start.3
  16.6 2.3 %collective-permute-start.12 = (bf16[16,256,128]{2,1,0:T(8,128)(2,1)S(1)}, bf16[16,256,128]{2,1,0:T(8,128)(2,1)}, u32[]{:S(2)}, u32[]{:S(2)}) collective-permute-start(bf16[16,256,128]{2,1,0:T(8,128)(2,1)S(1)} %get-tuple-element.16.ao.fo), channel_id=1, source_target_pairs={{0,16},{8,24},{32,48},{40,56},{64,80},{72,88},{96,112},{104,120},{... | collective-permute-start | bytes 3145736 | tf_op jit(solution)/shard_map/ppermute | solution.py:103
  18.9 10.8 %collective-permute-done.2.xsa = bf16[16,256,128]{2,1,0:T(8,128)(2,1)} collective-permute-done((bf16[16,256,128]{2,1,0:T(8,128)(2,1)S(1)}, bf16[16,256,128]{2,1,0:T(8,128)(2,1)}, u32[]{:S(2)}, u32[]{:S(2)}) %collective-permute-start.2) | collective-permute-done | bytes 1048608 | tf_op jit(solution)/shard_map/ppermute | solution.py:103
  29.8 1.1 dynamic-slice_bitcast_fusion.1
  30.9 10.2 %collective-permute-done.3.xsb = bf16[16,256,128]{2,1,0:T(8,128)(2,1)} collective-permute-done((bf16[16,256,128]{2,1,0:T(8,128)(2,1)S(1)}, bf16[16,256,128]{2,1,0:T(8,128)(2,1)}, u32[]{:S(2)}, u32[]{:S(2)}) %collective-permute-start.3) | collective-permute-done | bytes 1048608 | tf_op jit(solution)/shard_map/ppermute | solution.py:103
  41.0 1.1 dynamic-slice_bitcast_fusion
  42.1 0.1 pad_maximum_fusion
  42.2 0.1 collective-permute-start.6
  42.3 2.4 %collective-permute-start.11 = (bf16[16,256,128]{2,1,0:T(8,128)(2,1)S(1)}, bf16[16,256,128]{2,1,0:T(8,128)(2,1)}, u32[]{:S(2)}, u32[]{:S(2)}) collective-permute-start(bf16[16,256,128]{2,1,0:T(8,128)(2,1)S(1)} %get-tuple-element.15.ac.fc), channel_id=1, source_target_pairs={{0,16},{8,24},{32,48},{40,56},{64,80},{72,88},{96,112},{104,120},{... | collective-permute-start | bytes 3145736 | tf_op jit(solution)/shard_map/ppermute | solution.py:103
  44.7 0.0 collective-permute-start.1
  44.7 0.5 collective-permute-start.4
  45.2 0.0 collective-permute-start.5
  45.2 13.2 %collective-permute-done.6.x2s = bf16[2,8,256,128]{3,2,1,0:T(8,128)(2,1)} collective-permute-done((bf16[2,8,256,128]{3,2,1,0:T(8,128)(2,1)S(1)}, bf16[2,8,256,128]{3,2,1,0:T(8,128)(2,1)}, u32[]{:S(2)}, u32[]{:S(2)}) %collective-permute-start.6) | collective-permute-done | bytes 1048608 | tf_op jit(solution)/shard_map/ppermute | solution.py:103
  58.4 0.0 collective-permute-start.7
  58.4 0.1 and_select_fusion
  58.5 0.1 pad_add_fusion.s_ref
  58.6 9.8 %collective-permute-done.11.ac = bf16[16,256,128]{2,1,0:T(8,128)(2,1)} collective-permute-done((bf16[16,256,128]{2,1,0:T(8,128)(2,1)S(1)}, bf16[16,256,128]{2,1,0:T(8,128)(2,1)}, u32[]{:S(2)}, u32[]{:S(2)}) %collective-permute-start.11) | collective-permute-done | bytes 1048608 | tf_op jit(solution)/shard_map/ppermute | solution.py:103
  68.4 0.0 collective-permute-done.5.xob
  68.4 11.7 %gram.3 = (f32[256,512]{1,0:T(8,128)S(1)}, bf16[256,512]{1,0:T(8,128)(2,1)S(1)}, bf16[256,512]{1,0:T(8,128)(2,1)S(1)}, bf16[256,512]{1,0:T(8,128)(2,1)}) custom-call(s32[5]{0:T(128)S(1)} %pad_add_fusion.s_ref, bf16[16,256,128]{2,1,0:T(8,128)(2,1)} %collective-permute-done.11.ac, bf16[16,256,128]{2,1,0:T(8,128)(2,1)} %collective-permute-done.12.ao, ...), custom_call_target="tpu_custom_call" | custom-call | flops 2684354560 | bytes 12582912 | tf_op jit(solution)/shard_map/gram/pallas_call | solution.py:75
  80.1 0.8 copy-done.2
  80.9 1.5 %collective-permute-start.13 = (bf16[256,512]{1,0:T(8,128)(2,1)S(1)}, bf16[256,512]{1,0:T(8,128)(2,1)S(1)}, u32[]{:S(2)}, u32[]{:S(2)}) collective-permute-start(bf16[256,512]{1,0:T(8,128)(2,1)S(1)} %get-tuple-element.22), channel_id=1, source_target_pairs={{0,2},{8,10},{32,34},{40,42},{64,66},{72,74},{96,98},{104,106},{1,... | collective-permute-start | bytes 786440 | tf_op jit(solution)/shard_map/ppermute | solution.py:103
  82.4 1.8 %collective-permute-start.14 = (bf16[256,512]{1,0:T(8,128)(2,1)}, bf16[256,512]{1,0:T(8,128)(2,1)}, u32[]{:S(2)}, u32[]{:S(2)}) collective-permute-start(bf16[256,512]{1,0:T(8,128)(2,1)} %get-tuple-element.23), channel_id=1, source_target_pairs={{0,6},{8,14},{32,38},{40,46},{64,70},{72,78},{96,102},{104,110},{1... | collective-permute-start | bytes 786440 | tf_op jit(solution)/shard_map/ppermute | solution.py:103
  84.1 1.8 %collective-permute-start.15 = (bf16[256,512]{1,0:T(8,128)(2,1)S(1)}, bf16[256,512]{1,0:T(8,128)(2,1)}, u32[]{:S(2)}, u32[]{:S(2)}) collective-permute-start(bf16[256,512]{1,0:T(8,128)(2,1)S(1)} %get-tuple-element.24), channel_id=1, source_target_pairs={{0,4},{8,12},{32,36},{40,44},{64,68},{72,76},{96,100},{104,108},{1... | collective-permute-start | bytes 786440 | tf_op jit(solution)/shard_map/ppermute | solution.py:103
  85.9 1.2 copy-done.1
  87.2 11.1 %gram.2 = (f32[256,512]{1,0:T(8,128)S(1)}, bf16[256,512]{1,0:T(8,128)(2,1)}, bf16[256,512]{1,0:T(8,128)(2,1)}, bf16[256,512]{1,0:T(8,128)(2,1)}) custom-call(s32[5]{0:T(128)S(1)} %pad_add_fusion.s_ref, bf16[16,256,128]{2,1,0:T(8,128)(2,1)S(1)} %get-tuple-element.15.ac.fc, bf16[16,256,128]{2,1,0:T(8,128)(2,1)S(1)} %get-tuple-element.16.ao.fo, ...), custom_call_target="tpu_custom_call" | custom-call | flops 2684354560 | bytes 12582912 | tf_op jit(solution)/shard_map/gram/pallas_call | solution.py:75
  98.2 0.6 collective-permute-start.8
  98.9 2.6 %collective-permute-start.9 = (bf16[256,512]{1,0:T(8,128)(2,1)}, bf16[256,512]{1,0:T(8,128)(2,1)S(1)}, u32[]{:S(2)}, u32[]{:S(2)}) collective-permute-start(bf16[256,512]{1,0:T(8,128)(2,1)} %get-tuple-element.19), channel_id=1, source_target_pairs={{0,6},{8,14},{32,38},{40,46},{64,70},{72,78},{96,102},{104,110},{1... | collective-permute-start | bytes 786440 | tf_op jit(solution)/shard_map/ppermute | solution.py:103
  101.5 0.7 copy-done.4
  102.2 0.5 collective-permute-start.10
  102.7 8.9 %collective-permute-done.8 = bf16[256,512]{1,0:T(8,128)(2,1)S(1)} collective-permute-done((bf16[256,512]{1,0:T(8,128)(2,1)}, bf16[256,512]{1,0:T(8,128)(2,1)S(1)}, u32[]{:S(2)}, u32[]{:S(2)}) %collective-permute-start.8) | collective-permute-done | bytes 262176 | tf_op jit(solution)/shard_map/ppermute | solution.py:103
  111.7 1.4 select_convert_fusion
  113.1 0.7 collective-permute-start.16
  113.7 5.8 %collective-permute-done.16 = bf16[256,512]{1,0:T(8,128)(2,1)S(1)} collective-permute-done((bf16[256,512]{1,0:T(8,128)(2,1)S(1)}, bf16[256,512]{1,0:T(8,128)(2,1)S(1)}, u32[]{:S(2)}, u32[]{:S(2)}) %collective-permute-start.16) | collective-permute-done | bytes 262176 | tf_op jit(solution)/shard_map/ppermute | solution.py:103
  119.5 1.4 convert_add_fusion.1
  120.9 0.1 copy.3
  121.1 3.5 %collective-permute-start.17 = (bf16[256,512]{0,1:T(8,128)(2,1)S(1)}, bf16[256,512]{0,1:T(8,128)(2,1)S(1)}, u32[]{:S(2)}, u32[]{:S(2)}) collective-permute-start(bf16[256,512]{0,1:T(8,128)(2,1)S(1)} %copy.3), channel_id=1, source_target_pairs={{1,16},{9,24},{33,48},{41,56},{65,80},{73,88},{97,112},{105,120},{... | collective-permute-start | bytes 786440 | tf_op jit(solution)/shard_map/ppermute | solution.py:103
  124.6 2.1 %collective-permute-start.18 = (bf16[256,256]{0,1:T(8,128)(2,1)S(1)}, bf16[256,256]{0,1:T(8,128)(2,1)S(1)}, u32[]{:S(2)}, u32[]{:S(2)}) collective-permute-start(bf16[256,256]{0,1:T(8,128)(2,1)S(1)} %get-tuple-element.27), channel_id=1, source_target_pairs={{32,2},{40,10},{64,4},{72,12},{96,6},{104,14},{33,3},{41,11},{65,5... | collective-permute-start | bytes 393224 | tf_op jit(solution)/shard_map/ppermute | solution.py:103
  126.7 2.3 %collective-permute-start.19 = (bf16[256,256]{0,1:T(8,128)(2,1)S(1)}, bf16[256,256]{0,1:T(8,128)(2,1)S(1)}, u32[]{:S(2)}, u32[]{:S(2)}) collective-permute-start(bf16[256,256]{0,1:T(8,128)(2,1)S(1)} %get-tuple-element.28), channel_id=1, source_target_pairs={{32,10},{40,2},{64,12},{72,4},{96,14},{104,6},{33,11},{41,3},{65,1... | collective-permute-start | bytes 393224 | tf_op jit(solution)/shard_map/ppermute | solution.py:103
  129.0 0.3 collective-permute-done.17
  129.3 0.1 copy.4
  129.5 5.3 %collective-permute-done.18 = bf16[256,256]{0,1:T(8,128)(2,1)S(1)} collective-permute-done((bf16[256,256]{0,1:T(8,128)(2,1)S(1)}, bf16[256,256]{0,1:T(8,128)(2,1)S(1)}, u32[]{:S(2)}, u32[]{:S(2)}) %collective-permute-start.18) | collective-permute-done | bytes 131104 | tf_op jit(solution)/shard_map/ppermute | solution.py:103
  134.8 7.1 %collective-permute-done.19 = bf16[256,256]{0,1:T(8,128)(2,1)S(1)} collective-permute-done((bf16[256,256]{0,1:T(8,128)(2,1)S(1)}, bf16[256,256]{0,1:T(8,128)(2,1)S(1)}, u32[]{:S(2)}, u32[]{:S(2)}) %collective-permute-start.19) | collective-permute-done | bytes 131104 | tf_op jit(solution)/shard_map/ppermute | solution.py:103
  141.9 0.1 convert_add_fusion
  142.0 0.9 fusion
  (18 shorter events, 0.1 us)
Async XLA Ops:
  13.5 2.7 %collective-permute-start = (bf16[16,256,128]{2,1,0:T(8,128)(2,1)S(1)}, bf16[16,256,128]{2,1,0:T(8,128)(2,1)S(1)}, u32[]{:S(2)}, u32[]{:S(2)}) collective-permute-start(bf16[16,256,128]{2,1,0:T(8,128)(2,1)S(1)} %get-tuple-element.16.ao.fo), channel_id=1, source_target_pairs={{0,8},{8,0},{32,40},{40,32},{64,72},{72,64},{96,104},{104,96},{1,9... | collective-permute-start | bytes 3145736 | tf_op jit(solution)/shard_map/ppermute | solution.py:103
  13.6 16.2 %collective-permute-start.2 = (bf16[16,256,128]{2,1,0:T(8,128)(2,1)S(1)}, bf16[16,256,128]{2,1,0:T(8,128)(2,1)}, u32[]{:S(2)}, u32[]{:S(2)}) collective-permute-start(bf16[16,256,128]{2,1,0:T(8,128)(2,1)S(1)} %get-tuple-element.15.ac.fc), channel_id=1, source_target_pairs={{0,96},{8,40},{32,0},{40,72},{64,32},{72,104},{96,64},{104,8},{1,9... | collective-permute-start | bytes 3145736 | tf_op jit(solution)/shard_map/ppermute | solution.py:103
  16.2 52.1 %copy-start = (bf16[16,256,128]{2,1,0:T(8,128)(2,1)}, bf16[16,256,128]{2,1,0:T(8,128)(2,1)S(1)}, u32[]{:S(2)}) copy-start(bf16[16,256,128]{2,1,0:T(8,128)(2,1)S(1)} %collective-permute-done.gc) | copy-start | bytes 3145732
  16.2 24.8 %collective-permute-start.3 = (bf16[16,256,128]{2,1,0:T(8,128)(2,1)S(1)}, bf16[16,256,128]{2,1,0:T(8,128)(2,1)}, u32[]{:S(2)}, u32[]{:S(2)}) collective-permute-start(bf16[16,256,128]{2,1,0:T(8,128)(2,1)S(1)} %collective-permute-done.gc), channel_id=1, source_target_pairs={{0,96},{8,40},{32,0},{40,72},{64,32},{72,104},{96,64},{104,8},{1,9... | collective-permute-start | bytes 3145736 | tf_op jit(solution)/shard_map/ppermute | solution.py:103
  16.6 28.6 %collective-permute-start.12 = (bf16[16,256,128]{2,1,0:T(8,128)(2,1)S(1)}, bf16[16,256,128]{2,1,0:T(8,128)(2,1)}, u32[]{:S(2)}, u32[]{:S(2)}) collective-permute-start(bf16[16,256,128]{2,1,0:T(8,128)(2,1)S(1)} %get-tuple-element.16.ao.fo), channel_id=1, source_target_pairs={{0,16},{8,24},{32,48},{40,56},{64,80},{72,88},{96,112},{104,120},{... | collective-permute-start | bytes 3145736 | tf_op jit(solution)/shard_map/ppermute | solution.py:103
  42.2 16.2 %collective-permute-start.6 = (bf16[2,8,256,128]{3,2,1,0:T(8,128)(2,1)S(1)}, bf16[2,8,256,128]{3,2,1,0:T(8,128)(2,1)}, u32[]{:S(2)}, u32[]{:S(2)}) collective-permute-start(bf16[2,8,256,128]{3,2,1,0:T(8,128)(2,1)S(1)} %pad_maximum_fusion), channel_id=1, source_target_pairs={{0,96},{8,40},{32,0},{40,72},{64,32},{72,104},{96,64},{104,8},{1,9... | collective-permute-start | bytes 3145736 | tf_op jit(solution)/shard_map/ppermute | solution.py:103
  42.3 26.1 %collective-permute-start.11 = (bf16[16,256,128]{2,1,0:T(8,128)(2,1)S(1)}, bf16[16,256,128]{2,1,0:T(8,128)(2,1)}, u32[]{:S(2)}, u32[]{:S(2)}) collective-permute-start(bf16[16,256,128]{2,1,0:T(8,128)(2,1)S(1)} %get-tuple-element.15.ac.fc), channel_id=1, source_target_pairs={{0,16},{8,24},{32,48},{40,56},{64,80},{72,88},{96,112},{104,120},{... | collective-permute-start | bytes 3145736 | tf_op jit(solution)/shard_map/ppermute | solution.py:103
  44.7 23.7 %collective-permute-start.1 = (bf16[16,256,128]{2,1,0:T(8,128)(2,1)S(1)}, bf16[16,256,128]{2,1,0:T(8,128)(2,1)}, u32[]{:S(2)}, u32[]{:S(2)}) collective-permute-start(bf16[16,256,128]{2,1,0:T(8,128)(2,1)S(1)} %get-tuple-element.15.ac.fc), channel_id=1, source_target_pairs={{0,8},{8,0},{32,40},{40,32},{64,72},{72,64},{96,104},{104,96},{1,9... | collective-permute-start | bytes 3145736 | tf_op jit(solution)/shard_map/ppermute | solution.py:103
  44.7 23.7 %collective-permute-start.4 = (bf16[16,256,128]{2,1,0:T(8,128)(2,1)}, bf16[16,256,128]{2,1,0:T(8,128)(2,1)}, u32[]{:S(2)}, u32[]{:S(2)}) collective-permute-start(bf16[16,256,128]{2,1,0:T(8,128)(2,1)} %collective-permute-done.2.xsa), channel_id=1, source_target_pairs={{0,8},{8,0},{32,40},{40,32},{64,72},{72,64},{96,104},{104,96},{1,9... | collective-permute-start | bytes 3145736 | tf_op jit(solution)/shard_map/ppermute | solution.py:103
  45.2 23.2 %collective-permute-start.5 = (bf16[16,256,128]{2,1,0:T(8,128)(2,1)}, bf16[16,256,128]{2,1,0:T(8,128)(2,1)}, u32[]{:S(2)}, u32[]{:S(2)}) collective-permute-start(bf16[16,256,128]{2,1,0:T(8,128)(2,1)} %collective-permute-done.3.xsb), channel_id=1, source_target_pairs={{0,8},{8,0},{32,40},{40,32},{64,72},{72,64},{96,104},{104,96},{1,9... | collective-permute-start | bytes 3145736 | tf_op jit(solution)/shard_map/ppermute | solution.py:103
  58.4 10.0 %collective-permute-start.7 = (bf16[2,8,256,128]{3,2,1,0:T(8,128)(2,1)}, bf16[2,8,256,128]{3,2,1,0:T(8,128)(2,1)}, u32[]{:S(2)}, u32[]{:S(2)}) collective-permute-start(bf16[2,8,256,128]{3,2,1,0:T(8,128)(2,1)} %collective-permute-done.6.x2s), channel_id=1, source_target_pairs={{0,8},{8,0},{32,40},{40,32},{64,72},{72,64},{96,104},{104,96},{1,9... | collective-permute-start | bytes 3145736 | tf_op jit(solution)/shard_map/ppermute | solution.py:103
  80.1 0.8 copy-start.2
  80.9 20.6 %collective-permute-start.13 = (bf16[256,512]{1,0:T(8,128)(2,1)S(1)}, bf16[256,512]{1,0:T(8,128)(2,1)S(1)}, u32[]{:S(2)}, u32[]{:S(2)}) collective-permute-start(bf16[256,512]{1,0:T(8,128)(2,1)S(1)} %get-tuple-element.22), channel_id=1, source_target_pairs={{0,2},{8,10},{32,34},{40,42},{64,66},{72,74},{96,98},{104,106},{1,... | collective-permute-start | bytes 786440 | tf_op jit(solution)/shard_map/ppermute | solution.py:103
  82.4 20.3 %collective-permute-start.14 = (bf16[256,512]{1,0:T(8,128)(2,1)}, bf16[256,512]{1,0:T(8,128)(2,1)}, u32[]{:S(2)}, u32[]{:S(2)}) collective-permute-start(bf16[256,512]{1,0:T(8,128)(2,1)} %get-tuple-element.23), channel_id=1, source_target_pairs={{0,6},{8,14},{32,38},{40,46},{64,70},{72,78},{96,102},{104,110},{1... | collective-permute-start | bytes 786440 | tf_op jit(solution)/shard_map/ppermute | solution.py:103
  84.1 18.6 %collective-permute-start.15 = (bf16[256,512]{1,0:T(8,128)(2,1)S(1)}, bf16[256,512]{1,0:T(8,128)(2,1)}, u32[]{:S(2)}, u32[]{:S(2)}) collective-permute-start(bf16[256,512]{1,0:T(8,128)(2,1)S(1)} %get-tuple-element.24), channel_id=1, source_target_pairs={{0,4},{8,12},{32,36},{40,44},{64,68},{72,76},{96,100},{104,108},{1... | collective-permute-start | bytes 786440 | tf_op jit(solution)/shard_map/ppermute | solution.py:103
  85.9 1.2 copy-start.1
  87.2 24.5 %copy-start.3 = (f32[256,512]{1,0:T(8,128)S(1)}, f32[256,512]{1,0:T(8,128)}, u32[]{:S(2)}) copy-start(f32[256,512]{1,0:T(8,128)} %copy-done.2) | copy-start | bytes 1572868
  98.2 13.4 %collective-permute-start.8 = (bf16[256,512]{1,0:T(8,128)(2,1)}, bf16[256,512]{1,0:T(8,128)(2,1)S(1)}, u32[]{:S(2)}, u32[]{:S(2)}) collective-permute-start(bf16[256,512]{1,0:T(8,128)(2,1)} %get-tuple-element.18), channel_id=1, source_target_pairs={{0,2},{8,10},{32,34},{40,42},{64,66},{72,74},{96,98},{104,106},{1,... | collective-permute-start | bytes 786440 | tf_op jit(solution)/shard_map/ppermute | solution.py:103
  98.9 12.8 %collective-permute-start.9 = (bf16[256,512]{1,0:T(8,128)(2,1)}, bf16[256,512]{1,0:T(8,128)(2,1)S(1)}, u32[]{:S(2)}, u32[]{:S(2)}) collective-permute-start(bf16[256,512]{1,0:T(8,128)(2,1)} %get-tuple-element.19), channel_id=1, source_target_pairs={{0,6},{8,14},{32,38},{40,46},{64,70},{72,78},{96,102},{104,110},{1... | collective-permute-start | bytes 786440 | tf_op jit(solution)/shard_map/ppermute | solution.py:103
  101.5 0.7 copy-start.4
  102.2 9.4 %collective-permute-start.10 = (bf16[256,512]{1,0:T(8,128)(2,1)}, bf16[256,512]{1,0:T(8,128)(2,1)S(1)}, u32[]{:S(2)}, u32[]{:S(2)}) collective-permute-start(bf16[256,512]{1,0:T(8,128)(2,1)} %get-tuple-element.20), channel_id=1, source_target_pairs={{0,4},{8,12},{32,36},{40,44},{64,68},{72,76},{96,100},{104,108},{1... | collective-permute-start | bytes 786440 | tf_op jit(solution)/shard_map/ppermute | solution.py:103
  113.1 6.5 %collective-permute-start.16 = (bf16[256,512]{1,0:T(8,128)(2,1)S(1)}, bf16[256,512]{1,0:T(8,128)(2,1)S(1)}, u32[]{:S(2)}, u32[]{:S(2)}) collective-permute-start(bf16[256,512]{1,0:T(8,128)(2,1)S(1)} %select_convert_fusion), channel_id=1, source_target_pairs={{0,1},{8,9},{32,33},{40,41},{64,65},{72,73},{96,97},{104,105},{1,0... | collective-permute-start | bytes 786440 | tf_op jit(solution)/shard_map/ppermute | solution.py:103
  121.1 8.3 %collective-permute-start.17 = (bf16[256,512]{0,1:T(8,128)(2,1)S(1)}, bf16[256,512]{0,1:T(8,128)(2,1)S(1)}, u32[]{:S(2)}, u32[]{:S(2)}) collective-permute-start(bf16[256,512]{0,1:T(8,128)(2,1)S(1)} %copy.3), channel_id=1, source_target_pairs={{1,16},{9,24},{33,48},{41,56},{65,80},{73,88},{97,112},{105,120},{... | collective-permute-start | bytes 786440 | tf_op jit(solution)/shard_map/ppermute | solution.py:103
  124.6 10.2 %collective-permute-start.18 = (bf16[256,256]{0,1:T(8,128)(2,1)S(1)}, bf16[256,256]{0,1:T(8,128)(2,1)S(1)}, u32[]{:S(2)}, u32[]{:S(2)}) collective-permute-start(bf16[256,256]{0,1:T(8,128)(2,1)S(1)} %get-tuple-element.27), channel_id=1, source_target_pairs={{32,2},{40,10},{64,4},{72,12},{96,6},{104,14},{33,3},{41,11},{65,5... | collective-permute-start | bytes 393224 | tf_op jit(solution)/shard_map/ppermute | solution.py:103
  126.7 15.1 %collective-permute-start.19 = (bf16[256,256]{0,1:T(8,128)(2,1)S(1)}, bf16[256,256]{0,1:T(8,128)(2,1)S(1)}, u32[]{:S(2)}, u32[]{:S(2)}) collective-permute-start(bf16[256,256]{0,1:T(8,128)(2,1)S(1)} %get-tuple-element.28), channel_id=1, source_target_pairs={{32,10},{40,2},{64,12},{72,4},{96,14},{104,6},{33,11},{41,3},{65,1... | collective-permute-start | bytes 393224 | tf_op jit(solution)/shard_map/ppermute | solution.py:103

commit v2 on v0

v2 whole, which is shorter than its diff:
```python
import functools
import jax
import jax.numpy as jnp
from jax import lax
from jax.experimental import pallas as pl
from jax.experimental.pallas import tpu as pltpu
from jax.sharding import PartitionSpec as P

NT = (((1,), (1,)), ((), ()))
AXES = ("dp", "layer")
HALF = 16
PITCH = 68


def feature_kernel(core_ref, g_ref, i_ref, out_ref, prod):
    n = g_ref.shape[1]
    core = core_ref[0]
    for e in range(0, n, 4):
        four = lax.dot_general(
            g_ref[0, e : e + 4].reshape(256, 256),
            i_ref[0, e : e + 4].reshape(256, 256),
            NT,
            preferred_element_type=jnp.float32,
        )
        for k in range(4):
            prod[pl.ds((e + k) * PITCH, 64), :] = four[64 * k : 64 * k + 64, 128 * (k // 2) : 128 * (k // 2) + 128]
    even = lax.broadcasted_iota(jnp.int32, (n, 128), 0) % 2 == 0
    left = lax.broadcasted_iota(jnp.int32, (n, 128), 1) < 64
    in_place = even == left
    for part, half in ((0, core), (1, 1 - core)):
        for t in range(HALF):
            first = prod[pl.ds(half * 32 + 2 * t, n, stride=PITCH), :]
            second = prod[pl.ds(half * 32 + 2 * t + 1, n, stride=PITCH), :]
            moved = pltpu.roll(jnp.where(even, second, first), 64, 1)
            out_ref[part * HALF + t] = jnp.where(in_place, jnp.where(even, first, second), moved).astype(jnp.bfloat16)


def features(core, g, i, start, count, n=64):
    skip = start // n
    return pl.pallas_call(
        feature_kernel,
        grid_spec=pltpu.PrefetchScalarGridSpec(
            num_scalar_prefetch=1,
            grid=(count // n,),
            in_specs=[pl.BlockSpec((1, n, 64, 256), lambda s, c: (0, s + skip, 0, 0))] * 2,
            out_specs=pl.BlockSpec((2 * HALF, n, 128), lambda s, c: (0, s, 0)),
            scratch_shapes=[pltpu.VMEM((n * PITCH, 128), jnp.float32)],
        ),
        out_shape=jax.ShapeDtypeStruct((2 * HALF, count, 128), jnp.bfloat16),
        compiler_params=pltpu.CompilerParams(vmem_limit_bytes=48 << 20),
        cost_estimate=pl.CostEstimate(flops=2 * count * 64 * 64 * 256, bytes_accessed=count * 74000, transcendentals=0),
        name="features",
    )(core, g, i)


def wide(ref, first, count):
    return jnp.concatenate([ref[first + t] for t in range(count)], axis=1)


def gram_kernel(pieces, blocks, s_ref, *refs):
    n_in = pieces + 4 + 6 * len(blocks)
    ins, outs = refs[:n_in], refs[n_in : n_in + 4]
    rows, self_cols, side_cols, back_cols, two_cols, sems = refs[n_in + 4 :]
    row_in, own, mate = ins[:pieces], ins[pieces : pieces + 2], ins[pieces + 2 : pieces + 4]
    core = s_ref[5]
    used = iter(range(64))

    def copy(src, dst):
        return pltpu.make_async_copy(src, dst, sems.at[next(used)])

    row_waits, self_waits, side_waits, back_waits, two_waits = [], [], [], [], []
    at = 0
    for piece in row_in:
        size = piece.shape[1]
        moving = copy(piece, rows.at[:, pl.ds(at, size)])
        moving.start()
        row_waits.append(moving)
        at += size
    for k, b in enumerate(blocks):
        side, back, two = (ins[pieces + 4 + 6 * k + 2 * m : pieces + 6 + 6 * k + 2 * m] for m in range(3))
        waits = []
        for p in range(2):
            place = pl.ds(128 * p, 128)
            for h in range(2):
                here = self_cols.at[k, pl.ds(HALF * h, HALF), place]
                sem = sems.at[next(used)]
                mine = pltpu.make_async_copy(own[p].at[pl.ds(HALF * h, HALF)], here, sem)
                theirs = pltpu.make_async_copy(mate[p].at[pl.ds(HALF * (1 - h), HALF)], here, sem)

                @pl.when(core == b)
                def _():
                    mine.start()

                @pl.when(core != b)
                def _():
                    theirs.start()

                waits.append(mine)
        self_waits.append(waits)
        for source, target, group in ((side, side_cols, side_waits), (back, back_cols, back_waits)):
            waits = []
            for p in range(2):
                moving = copy(source[p], target.at[k, :, pl.ds(128 * p, 128)])
                moving.start()
                waits.append(moving)
            group.append(waits)
        waits = []
        for q in range(2):
            for p in range(2):
                moving = copy(two[q].at[p], two_cols.at[k, pl.ds(8 * q, 8), pl.ds(128 * p, 128)])
                moving.start()
                waits.append(moving)
        two_waits.append(waits)

    def finish(waits):
        for moving in waits:
            moving.wait()

    def put(which, k, value):
        for d in range(4):

            @pl.when(s_ref[which] == d)
            def _():
                outs[d][:, 256 * k : 256 * k + 256] = value.astype(outs[d].dtype)

    def dot(left, right):
        return lax.dot_general(left, right, NT, preferred_element_type=jnp.float32)

    finish(row_waits)
    quarter = s_ref[4] * 8
    for k in range(len(blocks)):
        finish(self_waits[k])
        put(0, k, dot(wide(rows, 0, 2 * HALF), wide(self_cols.at[k], 0, 2 * HALF)))
        finish(side_waits[k])
        put(1, k, dot(wide(rows, 0, HALF), wide(side_cols.at[k], 0, HALF)))
        finish(back_waits[k])
        put(2, k, dot(wide(rows, HALF, HALF), wide(back_cols.at[k], 0, HALF)))
        finish(two_waits[k])
        left = jnp.concatenate([wide(rows, quarter, 8), wide(rows, HALF + quarter, 8)], axis=1)
        put(3, k, dot(left, wide(two_cols.at[k], 0, HALF)))


def gram(slots, row_pieces, own, mate, blocks, columns):
    count = sum(piece.shape[1] for piece in row_pieces)
    width = 256 * len(blocks)
    operands = [*row_pieces, *own, *mate]
    for b in blocks:
        operands += columns[b]
    vmem = lambda *shape: pltpu.VMEM(shape, jnp.bfloat16)
    n = len(blocks)
    return pl.pallas_call(
        functools.partial(gram_kernel, len(row_pieces), blocks),
        in_specs=[pl.BlockSpec(memory_space=pltpu.SMEM)] + [pl.BlockSpec(memory_space=pl.ANY)] * len(operands),
        out_specs=[pl.BlockSpec(memory_space=pltpu.VMEM)] * 4,
        out_shape=[jax.ShapeDtypeStruct((count, width), jnp.float32)]
        + [jax.ShapeDtypeStruct((count, width), jnp.bfloat16)] * 3,
        scratch_shapes=[
            vmem(2 * HALF, count, 128),
            vmem(n, 2 * HALF, 256, 128),
            vmem(n, HALF, 256, 128),
            vmem(n, HALF, 256, 128),
            vmem(n, HALF, 256, 128),
            pltpu.SemaphoreType.DMA((len(row_pieces) + 12 * n,)),
        ],
        compiler_params=pltpu.CompilerParams(vmem_limit_bytes=48 << 20),
        cost_estimate=pl.CostEstimate(
            flops=2 * count * width * 10240, bytes_accessed=(5 * n << 20) + count * 8192, transcendentals=0
        ),
        name="gram",
    )(slots, *operands)


def device(x, y, z, c):
    x, y, z = x % 4, y % 4, z % 4
    return ((z * 2 + y // 2) * 2 + c) * 8 + x * 2 + y % 2


def shift(array, move):
    pairs = []
    for x in range(4):
        for y in range(4):
            for z in range(4):
                for c in range(2):
                    place = move(x, y, z, c)
                    if place is not None:
                        pairs.append((device(x, y, z, c), device(*place)))
    return lax.ppermute(array, AXES, pairs)


def other_core(x, y, z, c):
    return x, y, z, 1 - c


def other_half(x, y, z, c):
    return x, y + 2, z, c


def along_z(x, y, z, c):
    return x, y, z - 1 + 2 * c, c


def body(grads_proj, inputs_proj):
    f32, bf16 = jnp.float32, jnp.bfloat16
    dp = lax.axis_index("dp").astype(jnp.int32)
    layer = lax.axis_index("layer").astype(jnp.int32)
    core = dp % 2
    z = dp // 4
    y = (dp // 2) % 2 * 2 + layer % 2
    x = layer // 2
    ordered = lambda here, there: (jnp.where(core == 0, here, there), jnp.where(core == 0, there, here))

    own, far, mate, first, second = [], [], [], [], []
    for p in range(2):
        rows = features(core.reshape(1), grads_proj, inputs_proj, 128 * p, 128)
        own.append(rows)
        far.append(shift(rows, other_half))
        mate.append(shift(rows, other_core))
        a, b = ordered(rows[:HALF], mate[p][HALF:])
        first.append(a)
        second.append(b)
    start = (z - 1 + 2 * core) % 4 // 2 * 8
    columns = []
    for block in (first, second):
        side = [shift(piece, along_z) for piece in block]
        back = [shift(piece, other_core) for piece in side]
        two = shift(jnp.stack([lax.dynamic_slice_in_dim(piece, start, 8, 0) for piece in side]), along_z)
        columns.append([*side, *back, two, shift(two, other_core)])

    near_j = jnp.where(core == 0, 1, 3)
    slots = jnp.stack([z - x, z + near_j - x, z + 4 - near_j - x, z + 2 - x]) % 4
    slots = jnp.concatenate([slots, jnp.stack([z // 2, core])]).astype(jnp.int32)

    def spread(parts):
        return (
            parts[0],
            shift(parts[1], lambda x, y, z, c: (x + 1, y, z, c)),
            shift(parts[2], lambda x, y, z, c: (x + 2, y, z, c)),
            shift(parts[3], lambda x, y, z, c: (x - 1, y, z, c)),
        )

    def add(parts):
        return (parts[0] + parts[1].astype(f32)) + (parts[2].astype(f32) + parts[3].astype(f32))

    early = (own[0], own[1], far[0])
    part_a = gram(slots, early, own, mate, (0,), columns)
    slots, part_a = lax.optimization_barrier((slots, part_a))
    part_b = gram(slots, early, own, mate, (1,), columns)
    slots, part_b = lax.optimization_barrier((slots, part_b))
    part_c = gram(slots, (far[1],), own, mate, (0, 1), columns)
    sum_a, sum_b, sum_c = add(spread(part_a)), add(spread(part_b)), add(spread(part_c))
    both = jnp.concatenate([sum_a, sum_b], axis=1)
    near_sum = both[:256]
    far_sum = jnp.concatenate([both[256:], sum_c], axis=0)

    edge = (y == 0) | (y == 3)
    give = jnp.where(edge, far_sum, near_sum).astype(bf16)
    keep = jnp.where(edge, near_sum, far_sum)
    total = keep + shift(give, lambda x, y, z, c: (x, y ^ 1, z, c)).astype(f32)
    sent = total.astype(bf16)
    direct = shift(sent, lambda x, y, z, c: (x, 3 - y, z, c) if y in (1, 2) else None).astype(f32)
    direct = jnp.where(edge, total, direct)
    same, cross = ordered(sent[:, :256], sent[:, 256:])
    same = shift(same, lambda x, y, z, c: (z, y, x, c) if x != z else None)
    cross = shift(cross, lambda x, y, z, c: (z, y, x, 1 - c) if x != z else None)
    turned = jnp.concatenate(ordered(same.T, cross.T), axis=1).astype(f32)
    return (direct + turned) * (1.0 / (256.0 * jnp.sqrt(f32(8 * 4096))))


def solution(mesh):
    return jax.shard_map(
        body,
        mesh=mesh,
        in_specs=(P("layer", "dp", None, None), P("layer", "dp", None, None)),
        out_specs=P("dp", "layer"),
        check_vma=False,
    )
```

time: 343 us -> 139 us (0.41)
  waiting for transfers between devices: 291 us -> 50.9 us
  starting transfers between devices: 0.04 us -> 36.4 us
  Pallas kernels: 0 us -> 34.4 us
  matrix products: 27 us -> 0 us
  between operations: 13.4 us -> 0.33 us
  other arithmetic: 1.88 us -> 5.87 us
  local copies, waits for them, and re-layouts: 5.88 us -> 9.35 us
    all_gather x1 -> x0, waiting for transfers between devices: 202 us -> none  [body(): lax.all_gather(features, 'dp', axis=0, tiled=True)]
    reduce_scatter x1 -> x0, waiting for transfers between devices: 89.5 us -> none  [body(): lax.psum_scatter(partial_gram, 'layer', scatter_dimension=1, tiled=True)]
    ppermute x0 -> x29, waiting for transfers between devices: none -> 50.9 us  [shift(): return lax.ppermute(array, AXES, pairs)]
    ppermute x0 -> x29, starting transfers between devices: none -> 36.4 us  [shift(): return lax.ppermute(array, AXES, pairs)]
    pallas_call x0 -> x5, Pallas kernels: none -> 34.4 us  [the longest x3 25 us: gram(): pl.pallas_call(functools.partial(gram_kernel, len(row_pieces), blocks), i...]
    dot_general x2 -> x0, matrix products: 27 us -> none  [the longest x1 17 us: contract(): lax.dot_general(left, right, (((1,), (1,)), ((), ())), preferred_element_...]
    unnamed x0 -> x38, local copies, waits for them, and re-layouts: none -> 7.11 us
    convert_element_type x1, local copies, waits for them, and re-layouts: 5.88 us -> 0.14 us  [body(): shift(sent, lambda x, y, z, c: (x, 3 - y, z, c) if y in (1, 2) else None)]
  transfers between devices with their start and end apart: 2 -> 29, of which waited for: 2 -> 16; matrix products, arithmetic and copies ran while one was open for 0% -> 5% of each run, Pallas kernels for 0% -> 14%
where the time goes in v2:
time: 139 us; the launch traced here: 137 us
  waiting for transfers between devices  50.9 us (37%)
  starting transfers between devices  36.4 us (26%)
  Pallas kernels  34.4 us (25%)
  local copies, waits for them, and re-layouts  9.35 us (7%)
  other arithmetic  5.87 us (4%)
    ppermute x29, waiting for transfers between devices, shift(): return lax.ppermute(array, AXES, pairs)  50.9 us
    ppermute x29, starting transfers between devices, shift(): return lax.ppermute(array, AXES, pairs)  36.4 us
    pallas_call x3, Pallas kernels, gram(): pl.pallas_call(functools.partial(gram_kernel, len(row_pieces), blocks), i...  25 us
    pallas_call x2, Pallas kernels, features(): pl.pallas_call(feature_kernel, grid_spec=pltpu.PrefetchScalarGridSpec(num...  9.44 us
    unnamed x38, local copies, waits for them, and re-layouts  7.11 us
    select_n x2, other arithmetic, body(): jnp.where(core == 0, there, here)  4.27 us
  transfers between devices with their start and end apart: 29, of which 16 were waited for; matrix products, arithmetic and copies ran while one was open for 5% of the time, Pallas kernels for 14%

profile of v2, /device:TPU:104, one launch (start us, length us, event | category | flops | bytes accessed | tf_op | source)
XLA Modules:
  0.0 137.3 jit_solution(13759836296906433649)
XLA Ops:
  0.0 4.6 %features.2.refs_0_.refs_3_.refs_1_ = bf16[32,128,128]{2,1,0:T(8,128)(2,1)S(1)} custom-call(s32[1]{0:T(128)} %bitcast.5.core_ref, bf16[1,256,64,256]{3,2,1,0:T(8,128)(2,1)} %g_ref.3, bf16[1,256,64,256]{3,2,1,0:T(8,128)(2,1)} %i_ref.3), custom_call_target="tpu_custom_call" | custom-call | flops 268435456 | bytes 9472000 | tf_op jit(solution)/shard_map/features/pallas_call | solution.py:40
  4.7 4.9 %features.3.refs_1_.refs_4_.refs_2_ = bf16[32,128,128]{2,1,0:T(8,128)(2,1)S(1)} custom-call(s32[1]{0:T(128)} %bitcast.5.core_ref, bf16[1,256,64,256]{3,2,1,0:T(8,128)(2,1)} %g_ref.3, bf16[1,256,64,256]{3,2,1,0:T(8,128)(2,1)} %i_ref.3), custom_call_target="tpu_custom_call" | custom-call | flops 268435456 | bytes 9472000 | tf_op jit(solution)/shard_map/features/pallas_call | solution.py:40
  9.9 2.1 %broadcast_select_fusion.1 = (bf16[16,128,128]{2,1,0:T(8,128)(2,1)}, bf16[16,128,128]{2,1,0:T(8,128)(2,1)}) fusion(pred[]{:T(512)S(6)} %eq.26, bf16[32,128,128]{2,1,0:T(8,128)(2,1)} %collective-permute-done.1.refs_5_.refs_3_, bf16[32,128,128]{2,1,0:T(8,128)(2,1)S(1)} %features.2.refs_0_.refs_3_.refs_1_), kind=kLoop, calls=%fused_computation.11 | loop fusion | flops 524288 | bytes 2097153 | tf_op jit(solution)/shard_map/jit(_where)/select_n | solution.py:210
  12.4 2.1 %broadcast_select_fusion = (bf16[16,128,128]{2,1,0:T(8,128)(2,1)}, bf16[16,128,128]{2,1,0:T(8,128)(2,1)}) fusion(pred[]{:T(512)S(6)} %eq.26, bf16[32,128,128]{2,1,0:T(8,128)(2,1)} %collective-permute-done.2.refs_6_.refs_4_, bf16[32,128,128]{2,1,0:T(8,128)(2,1)S(1)} %features.3.refs_1_.refs_4_.refs_2_), kind=kLoop, calls=%fused_computation.10 | loop fusion | flops 524288 | bytes 2097153 | tf_op jit(solution)/shard_map/jit(_where)/select_n | solution.py:210
  15.1 2.3 %collective-permute-start = (bf16[32,128,128]{2,1,0:T(8,128)(2,1)S(1)}, bf16[32,128,128]{2,1,0:T(8,128)(2,1)}, u32[]{:S(2)}, u32[]{:S(2)}) collective-permute-start(bf16[32,128,128]{2,1,0:T(8,128)(2,1)S(1)} %features.2.refs_0_.refs_3_.refs_1_), channel_id=1, source_target_pairs={{0,16},{8,24},{32,48},{40,56},{64,80},{72,88},{96,112},{104,120},{... | collective-permute-start | bytes 3145736 | tf_op jit(solution)/shard_map/ppermute | solution.py:187
  17.4 3.7 %collective-permute-start.12 = (bf16[16,128,128]{2,1,0:T(8,128)(2,1)}, bf16[16,128,128]{2,1,0:T(8,128)(2,1)}, u32[]{:S(2)}, u32[]{:S(2)}) collective-permute-start(bf16[16,128,128]{2,1,0:T(8,128)(2,1)} %get-tuple-element.51), channel_id=1, source_target_pairs={{0,96},{8,40},{32,0},{40,72},{64,32},{72,104},{96,64},{104,8},{1,9... | collective-permute-start | bytes 1572872 | tf_op jit(solution)/shard_map/ppermute | solution.py:187
  21.1 1.5 %collective-permute-done.3.refs_7_.refs_5_ = bf16[16,128,128]{2,1,0:T(8,128)(2,1)S(1)} collective-permute-done((bf16[16,128,128]{2,1,0:T(8,128)(2,1)}, bf16[16,128,128]{2,1,0:T(8,128)(2,1)S(1)}, u32[]{:S(2)}, u32[]{:S(2)}) %collective-permute-start.3) | collective-permute-done | bytes 524320 | tf_op jit(solution)/shard_map/ppermute | solution.py:187
  22.6 5.6 %collective-permute-done.4.refs_8_.refs_6_ = bf16[16,128,128]{2,1,0:T(8,128)(2,1)S(1)} collective-permute-done((bf16[16,128,128]{2,1,0:T(8,128)(2,1)}, bf16[16,128,128]{2,1,0:T(8,128)(2,1)S(1)}, u32[]{:S(2)}, u32[]{:S(2)}) %collective-permute-start.4) | collective-permute-done | bytes 524320 | tf_op jit(solution)/shard_map/ppermute | solution.py:187
  28.5 5.5 %collective-permute-done.13.refs_8_.refs_12_ = bf16[16,128,128]{2,1,0:T(8,128)(2,1)} collective-permute-done((bf16[16,128,128]{2,1,0:T(8,128)(2,1)}, bf16[16,128,128]{2,1,0:T(8,128)(2,1)}, u32[]{:S(2)}, u32[]{:S(2)}) %collective-permute-start.13) | collective-permute-done | bytes 524320 | tf_op jit(solution)/shard_map/ppermute | solution.py:187
  34.0 1.0 dynamic-slice_bitcast_fusion
  34.9 4.6 %collective-permute-done.12.refs_7_.refs_11_ = bf16[16,128,128]{2,1,0:T(8,128)(2,1)} collective-permute-done((bf16[16,128,128]{2,1,0:T(8,128)(2,1)}, bf16[16,128,128]{2,1,0:T(8,128)(2,1)}, u32[]{:S(2)}, u32[]{:S(2)}) %collective-permute-start.12) | collective-permute-done | bytes 524320 | tf_op jit(solution)/shard_map/ppermute | solution.py:187
  39.6 1.0 dynamic-slice_bitcast_fusion.1
  40.7 1.6 %collective-permute-done.refs_2_ = bf16[32,128,128]{2,1,0:T(8,128)(2,1)} collective-permute-done((bf16[32,128,128]{2,1,0:T(8,128)(2,1)S(1)}, bf16[32,128,128]{2,1,0:T(8,128)(2,1)}, u32[]{:S(2)}, u32[]{:S(2)}) %collective-permute-start) | collective-permute-done | bytes 1048608 | tf_op jit(solution)/shard_map/ppermute | solution.py:187
  42.3 2.3 %collective-permute-start.21 = (bf16[32,128,128]{2,1,0:T(8,128)(2,1)S(1)}, bf16[32,128,128]{2,1,0:T(8,128)(2,1)}, u32[]{:S(2)}, u32[]{:S(2)}) collective-permute-start(bf16[32,128,128]{2,1,0:T(8,128)(2,1)S(1)} %features.3.refs_1_.refs_4_.refs_2_), channel_id=1, source_target_pairs={{0,16},{8,24},{32,48},{40,56},{64,80},{72,88},{96,112},{104,120},{... | collective-permute-start | bytes 3145736 | tf_op jit(solution)/shard_map/ppermute | solution.py:187
  44.6 0.6 collective-permute-done.7.refs_11_.refs_9_
  45.2 0.8 copy-done.2
  46.5 0.8 copy-done.5
  47.3 3.9 %collective-permute-done.16.refs_11_.refs_15_ = bf16[2,8,128,128]{3,2,1,0:T(8,128)(2,1)} collective-permute-done((bf16[2,8,128,128]{3,2,1,0:T(8,128)(2,1)S(1)}, bf16[2,8,128,128]{3,2,1,0:T(8,128)(2,1)}, u32[]{:S(2)}, u32[]{:S(2)}) %collective-permute-start.16) | collective-permute-done | bytes 524320 | tf_op jit(solution)/shard_map/ppermute | solution.py:187
  51.4 1.0 copy-done.3
  52.4 1.0 copy-done.6
  53.4 7.3 %gram.3 = (f32[384,256]{1,0:T(8,128)S(1)}, bf16[384,256]{1,0:T(8,128)(2,1)S(1)}, bf16[384,256]{1,0:T(8,128)(2,1)S(1)}, bf16[384,256]{1,0:T(8,128)(2,1)S(1)}) custom-call(s32[6]{0:T(128)S(1)} %pad_add_fusion.s_ref, bf16[32,128,128]{2,1,0:T(8,128)(2,1)S(1)} %features.2.refs_0_.refs_3_.refs_1_, bf16[32,128,128]{2,1,0:T(8,128)(2,1)} %copy-done.1, ...), custom_call_target="tpu_custom_call" | custom-call | flops 2013265920 | bytes 8388608 | tf_op jit(solution)/shard_map/gram/pallas_call | solution.py:151
  60.7 0.7 copy-done.12
  61.4 0.7 copy-done.16
  62.1 0.7 copy-done.18
  62.8 7.6 %gram.4 = (f32[384,256]{1,0:T(8,128)S(1)}, bf16[384,256]{1,0:T(8,128)(2,1)S(1)}, bf16[384,256]{1,0:T(8,128)(2,1)S(1)}, bf16[384,256]{1,0:T(8,128)(2,1)S(1)}) custom-call(s32[6]{0:T(128)S(1)} %pad_add_fusion.s_ref, bf16[32,128,128]{2,1,0:T(8,128)(2,1)S(1)} %features.2.refs_0_.refs_3_.refs_1_, bf16[32,128,128]{2,1,0:T(8,128)(2,1)} %copy-done.1, ...), custom_call_target="tpu_custom_call" | custom-call | flops 2013265920 | bytes 8388608 | tf_op jit(solution)/shard_map/gram/pallas_call | solution.py:151
  70.4 0.7 copy-done.10
  71.1 0.7 copy-done.14
  71.8 10.1 %gram.5 = (f32[128,512]{1,0:T(8,128)S(1)}, bf16[128,512]{1,0:T(8,128)(2,1)S(1)}, bf16[128,512]{1,0:T(8,128)(2,1)S(1)}, bf16[128,512]{1,0:T(8,128)(2,1)}) custom-call(s32[6]{0:T(128)S(1)} %pad_add_fusion.s_ref, bf16[32,128,128]{2,1,0:T(8,128)(2,1)} %collective-permute-done.21.refs_0_, bf16[32,128,128]{2,1,0:T(8,128)(2,1)} %copy-done, ...), custom_call_target="tpu_custom_call" | custom-call | flops 1342177280 | bytes 11534336 | tf_op jit(solution)/shard_map/gram/pallas_call | solution.py:151
  82.0 1.6 %collective-permute-start.22 = (bf16[128,512]{1,0:T(8,128)(2,1)S(1)}, bf16[128,512]{1,0:T(8,128)(2,1)S(1)}, u32[]{:S(2)}, u32[]{:S(2)}) collective-permute-start(bf16[128,512]{1,0:T(8,128)(2,1)S(1)} %get-tuple-element.46), channel_id=1, source_target_pairs={{0,2},{8,10},{32,34},{40,42},{64,66},{72,74},{96,98},{104,106},{1,... | collective-permute-start | bytes 393224 | tf_op jit(solution)/shard_map/ppermute | solution.py:187
  83.5 2.7 %collective-permute-start.23 = (bf16[128,512]{1,0:T(8,128)(2,1)S(1)}, bf16[128,512]{1,0:T(8,128)(2,1)S(1)}, u32[]{:S(2)}, u32[]{:S(2)}) collective-permute-start(bf16[128,512]{1,0:T(8,128)(2,1)S(1)} %get-tuple-element.47), channel_id=1, source_target_pairs={{0,4},{8,12},{32,36},{40,44},{64,68},{72,76},{96,100},{104,108},{1... | collective-permute-start | bytes 393224 | tf_op jit(solution)/shard_map/ppermute | solution.py:187
  86.3 1.4 %collective-permute-start.24 = (bf16[128,512]{1,0:T(8,128)(2,1)}, bf16[128,512]{1,0:T(8,128)(2,1)S(1)}, u32[]{:S(2)}, u32[]{:S(2)}) collective-permute-start(bf16[128,512]{1,0:T(8,128)(2,1)} %get-tuple-element.48), channel_id=1, source_target_pairs={{0,6},{8,14},{32,38},{40,46},{64,70},{72,78},{96,102},{104,110},{1... | collective-permute-start | bytes 393224 | tf_op jit(solution)/shard_map/ppermute | solution.py:187
  88.2 2.8 %collective-permute-start.11 = (bf16[384,256]{1,0:T(8,128)(2,1)}, bf16[384,256]{1,0:T(8,128)(2,1)S(1)}, u32[]{:S(2)}, u32[]{:S(2)}) collective-permute-start(bf16[384,256]{1,0:T(8,128)(2,1)} %copy-done.16), channel_id=1, source_target_pairs={{0,6},{8,14},{32,38},{40,46},{64,70},{72,78},{96,102},{104,110},{1... | collective-permute-start | bytes 589832 | tf_op jit(solution)/shard_map/ppermute | solution.py:187
  91.0 2.3 %collective-permute-done.23 = bf16[128,512]{1,0:T(8,128)(2,1)S(1)} collective-permute-done((bf16[128,512]{1,0:T(8,128)(2,1)S(1)}, bf16[128,512]{1,0:T(8,128)(2,1)S(1)}, u32[]{:S(2)}, u32[]{:S(2)}) %collective-permute-start.23) | collective-permute-done | bytes 131104 | tf_op jit(solution)/shard_map/ppermute | solution.py:187
  93.3 3.0 %collective-permute-start.19 = (bf16[384,256]{1,0:T(8,128)(2,1)S(1)}, bf16[384,256]{1,0:T(8,128)(2,1)S(1)}, u32[]{:S(2)}, u32[]{:S(2)}) collective-permute-start(bf16[384,256]{1,0:T(8,128)(2,1)S(1)} %copy-done.15), channel_id=1, source_target_pairs={{0,4},{8,12},{32,36},{40,44},{64,68},{72,76},{96,100},{104,108},{1... | collective-permute-start | bytes 589832 | tf_op jit(solution)/shard_map/ppermute | solution.py:187
  96.4 1.2 collective-permute-done.10
  97.6 2.6 %collective-permute-start.20 = (bf16[384,256]{1,0:T(8,128)(2,1)S(1)}, bf16[384,256]{1,0:T(8,128)(2,1)S(1)}, u32[]{:S(2)}, u32[]{:S(2)}) collective-permute-start(bf16[384,256]{1,0:T(8,128)(2,1)S(1)} %copy-done.11), channel_id=1, source_target_pairs={{0,6},{8,14},{32,38},{40,46},{64,70},{72,78},{96,102},{104,110},{1... | collective-permute-start | bytes 589832 | tf_op jit(solution)/shard_map/ppermute | solution.py:187
  100.2 1.5 %collective-permute-done.11 = bf16[384,256]{1,0:T(8,128)(2,1)S(1)} collective-permute-done((bf16[384,256]{1,0:T(8,128)(2,1)}, bf16[384,256]{1,0:T(8,128)(2,1)S(1)}, u32[]{:S(2)}, u32[]{:S(2)}) %collective-permute-start.11) | collective-permute-done | bytes 196640 | tf_op jit(solution)/shard_map/ppermute | solution.py:187
  101.8 4.1 %collective-permute-done.18 = bf16[384,256]{1,0:T(8,128)(2,1)S(1)} collective-permute-done((bf16[384,256]{1,0:T(8,128)(2,1)}, bf16[384,256]{1,0:T(8,128)(2,1)S(1)}, u32[]{:S(2)}, u32[]{:S(2)}) %collective-permute-start.18) | collective-permute-done | bytes 196640 | tf_op jit(solution)/shard_map/ppermute | solution.py:187
  105.9 4.0 %collective-permute-done.19 = bf16[384,256]{1,0:T(8,128)(2,1)S(1)} collective-permute-done((bf16[384,256]{1,0:T(8,128)(2,1)S(1)}, bf16[384,256]{1,0:T(8,128)(2,1)S(1)}, u32[]{:S(2)}, u32[]{:S(2)}) %collective-permute-start.19) | collective-permute-done | bytes 196640 | tf_op jit(solution)/shard_map/ppermute | solution.py:187
  110.1 0.5 collective-permute-start.25
  110.6 7.6 %collective-permute-done.25 = bf16[256,512]{1,0:T(8,128)(2,1)S(1)} collective-permute-done((bf16[256,512]{1,0:T(8,128)(2,1)S(1)}, bf16[256,512]{1,0:T(8,128)(2,1)S(1)}, u32[]{:S(2)}, u32[]{:S(2)}) %collective-permute-start.25) | collective-permute-done | bytes 262176 | tf_op jit(solution)/shard_map/ppermute | solution.py:187
  118.5 2.9 %collective-permute-start.27 = (bf16[256,256]{0,1:T(8,128)(2,1)S(1)}, bf16[256,256]{0,1:T(8,128)(2,1)S(1)}, u32[]{:S(2)}, u32[]{:S(2)}) collective-permute-start(bf16[256,256]{0,1:T(8,128)(2,1)S(1)} %get-tuple-element.55), channel_id=1, source_target_pairs={{32,2},{40,10},{64,4},{72,12},{96,6},{104,14},{33,3},{41,11},{65,5... | collective-permute-start | bytes 393224 | tf_op jit(solution)/shard_map/ppermute | solution.py:187
  121.4 4.6 %collective-permute-start.28 = (bf16[256,256]{0,1:T(8,128)(2,1)S(1)}, bf16[256,256]{0,1:T(8,128)(2,1)S(1)}, u32[]{:S(2)}, u32[]{:S(2)}) collective-permute-start(bf16[256,256]{0,1:T(8,128)(2,1)S(1)} %get-tuple-element.56), channel_id=1, source_target_pairs={{32,10},{40,2},{64,12},{72,4},{96,14},{104,6},{33,11},{41,3},{65,1... | collective-permute-start | bytes 393224 | tf_op jit(solution)/shard_map/ppermute | solution.py:187
  126.0 3.5 %collective-permute-start.26 = (bf16[256,512]{0,1:T(8,128)(2,1)S(1)}, bf16[256,512]{0,1:T(8,128)(2,1)S(1)}, u32[]{:S(2)}, u32[]{:S(2)}) collective-permute-start(bf16[256,512]{0,1:T(8,128)(2,1)S(1)} %copy.3), channel_id=1, source_target_pairs={{1,16},{9,24},{33,48},{41,56},{65,80},{73,88},{97,112},{105,120},{... | collective-permute-start | bytes 786440 | tf_op jit(solution)/shard_map/ppermute | solution.py:187
  129.5 3.2 %collective-permute-done.27 = bf16[256,256]{0,1:T(8,128)(2,1)S(1)} collective-permute-done((bf16[256,256]{0,1:T(8,128)(2,1)S(1)}, bf16[256,256]{0,1:T(8,128)(2,1)S(1)}, u32[]{:S(2)}, u32[]{:S(2)}) %collective-permute-start.27) | collective-permute-done | bytes 131104 | tf_op jit(solution)/shard_map/ppermute | solution.py:187
  132.7 2.1 %collective-permute-done.28 = bf16[256,256]{0,1:T(8,128)(2,1)S(1)} collective-permute-done((bf16[256,256]{0,1:T(8,128)(2,1)S(1)}, bf16[256,256]{0,1:T(8,128)(2,1)S(1)}, u32[]{:S(2)}, u32[]{:S(2)}) %collective-permute-start.28) | collective-permute-done | bytes 131104 | tf_op jit(solution)/shard_map/ppermute | solution.py:187
  134.8 1.4 %collective-permute-done.26 = bf16[256,512]{0,1:T(8,128)(2,1)S(1)} collective-permute-done((bf16[256,512]{0,1:T(8,128)(2,1)S(1)}, bf16[256,512]{0,1:T(8,128)(2,1)S(1)}, u32[]{:S(2)}, u32[]{:S(2)}) %collective-permute-start.26) | collective-permute-done | bytes 262176 | tf_op jit(solution)/shard_map/ppermute | solution.py:187
  136.4 0.9 add_multiply_fusion
  (73 shorter events, 3.7 us)
Async XLA Ops:
  4.6 58.2 %copy-start = (bf16[32,128,128]{2,1,0:T(8,128)(2,1)}, bf16[32,128,128]{2,1,0:T(8,128)(2,1)S(1)}, u32[]{:S(2)}) copy-start(bf16[32,128,128]{2,1,0:T(8,128)(2,1)S(1)} %features.2.refs_0_.refs_3_.refs_1_) | copy-start | bytes 3145732
  4.6 5.3 %collective-permute-start.1 = (bf16[32,128,128]{2,1,0:T(8,128)(2,1)S(1)}, bf16[32,128,128]{2,1,0:T(8,128)(2,1)}, u32[]{:S(2)}, u32[]{:S(2)}) collective-permute-start(bf16[32,128,128]{2,1,0:T(8,128)(2,1)S(1)} %features.2.refs_0_.refs_3_.refs_1_), channel_id=1, source_target_pairs={{0,8},{8,0},{32,40},{40,32},{64,72},{72,64},{96,104},{104,96},{1,9... | collective-permute-start | bytes 3145736 | tf_op jit(solution)/shard_map/ppermute | solution.py:187
  9.6 41.8 %copy-start.1 = (bf16[32,128,128]{2,1,0:T(8,128)(2,1)}, bf16[32,128,128]{2,1,0:T(8,128)(2,1)S(1)}, u32[]{:S(2)}) copy-start(bf16[32,128,128]{2,1,0:T(8,128)(2,1)S(1)} %features.3.refs_1_.refs_4_.refs_2_) | copy-start | bytes 3145732
  9.6 2.9 %collective-permute-start.2 = (bf16[32,128,128]{2,1,0:T(8,128)(2,1)S(1)}, bf16[32,128,128]{2,1,0:T(8,128)(2,1)}, u32[]{:S(2)}, u32[]{:S(2)}) collective-permute-start(bf16[32,128,128]{2,1,0:T(8,128)(2,1)S(1)} %features.3.refs_1_.refs_4_.refs_2_), channel_id=1, source_target_pairs={{0,8},{8,0},{32,40},{40,32},{64,72},{72,64},{96,104},{104,96},{1,9... | collective-permute-start | bytes 3145736 | tf_op jit(solution)/shard_map/ppermute | solution.py:187
  12.0 10.6 %collective-permute-start.3 = (bf16[16,128,128]{2,1,0:T(8,128)(2,1)}, bf16[16,128,128]{2,1,0:T(8,128)(2,1)S(1)}, u32[]{:S(2)}, u32[]{:S(2)}) collective-permute-start(bf16[16,128,128]{2,1,0:T(8,128)(2,1)} %get-tuple-element.52), channel_id=1, source_target_pairs={{0,96},{8,40},{32,0},{40,72},{64,32},{72,104},{96,64},{104,8},{1,9... | collective-permute-start | bytes 1572872 | tf_op jit(solution)/shard_map/ppermute | solution.py:187
  14.6 13.7 %collective-permute-start.4 = (bf16[16,128,128]{2,1,0:T(8,128)(2,1)}, bf16[16,128,128]{2,1,0:T(8,128)(2,1)S(1)}, u32[]{:S(2)}, u32[]{:S(2)}) collective-permute-start(bf16[16,128,128]{2,1,0:T(8,128)(2,1)} %get-tuple-element.50), channel_id=1, source_target_pairs={{0,96},{8,40},{32,0},{40,72},{64,32},{72,104},{96,64},{104,8},{1,9... | collective-permute-start | bytes 1572872 | tf_op jit(solution)/shard_map/ppermute | solution.py:187
  15.0 19.0 %collective-permute-start.13 = (bf16[16,128,128]{2,1,0:T(8,128)(2,1)}, bf16[16,128,128]{2,1,0:T(8,128)(2,1)}, u32[]{:S(2)}, u32[]{:S(2)}) collective-permute-start(bf16[16,128,128]{2,1,0:T(8,128)(2,1)} %get-tuple-element.49), channel_id=1, source_target_pairs={{0,96},{8,40},{32,0},{40,72},{64,32},{72,104},{96,64},{104,8},{1,9... | collective-permute-start | bytes 1572872 | tf_op jit(solution)/shard_map/ppermute | solution.py:187
  15.1 27.2 %collective-permute-start = (bf16[32,128,128]{2,1,0:T(8,128)(2,1)S(1)}, bf16[32,128,128]{2,1,0:T(8,128)(2,1)}, u32[]{:S(2)}, u32[]{:S(2)}) collective-permute-start(bf16[32,128,128]{2,1,0:T(8,128)(2,1)S(1)} %features.2.refs_0_.refs_3_.refs_1_), channel_id=1, source_target_pairs={{0,16},{8,24},{32,48},{40,56},{64,80},{72,88},{96,112},{104,120},{... | collective-permute-start | bytes 3145736 | tf_op jit(solution)/shard_map/ppermute | solution.py:187
  17.4 22.2 %collective-permute-start.12 = (bf16[16,128,128]{2,1,0:T(8,128)(2,1)}, bf16[16,128,128]{2,1,0:T(8,128)(2,1)}, u32[]{:S(2)}, u32[]{:S(2)}) collective-permute-start(bf16[16,128,128]{2,1,0:T(8,128)(2,1)} %get-tuple-element.51), channel_id=1, source_target_pairs={{0,96},{8,40},{32,0},{40,72},{64,32},{72,104},{96,64},{104,8},{1,9... | collective-permute-start | bytes 1572872 | tf_op jit(solution)/shard_map/ppermute | solution.py:187
  28.3 16.9 %collective-permute-start.7 = (bf16[2,8,128,128]{3,2,1,0:T(8,128)(2,1)S(1)}, bf16[2,8,128,128]{3,2,1,0:T(8,128)(2,1)}, u32[]{:S(2)}, u32[]{:S(2)}) collective-permute-start(bf16[2,8,128,128]{3,2,1,0:T(8,128)(2,1)S(1)} %pad_maximum_fusion.1), channel_id=1, source_target_pairs={{0,96},{8,40},{32,0},{40,72},{64,32},{72,104},{96,64},{104,8},{1,9... | collective-permute-start | bytes 1572872 | tf_op jit(solution)/shard_map/ppermute | solution.py:187
  28.4 16.8 %collective-permute-start.5 = (bf16[16,128,128]{2,1,0:T(8,128)(2,1)S(1)}, bf16[16,128,128]{2,1,0:T(8,128)(2,1)S(1)}, u32[]{:S(2)}, u32[]{:S(2)}) collective-permute-start(bf16[16,128,128]{2,1,0:T(8,128)(2,1)S(1)} %collective-permute-done.3.refs_7_.refs_5_), channel_id=1, source_target_pairs={{0,8},{8,0},{32,40},{40,32},{64,72},{72,64},{96,104},{104,96},{1,9... | collective-permute-start | bytes 1572872 | tf_op jit(solution)/shard_map/ppermute | solution.py:187
  34.0 12.5 %collective-permute-start.6 = (bf16[16,128,128]{2,1,0:T(8,128)(2,1)S(1)}, bf16[16,128,128]{2,1,0:T(8,128)(2,1)S(1)}, u32[]{:S(2)}, u32[]{:S(2)}) collective-permute-start(bf16[16,128,128]{2,1,0:T(8,128)(2,1)S(1)} %collective-permute-done.4.refs_8_.refs_6_), channel_id=1, source_target_pairs={{0,8},{8,0},{32,40},{40,32},{64,72},{72,64},{96,104},{104,96},{1,9... | collective-permute-start | bytes 1572872 | tf_op jit(solution)/shard_map/ppermute | solution.py:187
  40.6 10.6 %collective-permute-start.16 = (bf16[2,8,128,128]{3,2,1,0:T(8,128)(2,1)S(1)}, bf16[2,8,128,128]{3,2,1,0:T(8,128)(2,1)}, u32[]{:S(2)}, u32[]{:S(2)}) collective-permute-start(bf16[2,8,128,128]{3,2,1,0:T(8,128)(2,1)S(1)} %pad_maximum_fusion.2), channel_id=1, source_target_pairs={{0,96},{8,40},{32,0},{40,72},{64,32},{72,104},{96,64},{104,8},{1,9... | collective-permute-start | bytes 1572872 | tf_op jit(solution)/shard_map/ppermute | solution.py:187
  42.3 29.5 %collective-permute-start.21 = (bf16[32,128,128]{2,1,0:T(8,128)(2,1)S(1)}, bf16[32,128,128]{2,1,0:T(8,128)(2,1)}, u32[]{:S(2)}, u32[]{:S(2)}) collective-permute-start(bf16[32,128,128]{2,1,0:T(8,128)(2,1)S(1)} %features.3.refs_1_.refs_4_.refs_2_), channel_id=1, source_target_pairs={{0,16},{8,24},{32,48},{40,56},{64,80},{72,88},{96,112},{104,120},{... | collective-permute-start | bytes 3145736 | tf_op jit(solution)/shard_map/ppermute | solution.py:187
  45.2 6.1 %collective-permute-start.8 = (bf16[2,8,128,128]{3,2,1,0:T(8,128)(2,1)}, bf16[2,8,128,128]{3,2,1,0:T(8,128)(2,1)}, u32[]{:S(2)}, u32[]{:S(2)}) collective-permute-start(bf16[2,8,128,128]{3,2,1,0:T(8,128)(2,1)} %collective-permute-done.7.refs_11_.refs_9_), channel_id=1, source_target_pairs={{0,8},{8,0},{32,40},{40,32},{64,72},{72,64},{96,104},{104,96},{1,9... | collective-permute-start | bytes 1572872 | tf_op jit(solution)/shard_map/ppermute | solution.py:187
  45.2 0.8 copy-start.2
  46.0 16.8 %collective-permute-start.14 = (bf16[16,128,128]{2,1,0:T(8,128)(2,1)}, bf16[16,128,128]{2,1,0:T(8,128)(2,1)}, u32[]{:S(2)}, u32[]{:S(2)}) collective-permute-start(bf16[16,128,128]{2,1,0:T(8,128)(2,1)} %collective-permute-done.12.refs_7_.refs_11_), channel_id=1, source_target_pairs={{0,8},{8,0},{32,40},{40,32},{64,72},{72,64},{96,104},{104,96},{1,9... | collective-permute-start | bytes 1572872 | tf_op jit(solution)/shard_map/ppermute | solution.py:187
  46.5 0.8 copy-start.5
  47.3 15.5 %collective-permute-start.15 = (bf16[16,128,128]{2,1,0:T(8,128)(2,1)}, bf16[16,128,128]{2,1,0:T(8,128)(2,1)}, u32[]{:S(2)}, u32[]{:S(2)}) collective-permute-start(bf16[16,128,128]{2,1,0:T(8,128)(2,1)} %collective-permute-done.13.refs_8_.refs_12_), channel_id=1, source_target_pairs={{0,8},{8,0},{32,40},{40,32},{64,72},{72,64},{96,104},{104,96},{1,9... | collective-permute-start | bytes 1572872 | tf_op jit(solution)/shard_map/ppermute | solution.py:187
  51.2 11.6 %collective-permute-start.17 = (bf16[2,8,128,128]{3,2,1,0:T(8,128)(2,1)}, bf16[2,8,128,128]{3,2,1,0:T(8,128)(2,1)}, u32[]{:S(2)}, u32[]{:S(2)}) collective-permute-start(bf16[2,8,128,128]{3,2,1,0:T(8,128)(2,1)} %collective-permute-done.16.refs_11_.refs_15_), channel_id=1, source_target_pairs={{0,8},{8,0},{32,40},{40,32},{64,72},{72,64},{96,104},{104,96},{1,9... | collective-permute-start | bytes 1572872 | tf_op jit(solution)/shard_map/ppermute | solution.py:187
  51.3 1.0 copy-start.3
  52.4 1.0 copy-start.6
  53.4 18.4 %copy-start.4 = (bf16[16,128,128]{2,1,0:T(8,128)(2,1)S(1)}, bf16[16,128,128]{2,1,0:T(8,128)(2,1)}, u32[]{:S(2)}) copy-start(bf16[16,128,128]{2,1,0:T(8,128)(2,1)} %copy-done.2) | copy-start | bytes 1572868
  53.4 18.4 %copy-start.7 = (bf16[16,128,128]{2,1,0:T(8,128)(2,1)S(1)}, bf16[16,128,128]{2,1,0:T(8,128)(2,1)}, u32[]{:S(2)}) copy-start(bf16[16,128,128]{2,1,0:T(8,128)(2,1)} %copy-done.5) | copy-start | bytes 1572868
  60.7 0.7 copy-start.12
  61.4 0.7 copy-start.16
  62.1 0.7 copy-start.18
  62.8 7.6 %copy-start.8 = (f32[384,256]{1,0:T(8,128)}, f32[384,256]{1,0:T(8,128)S(1)}, u32[]{:S(2)}) copy-start(f32[384,256]{1,0:T(8,128)S(1)} %get-tuple-element.31) | copy-start | bytes 1179652
  70.4 0.7 copy-start.10
  71.1 0.7 copy-start.14
  71.8 10.2 %copy-start.17 = (bf16[384,256]{1,0:T(8,128)(2,1)}, bf16[384,256]{1,0:T(8,128)(2,1)S(1)}, u32[]{:S(2)}) copy-start(bf16[384,256]{1,0:T(8,128)(2,1)S(1)} %get-tuple-element.41) | copy-start | bytes 589828
  71.8 19.2 %copy-start.13 = (bf16[384,256]{1,0:T(8,128)(2,1)S(1)}, bf16[384,256]{1,0:T(8,128)(2,1)}, u32[]{:S(2)}) copy-start(bf16[384,256]{1,0:T(8,128)(2,1)} %copy-done.12) | copy-start | bytes 589828
  71.8 25.8 %copy-start.11 = (bf16[384,256]{1,0:T(8,128)(2,1)S(1)}, bf16[384,256]{1,0:T(8,128)(2,1)}, u32[]{:S(2)}) copy-start(bf16[384,256]{1,0:T(8,128)(2,1)} %copy-done.10) | copy-start | bytes 589828
  71.8 29.9 %copy-start.9 = (f32[384,256]{1,0:T(8,128)S(1)}, f32[384,256]{1,0:T(8,128)}, u32[]{:S(2)}) copy-start(f32[384,256]{1,0:T(8,128)} %copy-done.8) | copy-start | bytes 1179652
  71.8 21.5 %copy-start.15 = (bf16[384,256]{1,0:T(8,128)(2,1)S(1)}, bf16[384,256]{1,0:T(8,128)(2,1)}, u32[]{:S(2)}) copy-start(bf16[384,256]{1,0:T(8,128)(2,1)} %copy-done.14) | copy-start | bytes 589828
  82.0 9.0 %collective-permute-start.22 = (bf16[128,512]{1,0:T(8,128)(2,1)S(1)}, bf16[128,512]{1,0:T(8,128)(2,1)S(1)}, u32[]{:S(2)}, u32[]{:S(2)}) collective-permute-start(bf16[128,512]{1,0:T(8,128)(2,1)S(1)} %get-tuple-element.46), channel_id=1, source_target_pairs={{0,2},{8,10},{32,34},{40,42},{64,66},{72,74},{96,98},{104,106},{1,... | collective-permute-start | bytes 393224 | tf_op jit(solution)/shard_map/ppermute | solution.py:187
  83.5 9.8 %collective-permute-start.23 = (bf16[128,512]{1,0:T(8,128)(2,1)S(1)}, bf16[128,512]{1,0:T(8,128)(2,1)S(1)}, u32[]{:S(2)}, u32[]{:S(2)}) collective-permute-start(bf16[128,512]{1,0:T(8,128)(2,1)S(1)} %get-tuple-element.47), channel_id=1, source_target_pairs={{0,4},{8,12},{32,36},{40,44},{64,68},{72,76},{96,100},{104,108},{1... | collective-permute-start | bytes 393224 | tf_op jit(solution)/shard_map/ppermute | solution.py:187
  86.3 7.1 %collective-permute-start.24 = (bf16[128,512]{1,0:T(8,128)(2,1)}, bf16[128,512]{1,0:T(8,128)(2,1)S(1)}, u32[]{:S(2)}, u32[]{:S(2)}) collective-permute-start(bf16[128,512]{1,0:T(8,128)(2,1)} %get-tuple-element.48), channel_id=1, source_target_pairs={{0,6},{8,14},{32,38},{40,46},{64,70},{72,78},{96,102},{104,110},{1... | collective-permute-start | bytes 393224 | tf_op jit(solution)/shard_map/ppermute | solution.py:187
  87.7 9.9 %collective-permute-start.10 = (bf16[384,256]{1,0:T(8,128)(2,1)}, bf16[384,256]{1,0:T(8,128)(2,1)S(1)}, u32[]{:S(2)}, u32[]{:S(2)}) collective-permute-start(bf16[384,256]{1,0:T(8,128)(2,1)} %copy-done.18), channel_id=1, source_target_pairs={{0,4},{8,12},{32,36},{40,44},{64,68},{72,76},{96,100},{104,108},{1... | collective-permute-start | bytes 589832 | tf_op jit(solution)/shard_map/ppermute | solution.py:187
  88.2 13.5 %collective-permute-start.11 = (bf16[384,256]{1,0:T(8,128)(2,1)}, bf16[384,256]{1,0:T(8,128)(2,1)S(1)}, u32[]{:S(2)}, u32[]{:S(2)}) collective-permute-start(bf16[384,256]{1,0:T(8,128)(2,1)} %copy-done.16), channel_id=1, source_target_pairs={{0,6},{8,14},{32,38},{40,46},{64,70},{72,78},{96,102},{104,110},{1... | collective-permute-start | bytes 589832 | tf_op jit(solution)/shard_map/ppermute | solution.py:187
  91.0 10.8 %collective-permute-start.9 = (bf16[384,256]{1,0:T(8,128)(2,1)S(1)}, bf16[384,256]{1,0:T(8,128)(2,1)S(1)}, u32[]{:S(2)}, u32[]{:S(2)}) collective-permute-start(bf16[384,256]{1,0:T(8,128)(2,1)S(1)} %copy-done.13), channel_id=1, source_target_pairs={{0,2},{8,10},{32,34},{40,42},{64,66},{72,74},{96,98},{104,106},{1,... | collective-permute-start | bytes 589832 | tf_op jit(solution)/shard_map/ppermute | solution.py:187
  93.3 12.6 %collective-permute-start.18 = (bf16[384,256]{1,0:T(8,128)(2,1)}, bf16[384,256]{1,0:T(8,128)(2,1)S(1)}, u32[]{:S(2)}, u32[]{:S(2)}) collective-permute-start(bf16[384,256]{1,0:T(8,128)(2,1)} %copy-done.17), channel_id=1, source_target_pairs={{0,2},{8,10},{32,34},{40,42},{64,66},{72,74},{96,98},{104,106},{1,... | collective-permute-start | bytes 589832 | tf_op jit(solution)/shard_map/ppermute | solution.py:187
  93.3 16.6 %collective-permute-start.19 = (bf16[384,256]{1,0:T(8,128)(2,1)S(1)}, bf16[384,256]{1,0:T(8,128)(2,1)S(1)}, u32[]{:S(2)}, u32[]{:S(2)}) collective-permute-start(bf16[384,256]{1,0:T(8,128)(2,1)S(1)} %copy-done.15), channel_id=1, source_target_pairs={{0,4},{8,12},{32,36},{40,44},{64,68},{72,76},{96,100},{104,108},{1... | collective-permute-start | bytes 589832 | tf_op jit(solution)/shard_map/ppermute | solution.py:187
  97.6 12.4 %collective-permute-start.20 = (bf16[384,256]{1,0:T(8,128)(2,1)S(1)}, bf16[384,256]{1,0:T(8,128)(2,1)S(1)}, u32[]{:S(2)}, u32[]{:S(2)}) collective-permute-start(bf16[384,256]{1,0:T(8,128)(2,1)S(1)} %copy-done.11), channel_id=1, source_target_pairs={{0,6},{8,14},{32,38},{40,46},{64,70},{72,78},{96,102},{104,110},{1... | collective-permute-start | bytes 589832 | tf_op jit(solution)/shard_map/ppermute | solution.py:187
  110.1 8.1 %collective-permute-start.25 = (bf16[256,512]{1,0:T(8,128)(2,1)S(1)}, bf16[256,512]{1,0:T(8,128)(2,1)S(1)}, u32[]{:S(2)}, u32[]{:S(2)}) collective-permute-start(bf16[256,512]{1,0:T(8,128)(2,1)S(1)} %select_convert_fusion), channel_id=1, source_target_pairs={{0,1},{8,9},{32,33},{40,41},{64,65},{72,73},{96,97},{104,105},{1,0... | collective-permute-start | bytes 786440 | tf_op jit(solution)/shard_map/ppermute | solution.py:187
  118.5 14.2 %collective-permute-start.27 = (bf16[256,256]{0,1:T(8,128)(2,1)S(1)}, bf16[256,256]{0,1:T(8,128)(2,1)S(1)}, u32[]{:S(2)}, u32[]{:S(2)}) collective-permute-start(bf16[256,256]{0,1:T(8,128)(2,1)S(1)} %get-tuple-element.55), channel_id=1, source_target_pairs={{32,2},{40,10},{64,4},{72,12},{96,6},{104,14},{33,3},{41,11},{65,5... | collective-permute-start | bytes 393224 | tf_op jit(solution)/shard_map/ppermute | solution.py:187
  121.4 13.3 %collective-permute-start.28 = (bf16[256,256]{0,1:T(8,128)(2,1)S(1)}, bf16[256,256]{0,1:T(8,128)(2,1)S(1)}, u32[]{:S(2)}, u32[]{:S(2)}) collective-permute-start(bf16[256,256]{0,1:T(8,128)(2,1)S(1)} %get-tuple-element.56), channel_id=1, source_target_pairs={{32,10},{40,2},{64,12},{72,4},{96,14},{104,6},{33,11},{41,3},{65,1... | collective-permute-start | bytes 393224 | tf_op jit(solution)/shard_map/ppermute | solution.py:187
  126.0 10.2 %collective-permute-start.26 = (bf16[256,512]{0,1:T(8,128)(2,1)S(1)}, bf16[256,512]{0,1:T(8,128)(2,1)S(1)}, u32[]{:S(2)}, u32[]{:S(2)}) collective-permute-start(bf16[256,512]{0,1:T(8,128)(2,1)S(1)} %copy.3), channel_id=1, source_target_pairs={{1,16},{9,24},{33,48},{41,56},{65,80},{73,88},{97,112},{105,120},{... | collective-permute-start | bytes 786440 | tf_op jit(solution)/shard_map/ppermute | solution.py:187

commit v3 on v0

v3 whole, which is shorter than its diff:
```python
import functools
import jax
import jax.numpy as jnp
from jax import lax
from jax.experimental import pallas as pl
from jax.experimental.pallas import tpu as pltpu
from jax.sharding import PartitionSpec as P

NT = (((1,), (1,)), ((), ()))
AXES = ("dp", "layer")
HALF = 16
QUARTER = 8
PITCH = 68


def feature_kernel(s_ref, g_ref, i_ref, full_ref, *refs):
    pieces, prod = refs[:4], refs[4]
    n = g_ref.shape[1]
    for e in range(0, n, 4):
        four = lax.dot_general(
            g_ref[0, e : e + 4].reshape(256, 256),
            i_ref[0, e : e + 4].reshape(256, 256),
            NT,
            preferred_element_type=jnp.float32,
        )
        for k in range(4):
            prod[pl.ds((e + k) * PITCH, 64), :] = four[64 * k : 64 * k + 64, 128 * (k // 2) : 128 * (k // 2) + 128]
    even = lax.broadcasted_iota(jnp.int32, (n, 128), 0) % 2 == 0
    left = lax.broadcasted_iota(jnp.int32, (n, 128), 1) < 64
    in_place = even == left
    ahead = s_ref[0]
    for k, piece in enumerate(pieces):
        tile = k // 2 * HALF + (ahead if k % 2 == 0 else 1 - ahead) * QUARTER
        for t in range(QUARTER):
            first = prod[pl.ds(2 * tile + 2 * t, n, stride=PITCH), :]
            second = prod[pl.ds(2 * tile + 2 * t + 1, n, stride=PITCH), :]
            moved = pltpu.roll(jnp.where(even, second, first), 64, 1)
            value = jnp.where(in_place, jnp.where(even, first, second), moved).astype(jnp.bfloat16)
            piece[t] = value
            full_ref[tile + t] = value


FREE = pl.CostEstimate(flops=1, bytes_accessed=1, transcendentals=0)
IN_SMEM = pl.BlockSpec(memory_space=pltpu.SMEM)
IN_VMEM = pl.BlockSpec(memory_space=pltpu.VMEM)


def on_chip(*arrays):
    return [pltpu.with_memory_space_constraint(a, pltpu.VMEM) for a in arrays]


def features(ahead, g, i, n=64):
    count = g.shape[1]
    block = lambda tiles: pl.BlockSpec((tiles, n, 128), lambda s, a: (0, s, 0))
    shape = lambda tiles: jax.ShapeDtypeStruct((tiles, count, 128), jnp.bfloat16)
    return pl.pallas_call(
        feature_kernel,
        grid_spec=pltpu.PrefetchScalarGridSpec(
            num_scalar_prefetch=1,
            grid=(count // n,),
            in_specs=[pl.BlockSpec((1, n, 64, 256), lambda s, a: (0, s, 0, 0))] * 2,
            out_specs=[block(2 * HALF)] + [block(QUARTER)] * 4,
            scratch_shapes=[pltpu.VMEM((n * PITCH, 128), jnp.float32)],
        ),
        out_shape=[shape(2 * HALF)] + [shape(QUARTER)] * 4,
        compiler_params=pltpu.CompilerParams(vmem_limit_bytes=24 << 20),
        cost_estimate=FREE,
        name="features",
    )(ahead.reshape(1), *(pltpu.with_memory_space_constraint(a, pltpu.HBM) for a in (g, i)))


def wide(ref, first, count):
    return jnp.concatenate([ref[first + t] for t in range(count)], axis=1)


def gram_kernel(n_rows, s_ref, *refs):
    rows, (own, up_a, up_b, down_a, down_b, two_up, two_down) = refs[:n_rows], refs[n_rows : n_rows + 7]
    outs, slot = refs[-5:-1], refs[-1]

    def dot(left, right):
        return lax.dot_general(left, right, NT, preferred_element_type=jnp.float32)

    def beside(a, b):
        return jnp.concatenate([a, b], axis=1)

    def tall(first, count):
        return jnp.concatenate([wide(part, first, count) for part in rows], axis=0)

    def two_quarters(a, b):
        return beside(tall(a * QUARTER, QUARTER), tall(b * QUARTER, QUARTER))

    def pair(a, b):
        return beside(wide(a, 0, QUARTER), wide(b, 0, QUARTER))

    slot[s_ref[0]] = dot(tall(0, 2 * HALF), wide(own, 0, 2 * HALF))
    slot[s_ref[1]] = dot(two_quarters(s_ref[5], 1 - s_ref[5]), pair(up_a, up_b))
    slot[s_ref[2]] = dot(two_quarters(2 + s_ref[6], 3 - s_ref[6]), pair(down_a, down_b))
    slot[s_ref[3]] = dot(two_quarters(s_ref[4], 2 + s_ref[4]), pair(two_up, two_down))
    for d in range(4):
        outs[d][...] = slot[d].astype(outs[d].dtype)


def gram(scalars, rows, columns):
    count, width = len(rows) * rows[0].shape[1], columns[0].shape[1]
    operands = [*rows, *columns]
    return pl.pallas_call(
        functools.partial(gram_kernel, len(rows)),
        in_specs=[IN_SMEM] + [IN_VMEM] * len(operands),
        out_specs=[IN_VMEM] * 4,
        out_shape=[jax.ShapeDtypeStruct((count, width), jnp.float32)]
        + [jax.ShapeDtypeStruct((count, width), jnp.bfloat16)] * 3,
        scratch_shapes=[pltpu.VMEM((4, count, width), jnp.float32)],
        compiler_params=pltpu.CompilerParams(vmem_limit_bytes=16 << 20),
        cost_estimate=FREE,
        name="gram",
    )(scalars, *on_chip(*operands))


def device(x, y, z, c):
    x, y, z = x % 4, y % 4, z % 4
    return ((z * 2 + y // 2) * 2 + c) * 8 + x * 2 + y % 2


def shift(array, move):
    pairs = []
    for x in range(4):
        for y in range(4):
            for z in range(4):
                for c in range(2):
                    place = move(x, y, z, c)
                    if place is not None:
                        pairs.append((device(x, y, z, c), device(*place)))
    return lax.ppermute(array, AXES, pairs)


def other_core(x, y, z, c):
    return x, y, z, 1 - c


def other_half(x, y, z, c):
    return x, y + 2, z, c


def z_down(x, y, z, c):
    return x, y, z - 1, c


def z_up(x, y, z, c):
    return x, y, z + 1, c


def body(grads_proj, inputs_proj):
    f32, bf16 = jnp.float32, jnp.bfloat16
    after = lax.optimization_barrier
    dp = lax.axis_index("dp").astype(jnp.int32)
    layer = lax.axis_index("layer").astype(jnp.int32)
    core = dp % 2
    z = dp // 4
    y = (dp // 2) % 2 * 2 + layer % 2
    x = layer // 2
    half = lambda at: at % 4 // 2
    scalars = jnp.stack([z - x, z + 1 - x, z + 3 - x, z + 2 - x]) % 4
    scalars = jnp.concatenate([scalars, jnp.stack([half(z), 1 - half(z + 1), 1 - half(z - 1)])]).astype(jnp.int32)

    own, *pieces = features(1 - half(z), grads_proj, inputs_proj)
    up_a, down_a = shift(pieces[0], z_down), shift(pieces[2], z_up)
    up_b, down_b = shift(pieces[1], z_down), shift(pieces[3], z_up)
    mate, far = shift(own, other_core), shift(own, other_half)
    columns = [own, up_a, up_b, down_a, down_b, shift(up_a, z_down), shift(down_a, z_up)]

    def over_x(parts):
        moved = (
            shift(parts[1], lambda x, y, z, c: (x + 1, y, z, c)),
            shift(parts[2], lambda x, y, z, c: (x + 2, y, z, c)),
            shift(parts[3], lambda x, y, z, c: (x - 1, y, z, c)),
        )
        return (parts[0] + moved[0].astype(f32)) + (moved[1].astype(f32) + moved[2].astype(f32))

    near = gram(scalars, [own, mate], columns)
    near, far = after((near, far))
    near_sum = over_x(near)
    far_one = gram(scalars, [far], columns)
    far_mate = shift(far, other_core)
    far_one, far_mate = after((far_one, far_mate))
    far_two = gram(scalars, [far_mate], columns)

    edge = (y == 0) | (y == 3)

    def over_y(near_part, far_part):
        give = jnp.where(edge, far_part, near_part).astype(bf16)
        keep = jnp.where(edge, near_part, far_part)
        return keep + shift(give, lambda x, y, z, c: (x, y ^ 1, z, c)).astype(f32)

    def across(part):
        return shift(part, lambda x, y, z, c: (z, y, x, c) if x != z else None)

    one = over_y(near_sum[:256], over_x(far_one))
    sent_one = one.astype(bf16)
    turn_one = across(sent_one)
    here = shift(sent_one, lambda x, y, z, c: (x, 3 - y, z, c) if y in (1, 2) else None).astype(f32)
    here = jnp.where(edge, one, here)
    two = over_y(near_sum[256:], over_x(far_two))
    sent_two = two.astype(bf16)
    turn_two = across(sent_two)
    there = shift(sent_two, lambda x, y, z, c: (x, 3 - y if y in (1, 2) else y, z, 1 - c)).astype(f32)
    here = here + turn_one.T.astype(f32)
    there = there + turn_two.T.astype(f32)
    out = jnp.concatenate([jnp.where(core == 0, here, there), jnp.where(core == 0, there, here)], axis=1)
    return out * (1.0 / (256.0 * jnp.sqrt(f32(8 * 4096))))


def solution(mesh):
    return jax.shard_map(
        body,
        mesh=mesh,
        in_specs=(P("layer", "dp", None, None), P("layer", "dp", None, None)),
        out_specs=P("dp", "layer"),
        check_vma=False,
    )
```

time: 343 us -> 121 us (0.35)
  waiting for transfers between devices: 291 us -> 52.9 us
  starting transfers between devices: 0.04 us -> 36 us
  matrix products: 27 us -> 0 us
  Pallas kernels: 0 us -> 22.6 us
  between operations: 13.4 us -> 0.16 us
    all_gather x1 -> x0, waiting for transfers between devices: 202 us -> none  [body(): lax.all_gather(features, 'dp', axis=0, tiled=True)]
    reduce_scatter x1 -> x0, waiting for transfers between devices: 89.5 us -> none  [body(): lax.psum_scatter(partial_gram, 'layer', scatter_dimension=1, tiled=True)]
    ppermute x0 -> x24, waiting for transfers between devices: none -> 52.9 us  [shift(): return lax.ppermute(array, AXES, pairs)]
    ppermute x0 -> x24, starting transfers between devices: none -> 36 us  [shift(): return lax.ppermute(array, AXES, pairs)]
    dot_general x2 -> x0, matrix products: 27 us -> none  [the longest x1 17 us: contract(): lax.dot_general(left, right, (((1,), (1,)), ((), ())), preferred_element_...]
    pallas_call x0 -> x4, Pallas kernels: none -> 22.6 us  [the longest x3 13.7 us: gram(): pl.pallas_call(functools.partial(gram_kernel, len(rows)), in_specs=[IN_SM...]
    convert_element_type x1, local copies, waits for them, and re-layouts: 5.88 us -> 0.1 us  [body(): sent_two = two.astype(bf16)]
    unnamed x0 -> x10, local copies, waits for them, and re-layouts: none -> 4.38 us
  transfers between devices with their start and end apart: 2 -> 24, of which waited for: 2 -> 11; matrix products, arithmetic and copies ran while one was open for 0% -> 1% of each run, Pallas kernels for 0% -> 11%
where the time goes in v3:
time: 121 us
  waiting for transfers between devices  52.9 us (44%)
  starting transfers between devices  36 us (30%)
  Pallas kernels  22.6 us (19%)
  local copies, waits for them, and re-layouts  5.61 us (5%)
  other arithmetic  3.62 us (3%)
    ppermute x24, waiting for transfers between devices, shift(): return lax.ppermute(array, AXES, pairs)  52.9 us
    ppermute x24, starting transfers between devices, shift(): return lax.ppermute(array, AXES, pairs)  36 us
    pallas_call x3, Pallas kernels, gram(): pl.pallas_call(functools.partial(gram_kernel, len(rows)), in_specs=[IN_SM...  13.7 us
    pallas_call x1, Pallas kernels, features(): pl.pallas_call(feature_kernel, grid_spec=pltpu.PrefetchScalarGridSpec(num...  8.93 us
    unnamed x10, local copies, waits for them, and re-layouts  4.38 us
  transfers between devices with their start and end apart: 24, of which 11 were waited for; matrix products, arithmetic and copies ran while one was open for 1% of the time, Pallas kernels for 11%

profile of v3, /device:TPU:104, one launch (start us, length us, event | category | flops | bytes accessed | tf_op | source)
XLA Modules:
  0.0 121.0 jit_solution(2812048507163081855)
XLA Ops:
  0.0 8.9 %features.1 = (bf16[32,256,128]{2,1,0:T(8,128)(2,1)S(1)}, bf16[8,256,128]{2,1,0:T(8,128)(2,1)S(1)}, bf16[8,256,128]{2,1,0:T(8,128)(2,1)S(1)}, bf16[8,256,128]{2,1,0:T(8,128)(2,1)S(1)}, bf16[8,256,128]{2,1,0:T(8,128)(2,1)}) custom-call(s32[1]{0:T(128)} %bitcast.7.s_ref, bf16[1,256,64,256]{3,2,1,0:T(8,128)(2,1)} %g_ref.1, bf16[1,256,64,256]{3,2,1,0:T(8,128)(2,1)} %i_ref.1), custom_call_target="tpu_custom_call" | custom-call | flops 1 | bytes 1 | tf_op jit(solution)/shard_map/features/pallas_call | solution.py:56
  8.9 2.3 %collective-permute-start.7 = (bf16[32,256,128]{2,1,0:T(8,128)(2,1)S(1)}, bf16[32,256,128]{2,1,0:T(8,128)(2,1)}, u32[]{:S(2)}, u32[]{:S(2)}) collective-permute-start(bf16[32,256,128]{2,1,0:T(8,128)(2,1)S(1)} %get-tuple-element.32.refs_0_.refs_2_.refs_1_), channel_id=1, source_target_pairs={{0,16},{8,24},{32,48},{40,56},{64,80},{72,88},{96,112},{104,120},{... | collective-permute-start | bytes 6291464 | tf_op jit(solution)/shard_map/ppermute | solution.py:133
  11.2 0.4 collective-permute-start.1
  11.6 0.1 collective-permute-start.2
  11.7 3.1 %collective-permute-start.3 = (bf16[8,256,128]{2,1,0:T(8,128)(2,1)S(1)}, bf16[8,256,128]{2,1,0:T(8,128)(2,1)}, u32[]{:S(2)}, u32[]{:S(2)}) collective-permute-start(bf16[8,256,128]{2,1,0:T(8,128)(2,1)S(1)} %get-tuple-element.35), channel_id=1, source_target_pairs={{0,32},{8,40},{32,64},{40,72},{64,96},{72,104},{96,0},{104,8},{1,3... | collective-permute-start | bytes 1572872 | tf_op jit(solution)/shard_map/ppermute | solution.py:133
  14.9 12.3 %collective-permute-done.1.refs_3_.refs_2_ = bf16[8,256,128]{2,1,0:T(8,128)(2,1)S(1)} collective-permute-done((bf16[8,256,128]{2,1,0:T(8,128)(2,1)S(1)}, bf16[8,256,128]{2,1,0:T(8,128)(2,1)S(1)}, u32[]{:S(2)}, u32[]{:S(2)}) %collective-permute-start.1) | collective-permute-done | bytes 524320 | tf_op jit(solution)/shard_map/ppermute | solution.py:133
  27.2 10.5 %collective-permute-done.2.refs_4_.refs_3_ = bf16[8,256,128]{2,1,0:T(8,128)(2,1)S(1)} collective-permute-done((bf16[8,256,128]{2,1,0:T(8,128)(2,1)S(1)}, bf16[8,256,128]{2,1,0:T(8,128)(2,1)S(1)}, u32[]{:S(2)}, u32[]{:S(2)}) %collective-permute-start.2) | collective-permute-done | bytes 524320 | tf_op jit(solution)/shard_map/ppermute | solution.py:133
  37.7 3.2 %collective-permute-start.6 = (bf16[8,256,128]{2,1,0:T(8,128)(2,1)}, bf16[8,256,128]{2,1,0:T(8,128)(2,1)}, u32[]{:S(2)}, u32[]{:S(2)}) collective-permute-start(bf16[8,256,128]{2,1,0:T(8,128)(2,1)} %collective-permute-done.3.refs_5_.refs_4_), channel_id=1, source_target_pairs={{0,32},{8,40},{32,64},{40,72},{64,96},{72,104},{96,0},{104,8},{1,3... | collective-permute-start | bytes 1572872 | tf_op jit(solution)/shard_map/ppermute | solution.py:133
  41.0 0.1 and_select_fusion
  41.1 0.1 pad_add_fusion.s_ref
  41.1 11.1 %collective-permute-done.5.refs_7_.refs_6_ = bf16[8,256,128]{2,1,0:T(8,128)(2,1)} collective-permute-done((bf16[8,256,128]{2,1,0:T(8,128)(2,1)S(1)}, bf16[8,256,128]{2,1,0:T(8,128)(2,1)}, u32[]{:S(2)}, u32[]{:S(2)}) %collective-permute-start.5) | collective-permute-done | bytes 524320 | tf_op jit(solution)/shard_map/ppermute | solution.py:133
  52.3 6.0 %gram.3 = (f32[512,256]{1,0:T(8,128)S(1)}, bf16[512,256]{1,0:T(8,128)(2,1)}, bf16[512,256]{1,0:T(8,128)(2,1)}, bf16[512,256]{1,0:T(8,128)(2,1)}) custom-call(s32[7]{0:T(128)S(1)} %pad_add_fusion.s_ref, bf16[32,256,128]{2,1,0:T(8,128)(2,1)S(1)} %get-tuple-element.32.refs_0_.refs_2_.refs_1_, bf16[32,256,128]{2,1,0:T(8,128)(2,1)} %collective-permute-done.refs_1_, ...), custom_call_target="tpu_custom_call" | custom-call | flops 1 | bytes 1 | tf_op jit(solution)/shard_map/gram/pallas_call | solution.py:106
  58.3 0.8 copy-done.2
  59.1 2.8 %collective-permute-start.10 = (bf16[512,256]{1,0:T(8,128)(2,1)}, bf16[512,256]{1,0:T(8,128)(2,1)}, u32[]{:S(2)}, u32[]{:S(2)}) collective-permute-start(bf16[512,256]{1,0:T(8,128)(2,1)} %get-tuple-element.44), channel_id=1, source_target_pairs={{0,6},{8,14},{32,38},{40,46},{64,70},{72,78},{96,102},{104,110},{1... | collective-permute-start | bytes 786440 | tf_op jit(solution)/shard_map/ppermute | solution.py:133
  61.9 0.8 collective-permute-start.9
  62.7 0.9 collective-permute-start.8
  63.6 4.4 %gram.4 = (f32[256,256]{1,0:T(8,128)S(1)}, bf16[256,256]{1,0:T(8,128)(2,1)S(1)}, bf16[256,256]{1,0:T(8,128)(2,1)S(1)}, bf16[256,256]{1,0:T(8,128)(2,1)}) custom-call(s32[7]{0:T(128)S(1)} %pad_add_fusion.s_ref, bf16[32,256,128]{2,1,0:T(8,128)(2,1)} %collective-permute-done.7.refs_0_, bf16[32,256,128]{2,1,0:T(8,128)(2,1)S(1)} %get-tuple-element.32.refs_0_.refs_2_.refs_1_, ...), custom_call_target="tpu_custom_call" | custom-call | flops 1 | bytes 1 | tf_op jit(solution)/shard_map/gram/pallas_call | solution.py:106
  68.0 0.6 copy-done.4
  68.7 1.3 %copy-done = bf16[32,256,128]{2,1,0:T(8,128)(2,1)} copy-done((bf16[32,256,128]{2,1,0:T(8,128)(2,1)}, bf16[32,256,128]{2,1,0:T(8,128)(2,1)S(1)}, u32[]{:S(2)}) %copy-start) | copy-done | bytes 2097176
  70.0 2.4 %collective-permute-start.14 = (bf16[256,256]{1,0:T(8,128)(2,1)}, bf16[256,256]{1,0:T(8,128)(2,1)}, u32[]{:S(2)}, u32[]{:S(2)}) collective-permute-start(bf16[256,256]{1,0:T(8,128)(2,1)} %get-tuple-element.53), channel_id=1, source_target_pairs={{0,6},{8,14},{32,38},{40,46},{64,70},{72,78},{96,102},{104,110},{1... | collective-permute-start | bytes 393224 | tf_op jit(solution)/shard_map/ppermute | solution.py:133
  72.4 1.5 %collective-permute-start.13 = (bf16[256,256]{1,0:T(8,128)(2,1)}, bf16[256,256]{1,0:T(8,128)(2,1)S(1)}, u32[]{:S(2)}, u32[]{:S(2)}) collective-permute-start(bf16[256,256]{1,0:T(8,128)(2,1)} %copy-done.4), channel_id=1, source_target_pairs={{0,4},{8,12},{32,36},{40,44},{64,68},{72,76},{96,100},{104,108},{1... | collective-permute-start | bytes 393224 | tf_op jit(solution)/shard_map/ppermute | solution.py:133
  73.9 1.6 %copy-done.1 = bf16[32,256,128]{2,1,0:T(8,128)(2,1)S(1)} copy-done((bf16[32,256,128]{2,1,0:T(8,128)(2,1)S(1)}, bf16[32,256,128]{2,1,0:T(8,128)(2,1)}, u32[]{:S(2)}) %copy-start.1) | copy-done | bytes 2097176
  75.5 3.2 %gram.5 = (f32[256,256]{1,0:T(8,128)S(1)}, bf16[256,256]{1,0:T(8,128)(2,1)S(1)}, bf16[256,256]{1,0:T(8,128)(2,1)S(1)}, bf16[256,256]{1,0:T(8,128)(2,1)S(1)}) custom-call(s32[7]{0:T(128)S(1)} %pad_add_fusion.s_ref, bf16[32,256,128]{2,1,0:T(8,128)(2,1)S(1)} %copy-done.1, bf16[32,256,128]{2,1,0:T(8,128)(2,1)S(1)} %get-tuple-element.32.refs_0_.refs_2_.refs_1_, ...), custom_call_target="tpu_custom_call" | custom-call | flops 1 | bytes 1 | tf_op jit(solution)/shard_map/gram/pallas_call | solution.py:106
  78.7 0.1 collective-permute-start.12
  78.8 3.2 %collective-permute-start.20 = (bf16[256,256]{1,0:T(8,128)(2,1)S(1)}, bf16[256,256]{1,0:T(8,128)(2,1)S(1)}, u32[]{:S(2)}, u32[]{:S(2)}) collective-permute-start(bf16[256,256]{1,0:T(8,128)(2,1)S(1)} %get-tuple-element.58), channel_id=1, source_target_pairs={{0,6},{8,14},{32,38},{40,46},{64,70},{72,78},{96,102},{104,110},{1... | collective-permute-start | bytes 393224 | tf_op jit(solution)/shard_map/ppermute | solution.py:133
  82.0 0.8 collective-permute-start.19
  82.8 0.1 collective-permute-start.18
  83.0 1.2 %add_add_fusion = f32[512,256]{1,0:T(8,128)S(1)} fusion(bf16[512,256]{1,0:T(8,128)(2,1)} %collective-permute-done.10, bf16[512,256]{1,0:T(8,128)(2,1)} %collective-permute-done.9, f32[512,256]{1,0:T(8,128)S(1)} %copy-done.3, bf16[512,256]{1,0:T(8,128)(2,1)} %collective-permute-done.8), kind=kLoop, calls=%fused_computation.1 | loop fusion | flops 786432 | bytes 1835008 | tf_op jit(solution)/shard_map/add | solution.py:177
  84.2 2.3 %collective-permute-done.12 = bf16[256,256]{1,0:T(8,128)(2,1)S(1)} collective-permute-done((bf16[256,256]{1,0:T(8,128)(2,1)S(1)}, bf16[256,256]{1,0:T(8,128)(2,1)S(1)}, u32[]{:S(2)}, u32[]{:S(2)}) %collective-permute-start.12) | collective-permute-done | bytes 131104 | tf_op jit(solution)/shard_map/ppermute | solution.py:133
  86.5 0.1 collective-permute-done.20
  86.6 2.4 %collective-permute-done.19 = bf16[256,256]{1,0:T(8,128)(2,1)S(1)} collective-permute-done((bf16[256,256]{1,0:T(8,128)(2,1)S(1)}, bf16[256,256]{1,0:T(8,128)(2,1)S(1)}, u32[]{:S(2)}, u32[]{:S(2)}) %collective-permute-start.19) | collective-permute-done | bytes 131104 | tf_op jit(solution)/shard_map/ppermute | solution.py:133
  89.0 1.6 %collective-permute-done.18 = bf16[256,256]{1,0:T(8,128)(2,1)S(1)} collective-permute-done((bf16[256,256]{1,0:T(8,128)(2,1)S(1)}, bf16[256,256]{1,0:T(8,128)(2,1)S(1)}, u32[]{:S(2)}, u32[]{:S(2)}) %collective-permute-start.18) | collective-permute-done | bytes 131104 | tf_op jit(solution)/shard_map/ppermute | solution.py:133
  90.6 1.0 select_convert_fusion.1
  91.6 1.5 %collective-permute-start.15 = (bf16[256,256]{1,0:T(8,128)(2,1)S(1)}, bf16[256,256]{1,0:T(8,128)(2,1)S(1)}, u32[]{:S(2)}, u32[]{:S(2)}) collective-permute-start(bf16[256,256]{1,0:T(8,128)(2,1)S(1)} %get-tuple-element.64), channel_id=1, source_target_pairs={{0,1},{8,9},{32,33},{40,41},{64,65},{72,73},{96,97},{104,105},{1,0... | collective-permute-start | bytes 393224 | tf_op jit(solution)/shard_map/ppermute | solution.py:133
  93.1 0.6 collective-permute-start.21
  93.7 3.8 %collective-permute-done.15 = bf16[256,256]{1,0:T(8,128)(2,1)S(1)} collective-permute-done((bf16[256,256]{1,0:T(8,128)(2,1)S(1)}, bf16[256,256]{1,0:T(8,128)(2,1)S(1)}, u32[]{:S(2)}, u32[]{:S(2)}) %collective-permute-start.15) | collective-permute-done | bytes 131104 | tf_op jit(solution)/shard_map/ppermute | solution.py:133
  97.5 1.4 %collective-permute-done.21 = bf16[256,256]{1,0:T(8,128)(2,1)S(1)} collective-permute-done((bf16[256,256]{1,0:T(8,128)(2,1)S(1)}, bf16[256,256]{1,0:T(8,128)(2,1)S(1)}, u32[]{:S(2)}, u32[]{:S(2)}) %collective-permute-start.21) | collective-permute-done | bytes 131104 | tf_op jit(solution)/shard_map/ppermute | solution.py:133
  98.9 1.1 fusion.3
  100.0 2.9 %collective-permute-start.16 = (bf16[256,256]{1,0:T(8,128)(2,1)S(1)}, bf16[256,256]{1,0:T(8,128)(2,1)S(1)}, u32[]{:S(2)}, u32[]{:S(2)}) collective-permute-start(bf16[256,256]{1,0:T(8,128)(2,1)S(1)} %get-tuple-element.59), channel_id=1, source_target_pairs={{1,16},{9,24},{33,48},{41,56},{65,80},{73,88},{97,112},{105,120},{... | collective-permute-start | bytes 393224 | tf_op jit(solution)/shard_map/ppermute | solution.py:133
  103.0 3.4 %collective-permute-start.23 = (bf16[256,256]{1,0:T(8,128)(2,1)S(1)}, bf16[256,256]{1,0:T(8,128)(2,1)S(1)}, u32[]{:S(2)}, u32[]{:S(2)}) collective-permute-start(bf16[256,256]{1,0:T(8,128)(2,1)S(1)} %get-tuple-element.63), channel_id=1, source_target_pairs={{32,2},{40,10},{64,4},{72,12},{96,6},{104,14},{33,3},{41,11},{65,5... | collective-permute-start | bytes 393224 | tf_op jit(solution)/shard_map/ppermute | solution.py:133
  106.4 0.1 copy.4
  106.5 5.7 %collective-permute-start.17 = (bf16[256,256]{1,0:T(8,128)(2,1)S(1)}, bf16[256,256]{1,0:T(8,128)(2,1)S(1)}, u32[]{:S(2)}, u32[]{:S(2)}) collective-permute-start(bf16[256,256]{1,0:T(8,128)(2,1)S(1)} %get-tuple-element.59), channel_id=1, source_target_pairs={{32,2},{40,10},{64,4},{72,12},{96,6},{104,14},{33,3},{41,11},{65,5... | collective-permute-start | bytes 393224 | tf_op jit(solution)/shard_map/ppermute | solution.py:133
  112.3 0.1 collective-permute-start.22
  112.4 0.1 copy.3
  112.5 5.9 %collective-permute-done.23 = bf16[256,256]{1,0:T(8,128)(2,1)S(1)} collective-permute-done((bf16[256,256]{1,0:T(8,128)(2,1)S(1)}, bf16[256,256]{1,0:T(8,128)(2,1)S(1)}, u32[]{:S(2)}, u32[]{:S(2)}) %collective-permute-start.23) | collective-permute-done | bytes 131104 | tf_op jit(solution)/shard_map/ppermute | solution.py:133
  118.4 1.4 %collective-permute-done.17 = bf16[256,256]{1,0:T(8,128)(2,1)S(1)} collective-permute-done((bf16[256,256]{1,0:T(8,128)(2,1)S(1)}, bf16[256,256]{1,0:T(8,128)(2,1)S(1)}, u32[]{:S(2)}, u32[]{:S(2)}) %collective-permute-start.17) | collective-permute-done | bytes 131104 | tf_op jit(solution)/shard_map/ppermute | solution.py:133
  119.9 0.1 fusion.1
  120.0 1.0 copy.5
  (25 shorter events, 0.1 us)
Async XLA Ops:
  8.9 43.4 %collective-permute-start = (bf16[32,256,128]{2,1,0:T(8,128)(2,1)S(1)}, bf16[32,256,128]{2,1,0:T(8,128)(2,1)}, u32[]{:S(2)}, u32[]{:S(2)}) collective-permute-start(bf16[32,256,128]{2,1,0:T(8,128)(2,1)S(1)} %get-tuple-element.32.refs_0_.refs_2_.refs_1_), channel_id=1, source_target_pairs={{0,8},{8,0},{32,40},{40,32},{64,72},{72,64},{96,104},{104,96},{1,9... | collective-permute-start | bytes 6291464 | tf_op jit(solution)/shard_map/ppermute | solution.py:133
  8.9 50.2 %collective-permute-start.7 = (bf16[32,256,128]{2,1,0:T(8,128)(2,1)S(1)}, bf16[32,256,128]{2,1,0:T(8,128)(2,1)}, u32[]{:S(2)}, u32[]{:S(2)}) collective-permute-start(bf16[32,256,128]{2,1,0:T(8,128)(2,1)S(1)} %get-tuple-element.32.refs_0_.refs_2_.refs_1_), channel_id=1, source_target_pairs={{0,16},{8,24},{32,48},{40,56},{64,80},{72,88},{96,112},{104,120},{... | collective-permute-start | bytes 6291464 | tf_op jit(solution)/shard_map/ppermute | solution.py:133
  11.2 16.0 %collective-permute-start.1 = (bf16[8,256,128]{2,1,0:T(8,128)(2,1)S(1)}, bf16[8,256,128]{2,1,0:T(8,128)(2,1)S(1)}, u32[]{:S(2)}, u32[]{:S(2)}) collective-permute-start(bf16[8,256,128]{2,1,0:T(8,128)(2,1)S(1)} %get-tuple-element.33), channel_id=1, source_target_pairs={{0,96},{8,104},{32,0},{40,8},{64,32},{72,40},{96,64},{104,72},{1,9... | collective-permute-start | bytes 1572872 | tf_op jit(solution)/shard_map/ppermute | solution.py:133
  11.6 26.1 %collective-permute-start.2 = (bf16[8,256,128]{2,1,0:T(8,128)(2,1)S(1)}, bf16[8,256,128]{2,1,0:T(8,128)(2,1)S(1)}, u32[]{:S(2)}, u32[]{:S(2)}) collective-permute-start(bf16[8,256,128]{2,1,0:T(8,128)(2,1)S(1)} %get-tuple-element.34), channel_id=1, source_target_pairs={{0,96},{8,104},{32,0},{40,8},{64,32},{72,40},{96,64},{104,72},{1,9... | collective-permute-start | bytes 1572872 | tf_op jit(solution)/shard_map/ppermute | solution.py:133
  11.7 26.0 %collective-permute-start.3 = (bf16[8,256,128]{2,1,0:T(8,128)(2,1)S(1)}, bf16[8,256,128]{2,1,0:T(8,128)(2,1)}, u32[]{:S(2)}, u32[]{:S(2)}) collective-permute-start(bf16[8,256,128]{2,1,0:T(8,128)(2,1)S(1)} %get-tuple-element.35), channel_id=1, source_target_pairs={{0,32},{8,40},{32,64},{40,72},{64,96},{72,104},{96,0},{104,8},{1,3... | collective-permute-start | bytes 1572872 | tf_op jit(solution)/shard_map/ppermute | solution.py:133
  27.2 13.9 %collective-permute-start.4 = (bf16[8,256,128]{2,1,0:T(8,128)(2,1)}, bf16[8,256,128]{2,1,0:T(8,128)(2,1)}, u32[]{:S(2)}, u32[]{:S(2)}) collective-permute-start(bf16[8,256,128]{2,1,0:T(8,128)(2,1)} %get-tuple-element.36), channel_id=1, source_target_pairs={{0,32},{8,40},{32,64},{40,72},{64,96},{72,104},{96,0},{104,8},{1,3... | collective-permute-start | bytes 1572872 | tf_op jit(solution)/shard_map/ppermute | solution.py:133
  37.7 14.6 %collective-permute-start.5 = (bf16[8,256,128]{2,1,0:T(8,128)(2,1)S(1)}, bf16[8,256,128]{2,1,0:T(8,128)(2,1)}, u32[]{:S(2)}, u32[]{:S(2)}) collective-permute-start(bf16[8,256,128]{2,1,0:T(8,128)(2,1)S(1)} %collective-permute-done.1.refs_3_.refs_2_), channel_id=1, source_target_pairs={{0,96},{8,104},{32,0},{40,8},{64,32},{72,40},{96,64},{104,72},{1,9... | collective-permute-start | bytes 1572872 | tf_op jit(solution)/shard_map/ppermute | solution.py:133
  37.7 14.5 %collective-permute-start.6 = (bf16[8,256,128]{2,1,0:T(8,128)(2,1)}, bf16[8,256,128]{2,1,0:T(8,128)(2,1)}, u32[]{:S(2)}, u32[]{:S(2)}) collective-permute-start(bf16[8,256,128]{2,1,0:T(8,128)(2,1)} %collective-permute-done.3.refs_5_.refs_4_), channel_id=1, source_target_pairs={{0,32},{8,40},{32,64},{40,72},{64,96},{72,104},{96,0},{104,8},{1,3... | collective-permute-start | bytes 1572872 | tf_op jit(solution)/shard_map/ppermute | solution.py:133
  58.3 0.8 copy-start.2
  59.1 9.6 %collective-permute-start.11 = (bf16[32,256,128]{2,1,0:T(8,128)(2,1)}, bf16[32,256,128]{2,1,0:T(8,128)(2,1)S(1)}, u32[]{:S(2)}, u32[]{:S(2)}) collective-permute-start(bf16[32,256,128]{2,1,0:T(8,128)(2,1)} %collective-permute-done.7.refs_0_), channel_id=1, source_target_pairs={{0,8},{8,0},{32,40},{40,32},{64,72},{72,64},{96,104},{104,96},{1,9... | collective-permute-start | bytes 6291464 | tf_op jit(solution)/shard_map/ppermute | solution.py:133
  59.1 19.6 %collective-permute-start.10 = (bf16[512,256]{1,0:T(8,128)(2,1)}, bf16[512,256]{1,0:T(8,128)(2,1)}, u32[]{:S(2)}, u32[]{:S(2)}) collective-permute-start(bf16[512,256]{1,0:T(8,128)(2,1)} %get-tuple-element.44), channel_id=1, source_target_pairs={{0,6},{8,14},{32,38},{40,46},{64,70},{72,78},{96,102},{104,110},{1... | collective-permute-start | bytes 786440 | tf_op jit(solution)/shard_map/ppermute | solution.py:133
  61.9 16.9 %collective-permute-start.9 = (bf16[512,256]{1,0:T(8,128)(2,1)}, bf16[512,256]{1,0:T(8,128)(2,1)}, u32[]{:S(2)}, u32[]{:S(2)}) collective-permute-start(bf16[512,256]{1,0:T(8,128)(2,1)} %get-tuple-element.43), channel_id=1, source_target_pairs={{0,4},{8,12},{32,36},{40,44},{64,68},{72,76},{96,100},{104,108},{1... | collective-permute-start | bytes 786440 | tf_op jit(solution)/shard_map/ppermute | solution.py:133
  62.7 19.3 %collective-permute-start.8 = (bf16[512,256]{1,0:T(8,128)(2,1)}, bf16[512,256]{1,0:T(8,128)(2,1)}, u32[]{:S(2)}, u32[]{:S(2)}) collective-permute-start(bf16[512,256]{1,0:T(8,128)(2,1)} %get-tuple-element.42), channel_id=1, source_target_pairs={{0,2},{8,10},{32,34},{40,42},{64,66},{72,74},{96,98},{104,106},{1,... | collective-permute-start | bytes 786440 | tf_op jit(solution)/shard_map/ppermute | solution.py:133
  68.0 0.7 copy-start.4
  68.7 1.3 %copy-start = (bf16[32,256,128]{2,1,0:T(8,128)(2,1)}, bf16[32,256,128]{2,1,0:T(8,128)(2,1)S(1)}, u32[]{:S(2)}) copy-start(bf16[32,256,128]{2,1,0:T(8,128)(2,1)S(1)} %collective-permute-done.11.refs_0_) | copy-start | bytes 6291460
  70.0 12.8 %collective-permute-start.14 = (bf16[256,256]{1,0:T(8,128)(2,1)}, bf16[256,256]{1,0:T(8,128)(2,1)}, u32[]{:S(2)}, u32[]{:S(2)}) collective-permute-start(bf16[256,256]{1,0:T(8,128)(2,1)} %get-tuple-element.53), channel_id=1, source_target_pairs={{0,6},{8,14},{32,38},{40,46},{64,70},{72,78},{96,102},{104,110},{1... | collective-permute-start | bytes 393224 | tf_op jit(solution)/shard_map/ppermute | solution.py:133
  72.4 11.8 %collective-permute-start.13 = (bf16[256,256]{1,0:T(8,128)(2,1)}, bf16[256,256]{1,0:T(8,128)(2,1)S(1)}, u32[]{:S(2)}, u32[]{:S(2)}) collective-permute-start(bf16[256,256]{1,0:T(8,128)(2,1)} %copy-done.4), channel_id=1, source_target_pairs={{0,4},{8,12},{32,36},{40,44},{64,68},{72,76},{96,100},{104,108},{1... | collective-permute-start | bytes 393224 | tf_op jit(solution)/shard_map/ppermute | solution.py:133
  73.9 1.6 %copy-start.1 = (bf16[32,256,128]{2,1,0:T(8,128)(2,1)S(1)}, bf16[32,256,128]{2,1,0:T(8,128)(2,1)}, u32[]{:S(2)}) copy-start(bf16[32,256,128]{2,1,0:T(8,128)(2,1)} %copy-done) | copy-start | bytes 6291460
  75.5 7.5 %copy-start.3 = (f32[512,256]{1,0:T(8,128)S(1)}, f32[512,256]{1,0:T(8,128)}, u32[]{:S(2)}) copy-start(f32[512,256]{1,0:T(8,128)} %copy-done.2) | copy-start | bytes 1572868
  78.7 7.8 %collective-permute-start.12 = (bf16[256,256]{1,0:T(8,128)(2,1)S(1)}, bf16[256,256]{1,0:T(8,128)(2,1)S(1)}, u32[]{:S(2)}, u32[]{:S(2)}) collective-permute-start(bf16[256,256]{1,0:T(8,128)(2,1)S(1)} %get-tuple-element.51), channel_id=1, source_target_pairs={{0,2},{8,10},{32,34},{40,42},{64,66},{72,74},{96,98},{104,106},{1,... | collective-permute-start | bytes 393224 | tf_op jit(solution)/shard_map/ppermute | solution.py:133
  78.8 7.8 %collective-permute-start.20 = (bf16[256,256]{1,0:T(8,128)(2,1)S(1)}, bf16[256,256]{1,0:T(8,128)(2,1)S(1)}, u32[]{:S(2)}, u32[]{:S(2)}) collective-permute-start(bf16[256,256]{1,0:T(8,128)(2,1)S(1)} %get-tuple-element.58), channel_id=1, source_target_pairs={{0,6},{8,14},{32,38},{40,46},{64,70},{72,78},{96,102},{104,110},{1... | collective-permute-start | bytes 393224 | tf_op jit(solution)/shard_map/ppermute | solution.py:133
  82.0 7.0 %collective-permute-start.19 = (bf16[256,256]{1,0:T(8,128)(2,1)S(1)}, bf16[256,256]{1,0:T(8,128)(2,1)S(1)}, u32[]{:S(2)}, u32[]{:S(2)}) collective-permute-start(bf16[256,256]{1,0:T(8,128)(2,1)S(1)} %get-tuple-element.57), channel_id=1, source_target_pairs={{0,4},{8,12},{32,36},{40,44},{64,68},{72,76},{96,100},{104,108},{1... | collective-permute-start | bytes 393224 | tf_op jit(solution)/shard_map/ppermute | solution.py:133
  82.8 7.7 %collective-permute-start.18 = (bf16[256,256]{1,0:T(8,128)(2,1)S(1)}, bf16[256,256]{1,0:T(8,128)(2,1)S(1)}, u32[]{:S(2)}, u32[]{:S(2)}) collective-permute-start(bf16[256,256]{1,0:T(8,128)(2,1)S(1)} %get-tuple-element.56), channel_id=1, source_target_pairs={{0,2},{8,10},{32,34},{40,42},{64,66},{72,74},{96,98},{104,106},{1,... | collective-permute-start | bytes 393224 | tf_op jit(solution)/shard_map/ppermute | solution.py:133
  91.6 5.9 %collective-permute-start.15 = (bf16[256,256]{1,0:T(8,128)(2,1)S(1)}, bf16[256,256]{1,0:T(8,128)(2,1)S(1)}, u32[]{:S(2)}, u32[]{:S(2)}) collective-permute-start(bf16[256,256]{1,0:T(8,128)(2,1)S(1)} %get-tuple-element.64), channel_id=1, source_target_pairs={{0,1},{8,9},{32,33},{40,41},{64,65},{72,73},{96,97},{104,105},{1,0... | collective-permute-start | bytes 393224 | tf_op jit(solution)/shard_map/ppermute | solution.py:133
  93.1 5.8 %collective-permute-start.21 = (bf16[256,256]{1,0:T(8,128)(2,1)S(1)}, bf16[256,256]{1,0:T(8,128)(2,1)S(1)}, u32[]{:S(2)}, u32[]{:S(2)}) collective-permute-start(bf16[256,256]{1,0:T(8,128)(2,1)S(1)} %get-tuple-element.65), channel_id=1, source_target_pairs={{0,1},{8,9},{32,33},{40,41},{64,65},{72,73},{96,97},{104,105},{1,0... | collective-permute-start | bytes 393224 | tf_op jit(solution)/shard_map/ppermute | solution.py:133
  100.0 12.3 %collective-permute-start.16 = (bf16[256,256]{1,0:T(8,128)(2,1)S(1)}, bf16[256,256]{1,0:T(8,128)(2,1)S(1)}, u32[]{:S(2)}, u32[]{:S(2)}) collective-permute-start(bf16[256,256]{1,0:T(8,128)(2,1)S(1)} %get-tuple-element.59), channel_id=1, source_target_pairs={{1,16},{9,24},{33,48},{41,56},{65,80},{73,88},{97,112},{105,120},{... | collective-permute-start | bytes 393224 | tf_op jit(solution)/shard_map/ppermute | solution.py:133
  103.0 15.5 %collective-permute-start.23 = (bf16[256,256]{1,0:T(8,128)(2,1)S(1)}, bf16[256,256]{1,0:T(8,128)(2,1)S(1)}, u32[]{:S(2)}, u32[]{:S(2)}) collective-permute-start(bf16[256,256]{1,0:T(8,128)(2,1)S(1)} %get-tuple-element.63), channel_id=1, source_target_pairs={{32,2},{40,10},{64,4},{72,12},{96,6},{104,14},{33,3},{41,11},{65,5... | collective-permute-start | bytes 393224 | tf_op jit(solution)/shard_map/ppermute | solution.py:133
  106.5 13.3 %collective-permute-start.17 = (bf16[256,256]{1,0:T(8,128)(2,1)S(1)}, bf16[256,256]{1,0:T(8,128)(2,1)S(1)}, u32[]{:S(2)}, u32[]{:S(2)}) collective-permute-start(bf16[256,256]{1,0:T(8,128)(2,1)S(1)} %get-tuple-element.59), channel_id=1, source_target_pairs={{32,2},{40,10},{64,4},{72,12},{96,6},{104,14},{33,3},{41,11},{65,5... | collective-permute-start | bytes 393224 | tf_op jit(solution)/shard_map/ppermute | solution.py:133
  112.3 6.2 %collective-permute-start.22 = (bf16[256,256]{0,1:T(8,128)(2,1)S(1)}, bf16[256,256]{0,1:T(8,128)(2,1)S(1)}, u32[]{:S(2)}, u32[]{:S(2)}) collective-permute-start(bf16[256,256]{0,1:T(8,128)(2,1)S(1)} %copy.4), channel_id=1, source_target_pairs={{0,8},{8,0},{32,40},{40,32},{64,72},{72,64},{96,104},{104,96},{1,2... | collective-permute-start | bytes 393224 | tf_op jit(solution)/shard_map/ppermute | solution.py:133

commit v4 on v3

--- a/solution.py
+++ b/solution.py
@@ -164,8 +164,9 @@
 
     own, *pieces = features(1 - half(z), grads_proj, inputs_proj)
     up_a, down_a = shift(pieces[0], z_down), shift(pieces[2], z_up)
-    up_b, down_b = shift(pieces[1], z_down), shift(pieces[3], z_up)
     mate, far = shift(own, other_core), shift(own, other_half)
+    mate, *later = after((mate, pieces[1], pieces[3]))
+    up_b, down_b = shift(later[0], z_down), shift(later[1], z_up)
     columns = [own, up_a, up_b, down_a, down_b, shift(up_a, z_down), shift(down_a, z_up)]
 
     def over_x(parts):
@@ -199,7 +200,8 @@
     turn_one = across(sent_one)
     here = shift(sent_one, lambda x, y, z, c: (x, 3 - y, z, c) if y in (1, 2) else None).astype(f32)
     here = jnp.where(edge, one, here)
-    two = over_y(near_sum[256:], over_x(far_two))
+    one_done, far_two = after((one, over_x(far_two)))
+    two = over_y(near_sum[256:], far_two)
     sent_two = two.astype(bf16)
     turn_two = across(sent_two)
     there = shift(sent_two, lambda x, y, z, c: (x, 3 - y if y in (1, 2) else y, z, 1 - c)).astype(f32)

time: 121 us -> 119 us (0.983); the launches traced: 121 us -> 118 us
  waiting for transfers between devices: 52.9 us -> 49.8 us
  starting transfers between devices: 36 us -> 37.8 us
    ppermute x24, waiting for transfers between devices: 52.9 us -> 49.8 us  [shift(): return lax.ppermute(array, AXES, pairs)]
    ppermute x24, starting transfers between devices: 36 us -> 37.8 us  [shift(): return lax.ppermute(array, AXES, pairs)]
  transfers between devices with their start and end apart: 24 -> 24, of which waited for: 11 -> 10; matrix products, arithmetic and copies ran while one was open for 1% -> 2% of each run, Pallas kernels for 11% -> 11%
where the time goes in v4:
time: 119 us; the launch traced here: 118 us
  waiting for transfers between devices  49.8 us (42%)
  starting transfers between devices  37.8 us (32%)
  Pallas kernels  22.2 us (19%)
  local copies, waits for them, and re-layouts  4.95 us (4%)
  other arithmetic  2.76 us (2%)
    ppermute x24, waiting for transfers between devices, shift(): return lax.ppermute(array, AXES, pairs)  49.8 us
    ppermute x24, starting transfers between devices, shift(): return lax.ppermute(array, AXES, pairs)  37.8 us
    pallas_call x3, Pallas kernels, gram(): pl.pallas_call(functools.partial(gram_kernel, len(rows)), in_specs=[IN_SM...  13.2 us
    pallas_call x1, Pallas kernels, features(): pl.pallas_call(feature_kernel, grid_spec=pltpu.PrefetchScalarGridSpec(num...  9.04 us
    unnamed x10, local copies, waits for them, and re-layouts  3.73 us
  transfers between devices with their start and end apart: 24, of which 10 were waited for; matrix products, arithmetic and copies ran while one was open for 2% of the time, Pallas kernels for 11%

profile of v4, /device:TPU:104, one launch (start us, length us, event | category | flops | bytes accessed | tf_op | source)
XLA Modules:
  0.0 117.7 jit_solution(10811111253997979080)
XLA Ops:
  0.0 9.0 %features.1 = (bf16[32,256,128]{2,1,0:T(8,128)(2,1)S(1)}, bf16[8,256,128]{2,1,0:T(8,128)(2,1)S(1)}, bf16[8,256,128]{2,1,0:T(8,128)(2,1)}, bf16[8,256,128]{2,1,0:T(8,128)(2,1)S(1)}, bf16[8,256,128]{2,1,0:T(8,128)(2,1)}) custom-call(s32[1]{0:T(128)} %bitcast.7.s_ref, bf16[1,256,64,256]{3,2,1,0:T(8,128)(2,1)} %g_ref.1, bf16[1,256,64,256]{3,2,1,0:T(8,128)(2,1)} %i_ref.1), custom_call_target="tpu_custom_call" | custom-call | flops 1 | bytes 1 | tf_op jit(solution)/shard_map/features/pallas_call | solution.py:56
  9.0 2.3 %collective-permute-start.7 = (bf16[32,256,128]{2,1,0:T(8,128)(2,1)S(1)}, bf16[32,256,128]{2,1,0:T(8,128)(2,1)}, u32[]{:S(2)}, u32[]{:S(2)}) collective-permute-start(bf16[32,256,128]{2,1,0:T(8,128)(2,1)S(1)} %get-tuple-element.36.refs_0_.refs_2_.refs_1_), channel_id=1, source_target_pairs={{0,16},{8,24},{32,48},{40,56},{64,80},{72,88},{96,112},{104,120},{... | collective-permute-start | bytes 6291464 | tf_op jit(solution)/shard_map/ppermute | solution.py:133
  11.4 0.4 collective-permute-start.1
  11.8 2.8 %collective-permute-start.3 = (bf16[8,256,128]{2,1,0:T(8,128)(2,1)S(1)}, bf16[8,256,128]{2,1,0:T(8,128)(2,1)S(1)}, u32[]{:S(2)}, u32[]{:S(2)}) collective-permute-start(bf16[8,256,128]{2,1,0:T(8,128)(2,1)S(1)} %get-tuple-element.42), channel_id=1, source_target_pairs={{0,32},{8,40},{32,64},{40,72},{64,96},{72,104},{96,0},{104,8},{1,3... | collective-permute-start | bytes 1572872 | tf_op jit(solution)/shard_map/ppermute | solution.py:133
  14.6 12.0 %collective-permute-done.1.refs_3_.refs_2_ = bf16[8,256,128]{2,1,0:T(8,128)(2,1)S(1)} collective-permute-done((bf16[8,256,128]{2,1,0:T(8,128)(2,1)S(1)}, bf16[8,256,128]{2,1,0:T(8,128)(2,1)S(1)}, u32[]{:S(2)}, u32[]{:S(2)}) %collective-permute-start.1) | collective-permute-done | bytes 524320 | tf_op jit(solution)/shard_map/ppermute | solution.py:133
  26.6 3.2 %collective-permute-start.6 = (bf16[8,256,128]{2,1,0:T(8,128)(2,1)S(1)}, bf16[8,256,128]{2,1,0:T(8,128)(2,1)}, u32[]{:S(2)}, u32[]{:S(2)}) collective-permute-start(bf16[8,256,128]{2,1,0:T(8,128)(2,1)S(1)} %collective-permute-done.3.refs_5_.refs_4_), channel_id=1, source_target_pairs={{0,32},{8,40},{32,64},{40,72},{64,96},{72,104},{96,0},{104,8},{1,3... | collective-permute-start | bytes 1572872 | tf_op jit(solution)/shard_map/ppermute | solution.py:133
  29.9 1.3 %copy-done = bf16[32,256,128]{2,1,0:T(8,128)(2,1)} copy-done((bf16[32,256,128]{2,1,0:T(8,128)(2,1)}, bf16[32,256,128]{2,1,0:T(8,128)(2,1)S(1)}, u32[]{:S(2)}) %copy-start) | copy-done | bytes 2097176
  31.2 3.2 %collective-permute-start.4 = (bf16[8,256,128]{2,1,0:T(8,128)(2,1)}, bf16[8,256,128]{2,1,0:T(8,128)(2,1)}, u32[]{:S(2)}, u32[]{:S(2)}) collective-permute-start(bf16[8,256,128]{2,1,0:T(8,128)(2,1)} %get-tuple-element.43), channel_id=1, source_target_pairs={{0,32},{8,40},{32,64},{40,72},{64,96},{72,104},{96,0},{104,8},{1,3... | collective-permute-start | bytes 1572872 | tf_op jit(solution)/shard_map/ppermute | solution.py:133
  34.4 0.1 and_select_fusion
  34.5 0.1 pad_add_fusion.s_ref
  34.6 8.2 %collective-permute-done.5.refs_7_.refs_6_ = bf16[8,256,128]{2,1,0:T(8,128)(2,1)} collective-permute-done((bf16[8,256,128]{2,1,0:T(8,128)(2,1)S(1)}, bf16[8,256,128]{2,1,0:T(8,128)(2,1)}, u32[]{:S(2)}, u32[]{:S(2)}) %collective-permute-start.5) | collective-permute-done | bytes 524320 | tf_op jit(solution)/shard_map/ppermute | solution.py:133
  42.8 9.6 %collective-permute-done.2.refs_4_.refs_3_ = bf16[8,256,128]{2,1,0:T(8,128)(2,1)} collective-permute-done((bf16[8,256,128]{2,1,0:T(8,128)(2,1)}, bf16[8,256,128]{2,1,0:T(8,128)(2,1)}, u32[]{:S(2)}, u32[]{:S(2)}) %collective-permute-start.2) | collective-permute-done | bytes 524320 | tf_op jit(solution)/shard_map/ppermute | solution.py:133
  52.4 1.6 %copy-done.1 = bf16[32,256,128]{2,1,0:T(8,128)(2,1)S(1)} copy-done((bf16[32,256,128]{2,1,0:T(8,128)(2,1)S(1)}, bf16[32,256,128]{2,1,0:T(8,128)(2,1)}, u32[]{:S(2)}) %copy-start.1) | copy-done | bytes 2097176
  53.9 5.4 %gram.3 = (f32[512,256]{1,0:T(8,128)S(1)}, bf16[512,256]{1,0:T(8,128)(2,1)S(1)}, bf16[512,256]{1,0:T(8,128)(2,1)}, bf16[512,256]{1,0:T(8,128)(2,1)}) custom-call(s32[7]{0:T(128)S(1)} %pad_add_fusion.s_ref, bf16[32,256,128]{2,1,0:T(8,128)(2,1)S(1)} %get-tuple-element.36.refs_0_.refs_2_.refs_1_, bf16[32,256,128]{2,1,0:T(8,128)(2,1)S(1)} %copy-done.1, ...), custom_call_target="tpu_custom_call" | custom-call | flops 1 | bytes 1 | tf_op jit(solution)/shard_map/gram/pallas_call | solution.py:106
  59.3 0.8 copy-done.2
  60.1 2.8 %collective-permute-start.10 = (bf16[512,256]{1,0:T(8,128)(2,1)}, bf16[512,256]{1,0:T(8,128)(2,1)}, u32[]{:S(2)}, u32[]{:S(2)}) collective-permute-start(bf16[512,256]{1,0:T(8,128)(2,1)} %get-tuple-element.51), channel_id=1, source_target_pairs={{0,6},{8,14},{32,38},{40,46},{64,70},{72,78},{96,102},{104,110},{1... | collective-permute-start | bytes 786440 | tf_op jit(solution)/shard_map/ppermute | solution.py:133
  62.9 0.8 collective-permute-start.9
  63.7 0.9 collective-permute-start.8
  64.6 3.8 %gram.4 = (f32[256,256]{1,0:T(8,128)S(1)}, bf16[256,256]{1,0:T(8,128)(2,1)S(1)}, bf16[256,256]{1,0:T(8,128)(2,1)S(1)}, bf16[256,256]{1,0:T(8,128)(2,1)S(1)}) custom-call(s32[7]{0:T(128)S(1)} %pad_add_fusion.s_ref, bf16[32,256,128]{2,1,0:T(8,128)(2,1)} %collective-permute-done.7.refs_0_, bf16[32,256,128]{2,1,0:T(8,128)(2,1)S(1)} %get-tuple-element.36.refs_0_.refs_2_.refs_1_, ...), custom_call_target="tpu_custom_call" | custom-call | flops 1 | bytes 1 | tf_op jit(solution)/shard_map/gram/pallas_call | solution.py:106
  68.4 2.4 %collective-permute-start.14 = (bf16[256,256]{1,0:T(8,128)(2,1)S(1)}, bf16[256,256]{1,0:T(8,128)(2,1)S(1)}, u32[]{:S(2)}, u32[]{:S(2)}) collective-permute-start(bf16[256,256]{1,0:T(8,128)(2,1)S(1)} %get-tuple-element.60), channel_id=1, source_target_pairs={{0,6},{8,14},{32,38},{40,46},{64,70},{72,78},{96,102},{104,110},{1... | collective-permute-start | bytes 393224 | tf_op jit(solution)/shard_map/ppermute | solution.py:133
  70.8 1.5 %collective-permute-start.13 = (bf16[256,256]{1,0:T(8,128)(2,1)S(1)}, bf16[256,256]{1,0:T(8,128)(2,1)S(1)}, u32[]{:S(2)}, u32[]{:S(2)}) collective-permute-start(bf16[256,256]{1,0:T(8,128)(2,1)S(1)} %get-tuple-element.59), channel_id=1, source_target_pairs={{0,4},{8,12},{32,36},{40,44},{64,68},{72,76},{96,100},{104,108},{1... | collective-permute-start | bytes 393224 | tf_op jit(solution)/shard_map/ppermute | solution.py:133
  72.4 2.9 %collective-permute-done.10 = bf16[512,256]{1,0:T(8,128)(2,1)} collective-permute-done((bf16[512,256]{1,0:T(8,128)(2,1)}, bf16[512,256]{1,0:T(8,128)(2,1)}, u32[]{:S(2)}, u32[]{:S(2)}) %collective-permute-start.10) | collective-permute-done | bytes 262176 | tf_op jit(solution)/shard_map/ppermute | solution.py:133
  75.3 4.1 %collective-permute-done.8 = bf16[512,256]{1,0:T(8,128)(2,1)} collective-permute-done((bf16[512,256]{1,0:T(8,128)(2,1)S(1)}, bf16[512,256]{1,0:T(8,128)(2,1)}, u32[]{:S(2)}, u32[]{:S(2)}) %collective-permute-start.8) | collective-permute-done | bytes 262176 | tf_op jit(solution)/shard_map/ppermute | solution.py:133
  79.4 1.2 %add_add_fusion = f32[512,256]{1,0:T(8,128)S(1)} fusion(bf16[512,256]{1,0:T(8,128)(2,1)} %collective-permute-done.10, bf16[512,256]{1,0:T(8,128)(2,1)} %collective-permute-done.9, f32[512,256]{1,0:T(8,128)S(1)} %copy-done.3, bf16[512,256]{1,0:T(8,128)(2,1)} %collective-permute-done.8), kind=kLoop, calls=%fused_computation.1 | loop fusion | flops 786432 | bytes 1835008 | tf_op jit(solution)/shard_map/add | solution.py:178
  80.6 0.0 copy-start.4
  80.7 4.0 %gram.5 = (f32[256,256]{1,0:T(8,128)S(1)}, bf16[256,256]{1,0:T(8,128)(2,1)S(1)}, bf16[256,256]{1,0:T(8,128)(2,1)S(1)}, bf16[256,256]{1,0:T(8,128)(2,1)S(1)}) custom-call(s32[7]{0:T(128)S(1)} %pad_add_fusion.s_ref, bf16[32,256,128]{2,1,0:T(8,128)(2,1)} %collective-permute-done.11.refs_0_, bf16[32,256,128]{2,1,0:T(8,128)(2,1)S(1)} %get-tuple-element.36.refs_0_.refs_2_.refs_1_, ...), custom_call_target="tpu_custom_call" | custom-call | flops 1 | bytes 1 | tf_op jit(solution)/shard_map/gram/pallas_call | solution.py:106
  84.6 0.7 collective-permute-start.20
  85.3 0.8 collective-permute-start.19
  86.1 1.2 collective-permute-start.18
  87.3 0.1 select_convert_fusion.1
  87.4 1.5 %collective-permute-start.15 = (bf16[256,256]{1,0:T(8,128)(2,1)S(1)}, bf16[256,256]{1,0:T(8,128)(2,1)S(1)}, u32[]{:S(2)}, u32[]{:S(2)}) collective-permute-start(bf16[256,256]{1,0:T(8,128)(2,1)S(1)} %select_convert_fusion.1), channel_id=1, source_target_pairs={{0,1},{8,9},{32,33},{40,41},{64,65},{72,73},{96,97},{104,105},{1,0... | collective-permute-start | bytes 393224 | tf_op jit(solution)/shard_map/ppermute | solution.py:133
  88.9 2.2 %collective-permute-done.20 = bf16[256,256]{1,0:T(8,128)(2,1)S(1)} collective-permute-done((bf16[256,256]{1,0:T(8,128)(2,1)S(1)}, bf16[256,256]{1,0:T(8,128)(2,1)S(1)}, u32[]{:S(2)}, u32[]{:S(2)}) %collective-permute-start.20) | collective-permute-done | bytes 131104 | tf_op jit(solution)/shard_map/ppermute | solution.py:133
  91.1 1.9 %collective-permute-done.19 = bf16[256,256]{1,0:T(8,128)(2,1)S(1)} collective-permute-done((bf16[256,256]{1,0:T(8,128)(2,1)S(1)}, bf16[256,256]{1,0:T(8,128)(2,1)S(1)}, u32[]{:S(2)}, u32[]{:S(2)}) %collective-permute-start.19) | collective-permute-done | bytes 131104 | tf_op jit(solution)/shard_map/ppermute | solution.py:133
  92.9 1.5 %collective-permute-done.18 = bf16[256,256]{1,0:T(8,128)(2,1)S(1)} collective-permute-done((bf16[256,256]{1,0:T(8,128)(2,1)S(1)}, bf16[256,256]{1,0:T(8,128)(2,1)S(1)}, u32[]{:S(2)}, u32[]{:S(2)}) %collective-permute-start.18) | collective-permute-done | bytes 131104 | tf_op jit(solution)/shard_map/ppermute | solution.py:133
  94.4 0.1 add_add_fusion.1
  94.5 0.1 fusion.3
  94.6 1.5 %collective-permute-start.21 = (bf16[256,256]{1,0:T(8,128)(2,1)S(1)}, bf16[256,256]{1,0:T(8,128)(2,1)S(1)}, u32[]{:S(2)}, u32[]{:S(2)}) collective-permute-start(bf16[256,256]{1,0:T(8,128)(2,1)S(1)} %select_convert_fusion), channel_id=1, source_target_pairs={{0,1},{8,9},{32,33},{40,41},{64,65},{72,73},{96,97},{104,105},{1,0... | collective-permute-start | bytes 393224 | tf_op jit(solution)/shard_map/ppermute | solution.py:133
  96.2 2.3 %collective-permute-start.16 = (bf16[256,256]{1,0:T(8,128)(2,1)S(1)}, bf16[256,256]{1,0:T(8,128)(2,1)S(1)}, u32[]{:S(2)}, u32[]{:S(2)}) collective-permute-start(bf16[256,256]{1,0:T(8,128)(2,1)S(1)} %get-tuple-element.67), channel_id=1, source_target_pairs={{1,16},{9,24},{33,48},{41,56},{65,80},{73,88},{97,112},{105,120},{... | collective-permute-start | bytes 393224 | tf_op jit(solution)/shard_map/ppermute | solution.py:133
  98.5 5.4 %collective-permute-start.17 = (bf16[256,256]{1,0:T(8,128)(2,1)S(1)}, bf16[256,256]{1,0:T(8,128)(2,1)S(1)}, u32[]{:S(2)}, u32[]{:S(2)}) collective-permute-start(bf16[256,256]{1,0:T(8,128)(2,1)S(1)} %get-tuple-element.67), channel_id=1, source_target_pairs={{32,2},{40,10},{64,4},{72,12},{96,6},{104,14},{33,3},{41,11},{65,5... | collective-permute-start | bytes 393224 | tf_op jit(solution)/shard_map/ppermute | solution.py:133
  103.9 1.0 add_convert_fusion
  104.9 3.8 %collective-permute-start.23 = (bf16[256,256]{1,0:T(8,128)(2,1)S(1)}, bf16[256,256]{1,0:T(8,128)(2,1)S(1)}, u32[]{:S(2)}, u32[]{:S(2)}) collective-permute-start(bf16[256,256]{1,0:T(8,128)(2,1)S(1)} %add_convert_fusion), channel_id=1, source_target_pairs={{32,2},{40,10},{64,4},{72,12},{96,6},{104,14},{33,3},{41,11},{65,5... | collective-permute-start | bytes 393224 | tf_op jit(solution)/shard_map/ppermute | solution.py:133
  108.7 0.1 copy.4
  108.8 0.1 collective-permute-start.22
  109.0 0.1 copy.3
  109.1 1.7 %collective-permute-done.17 = bf16[256,256]{1,0:T(8,128)(2,1)S(1)} collective-permute-done((bf16[256,256]{1,0:T(8,128)(2,1)S(1)}, bf16[256,256]{1,0:T(8,128)(2,1)S(1)}, u32[]{:S(2)}, u32[]{:S(2)}) %collective-permute-start.17) | collective-permute-done | bytes 131104 | tf_op jit(solution)/shard_map/ppermute | solution.py:133
  110.8 5.7 %collective-permute-done.23 = bf16[256,256]{1,0:T(8,128)(2,1)S(1)} collective-permute-done((bf16[256,256]{1,0:T(8,128)(2,1)S(1)}, bf16[256,256]{1,0:T(8,128)(2,1)S(1)}, u32[]{:S(2)}, u32[]{:S(2)}) %collective-permute-start.23) | collective-permute-done | bytes 131104 | tf_op jit(solution)/shard_map/ppermute | solution.py:133
  116.6 0.1 fusion.1
  116.7 1.0 copy.5
  (28 shorter events, 0.2 us)
Async XLA Ops:
  9.0 20.8 %collective-permute-start = (bf16[32,256,128]{2,1,0:T(8,128)(2,1)S(1)}, bf16[32,256,128]{2,1,0:T(8,128)(2,1)S(1)}, u32[]{:S(2)}, u32[]{:S(2)}) collective-permute-start(bf16[32,256,128]{2,1,0:T(8,128)(2,1)S(1)} %get-tuple-element.36.refs_0_.refs_2_.refs_1_), channel_id=1, source_target_pairs={{0,8},{8,0},{32,40},{40,32},{64,72},{72,64},{96,104},{104,96},{1,9... | collective-permute-start | bytes 6291464 | tf_op jit(solution)/shard_map/ppermute | solution.py:133
  9.0 51.1 %collective-permute-start.7 = (bf16[32,256,128]{2,1,0:T(8,128)(2,1)S(1)}, bf16[32,256,128]{2,1,0:T(8,128)(2,1)}, u32[]{:S(2)}, u32[]{:S(2)}) collective-permute-start(bf16[32,256,128]{2,1,0:T(8,128)(2,1)S(1)} %get-tuple-element.36.refs_0_.refs_2_.refs_1_), channel_id=1, source_target_pairs={{0,16},{8,24},{32,48},{40,56},{64,80},{72,88},{96,112},{104,120},{... | collective-permute-start | bytes 6291464 | tf_op jit(solution)/shard_map/ppermute | solution.py:133
  11.4 15.2 %collective-permute-start.1 = (bf16[8,256,128]{2,1,0:T(8,128)(2,1)S(1)}, bf16[8,256,128]{2,1,0:T(8,128)(2,1)S(1)}, u32[]{:S(2)}, u32[]{:S(2)}) collective-permute-start(bf16[8,256,128]{2,1,0:T(8,128)(2,1)S(1)} %get-tuple-element.40), channel_id=1, source_target_pairs={{0,96},{8,104},{32,0},{40,8},{64,32},{72,40},{96,64},{104,72},{1,9... | collective-permute-start | bytes 1572872 | tf_op jit(solution)/shard_map/ppermute | solution.py:133
  11.8 14.8 %collective-permute-start.3 = (bf16[8,256,128]{2,1,0:T(8,128)(2,1)S(1)}, bf16[8,256,128]{2,1,0:T(8,128)(2,1)S(1)}, u32[]{:S(2)}, u32[]{:S(2)}) collective-permute-start(bf16[8,256,128]{2,1,0:T(8,128)(2,1)S(1)} %get-tuple-element.42), channel_id=1, source_target_pairs={{0,32},{8,40},{32,64},{40,72},{64,96},{72,104},{96,0},{104,8},{1,3... | collective-permute-start | bytes 1572872 | tf_op jit(solution)/shard_map/ppermute | solution.py:133
  26.6 16.2 %collective-permute-start.5 = (bf16[8,256,128]{2,1,0:T(8,128)(2,1)S(1)}, bf16[8,256,128]{2,1,0:T(8,128)(2,1)}, u32[]{:S(2)}, u32[]{:S(2)}) collective-permute-start(bf16[8,256,128]{2,1,0:T(8,128)(2,1)S(1)} %collective-permute-done.1.refs_3_.refs_2_), channel_id=1, source_target_pairs={{0,96},{8,104},{32,0},{40,8},{64,32},{72,40},{96,64},{104,72},{1,9... | collective-permute-start | bytes 1572872 | tf_op jit(solution)/shard_map/ppermute | solution.py:133
  26.6 16.2 %collective-permute-start.6 = (bf16[8,256,128]{2,1,0:T(8,128)(2,1)S(1)}, bf16[8,256,128]{2,1,0:T(8,128)(2,1)}, u32[]{:S(2)}, u32[]{:S(2)}) collective-permute-start(bf16[8,256,128]{2,1,0:T(8,128)(2,1)S(1)} %collective-permute-done.3.refs_5_.refs_4_), channel_id=1, source_target_pairs={{0,32},{8,40},{32,64},{40,72},{64,96},{72,104},{96,0},{104,8},{1,3... | collective-permute-start | bytes 1572872 | tf_op jit(solution)/shard_map/ppermute | solution.py:133
  29.9 1.3 %copy-start = (bf16[32,256,128]{2,1,0:T(8,128)(2,1)}, bf16[32,256,128]{2,1,0:T(8,128)(2,1)S(1)}, u32[]{:S(2)}) copy-start(bf16[32,256,128]{2,1,0:T(8,128)(2,1)S(1)} %collective-permute-done.refs_1_) | copy-start | bytes 6291460
  31.2 21.2 %collective-permute-start.2 = (bf16[8,256,128]{2,1,0:T(8,128)(2,1)}, bf16[8,256,128]{2,1,0:T(8,128)(2,1)}, u32[]{:S(2)}, u32[]{:S(2)}) collective-permute-start(bf16[8,256,128]{2,1,0:T(8,128)(2,1)} %get-tuple-element.41), channel_id=1, source_target_pairs={{0,96},{8,104},{32,0},{40,8},{64,32},{72,40},{96,64},{104,72},{1,9... | collective-permute-start | bytes 1572872 | tf_op jit(solution)/shard_map/ppermute | solution.py:133
  31.2 21.2 %collective-permute-start.4 = (bf16[8,256,128]{2,1,0:T(8,128)(2,1)}, bf16[8,256,128]{2,1,0:T(8,128)(2,1)}, u32[]{:S(2)}, u32[]{:S(2)}) collective-permute-start(bf16[8,256,128]{2,1,0:T(8,128)(2,1)} %get-tuple-element.43), channel_id=1, source_target_pairs={{0,32},{8,40},{32,64},{40,72},{64,96},{72,104},{96,0},{104,8},{1,3... | collective-permute-start | bytes 1572872 | tf_op jit(solution)/shard_map/ppermute | solution.py:133
  52.4 1.6 %copy-start.1 = (bf16[32,256,128]{2,1,0:T(8,128)(2,1)S(1)}, bf16[32,256,128]{2,1,0:T(8,128)(2,1)}, u32[]{:S(2)}) copy-start(bf16[32,256,128]{2,1,0:T(8,128)(2,1)} %copy-done) | copy-start | bytes 6291460
  59.3 0.8 copy-start.2
  60.1 8.3 %collective-permute-start.11 = (bf16[32,256,128]{2,1,0:T(8,128)(2,1)}, bf16[32,256,128]{2,1,0:T(8,128)(2,1)}, u32[]{:S(2)}, u32[]{:S(2)}) collective-permute-start(bf16[32,256,128]{2,1,0:T(8,128)(2,1)} %collective-permute-done.7.refs_0_), channel_id=1, source_target_pairs={{0,8},{8,0},{32,40},{40,32},{64,72},{72,64},{96,104},{104,96},{1,9... | collective-permute-start | bytes 6291464 | tf_op jit(solution)/shard_map/ppermute | solution.py:133
  60.1 15.2 %collective-permute-start.10 = (bf16[512,256]{1,0:T(8,128)(2,1)}, bf16[512,256]{1,0:T(8,128)(2,1)}, u32[]{:S(2)}, u32[]{:S(2)}) collective-permute-start(bf16[512,256]{1,0:T(8,128)(2,1)} %get-tuple-element.51), channel_id=1, source_target_pairs={{0,6},{8,14},{32,38},{40,46},{64,70},{72,78},{96,102},{104,110},{1... | collective-permute-start | bytes 786440 | tf_op jit(solution)/shard_map/ppermute | solution.py:133
  62.9 12.4 %collective-permute-start.9 = (bf16[512,256]{1,0:T(8,128)(2,1)}, bf16[512,256]{1,0:T(8,128)(2,1)}, u32[]{:S(2)}, u32[]{:S(2)}) collective-permute-start(bf16[512,256]{1,0:T(8,128)(2,1)} %get-tuple-element.50), channel_id=1, source_target_pairs={{0,4},{8,12},{32,36},{40,44},{64,68},{72,76},{96,100},{104,108},{1... | collective-permute-start | bytes 786440 | tf_op jit(solution)/shard_map/ppermute | solution.py:133
  63.7 15.7 %collective-permute-start.8 = (bf16[512,256]{1,0:T(8,128)(2,1)S(1)}, bf16[512,256]{1,0:T(8,128)(2,1)}, u32[]{:S(2)}, u32[]{:S(2)}) collective-permute-start(bf16[512,256]{1,0:T(8,128)(2,1)S(1)} %get-tuple-element.49), channel_id=1, source_target_pairs={{0,2},{8,10},{32,34},{40,42},{64,66},{72,74},{96,98},{104,106},{1,... | collective-permute-start | bytes 786440 | tf_op jit(solution)/shard_map/ppermute | solution.py:133
  64.6 14.9 %copy-start.3 = (f32[512,256]{1,0:T(8,128)S(1)}, f32[512,256]{1,0:T(8,128)}, u32[]{:S(2)}) copy-start(f32[512,256]{1,0:T(8,128)} %copy-done.2) | copy-start | bytes 1572868
  68.4 17.7 %collective-permute-start.14 = (bf16[256,256]{1,0:T(8,128)(2,1)S(1)}, bf16[256,256]{1,0:T(8,128)(2,1)S(1)}, u32[]{:S(2)}, u32[]{:S(2)}) collective-permute-start(bf16[256,256]{1,0:T(8,128)(2,1)S(1)} %get-tuple-element.60), channel_id=1, source_target_pairs={{0,6},{8,14},{32,38},{40,46},{64,70},{72,78},{96,102},{104,110},{1... | collective-permute-start | bytes 393224 | tf_op jit(solution)/shard_map/ppermute | solution.py:133
  70.8 16.5 %collective-permute-start.13 = (bf16[256,256]{1,0:T(8,128)(2,1)S(1)}, bf16[256,256]{1,0:T(8,128)(2,1)S(1)}, u32[]{:S(2)}, u32[]{:S(2)}) collective-permute-start(bf16[256,256]{1,0:T(8,128)(2,1)S(1)} %get-tuple-element.59), channel_id=1, source_target_pairs={{0,4},{8,12},{32,36},{40,44},{64,68},{72,76},{96,100},{104,108},{1... | collective-permute-start | bytes 393224 | tf_op jit(solution)/shard_map/ppermute | solution.py:133
  75.3 12.0 %collective-permute-start.12 = (bf16[256,256]{1,0:T(8,128)(2,1)S(1)}, bf16[256,256]{1,0:T(8,128)(2,1)S(1)}, u32[]{:S(2)}, u32[]{:S(2)}) collective-permute-start(bf16[256,256]{1,0:T(8,128)(2,1)S(1)} %get-tuple-element.58), channel_id=1, source_target_pairs={{0,2},{8,10},{32,34},{40,42},{64,66},{72,74},{96,98},{104,106},{1,... | collective-permute-start | bytes 393224 | tf_op jit(solution)/shard_map/ppermute | solution.py:133
  80.6 13.9 %copy-start.4 = (f32[512,256]{1,0:T(8,128)}, f32[512,256]{1,0:T(8,128)S(1)}, u32[]{:S(2)}) copy-start(f32[512,256]{1,0:T(8,128)S(1)} %add_add_fusion) | copy-start | bytes 1572868
  84.6 6.4 %collective-permute-start.20 = (bf16[256,256]{1,0:T(8,128)(2,1)S(1)}, bf16[256,256]{1,0:T(8,128)(2,1)S(1)}, u32[]{:S(2)}, u32[]{:S(2)}) collective-permute-start(bf16[256,256]{1,0:T(8,128)(2,1)S(1)} %get-tuple-element.65), channel_id=1, source_target_pairs={{0,6},{8,14},{32,38},{40,46},{64,70},{72,78},{96,102},{104,110},{1... | collective-permute-start | bytes 393224 | tf_op jit(solution)/shard_map/ppermute | solution.py:133
  85.3 7.6 %collective-permute-start.19 = (bf16[256,256]{1,0:T(8,128)(2,1)S(1)}, bf16[256,256]{1,0:T(8,128)(2,1)S(1)}, u32[]{:S(2)}, u32[]{:S(2)}) collective-permute-start(bf16[256,256]{1,0:T(8,128)(2,1)S(1)} %get-tuple-element.64), channel_id=1, source_target_pairs={{0,4},{8,12},{32,36},{40,44},{64,68},{72,76},{96,100},{104,108},{1... | collective-permute-start | bytes 393224 | tf_op jit(solution)/shard_map/ppermute | solution.py:133
  86.1 8.3 %collective-permute-start.18 = (bf16[256,256]{1,0:T(8,128)(2,1)S(1)}, bf16[256,256]{1,0:T(8,128)(2,1)S(1)}, u32[]{:S(2)}, u32[]{:S(2)}) collective-permute-start(bf16[256,256]{1,0:T(8,128)(2,1)S(1)} %get-tuple-element.63), channel_id=1, source_target_pairs={{0,2},{8,10},{32,34},{40,42},{64,66},{72,74},{96,98},{104,106},{1,... | collective-permute-start | bytes 393224 | tf_op jit(solution)/shard_map/ppermute | solution.py:133
  87.4 7.1 %collective-permute-start.15 = (bf16[256,256]{1,0:T(8,128)(2,1)S(1)}, bf16[256,256]{1,0:T(8,128)(2,1)S(1)}, u32[]{:S(2)}, u32[]{:S(2)}) collective-permute-start(bf16[256,256]{1,0:T(8,128)(2,1)S(1)} %select_convert_fusion.1), channel_id=1, source_target_pairs={{0,1},{8,9},{32,33},{40,41},{64,65},{72,73},{96,97},{104,105},{1,0... | collective-permute-start | bytes 393224 | tf_op jit(solution)/shard_map/ppermute | solution.py:133
  94.6 9.3 %collective-permute-start.21 = (bf16[256,256]{1,0:T(8,128)(2,1)S(1)}, bf16[256,256]{1,0:T(8,128)(2,1)S(1)}, u32[]{:S(2)}, u32[]{:S(2)}) collective-permute-start(bf16[256,256]{1,0:T(8,128)(2,1)S(1)} %select_convert_fusion), channel_id=1, source_target_pairs={{0,1},{8,9},{32,33},{40,41},{64,65},{72,73},{96,97},{104,105},{1,0... | collective-permute-start | bytes 393224 | tf_op jit(solution)/shard_map/ppermute | solution.py:133
  96.2 12.7 %collective-permute-start.16 = (bf16[256,256]{1,0:T(8,128)(2,1)S(1)}, bf16[256,256]{1,0:T(8,128)(2,1)S(1)}, u32[]{:S(2)}, u32[]{:S(2)}) collective-permute-start(bf16[256,256]{1,0:T(8,128)(2,1)S(1)} %get-tuple-element.67), channel_id=1, source_target_pairs={{1,16},{9,24},{33,48},{41,56},{65,80},{73,88},{97,112},{105,120},{... | collective-permute-start | bytes 393224 | tf_op jit(solution)/shard_map/ppermute | solution.py:133
  98.5 12.3 %collective-permute-start.17 = (bf16[256,256]{1,0:T(8,128)(2,1)S(1)}, bf16[256,256]{1,0:T(8,128)(2,1)S(1)}, u32[]{:S(2)}, u32[]{:S(2)}) collective-permute-start(bf16[256,256]{1,0:T(8,128)(2,1)S(1)} %get-tuple-element.67), channel_id=1, source_target_pairs={{32,2},{40,10},{64,4},{72,12},{96,6},{104,14},{33,3},{41,11},{65,5... | collective-permute-start | bytes 393224 | tf_op jit(solution)/shard_map/ppermute | solution.py:133
  104.9 11.6 %collective-permute-start.23 = (bf16[256,256]{1,0:T(8,128)(2,1)S(1)}, bf16[256,256]{1,0:T(8,128)(2,1)S(1)}, u32[]{:S(2)}, u32[]{:S(2)}) collective-permute-start(bf16[256,256]{1,0:T(8,128)(2,1)S(1)} %add_convert_fusion), channel_id=1, source_target_pairs={{32,2},{40,10},{64,4},{72,12},{96,6},{104,14},{33,3},{41,11},{65,5... | collective-permute-start | bytes 393224 | tf_op jit(solution)/shard_map/ppermute | solution.py:133
  108.8 7.7 %collective-permute-start.22 = (bf16[256,256]{0,1:T(8,128)(2,1)S(1)}, bf16[256,256]{0,1:T(8,128)(2,1)S(1)}, u32[]{:S(2)}, u32[]{:S(2)}) collective-permute-start(bf16[256,256]{0,1:T(8,128)(2,1)S(1)} %copy.4), channel_id=1, source_target_pairs={{0,8},{8,0},{32,40},{40,32},{64,72},{72,64},{96,104},{104,96},{1,2... | collective-permute-start | bytes 393224 | tf_op jit(solution)/shard_map/ppermute | solution.py:133

commit v5 on v3

--- a/solution.py
+++ b/solution.py
@@ -199,7 +199,8 @@
     turn_one = across(sent_one)
     here = shift(sent_one, lambda x, y, z, c: (x, 3 - y, z, c) if y in (1, 2) else None).astype(f32)
     here = jnp.where(edge, one, here)
-    two = over_y(near_sum[256:], over_x(far_two))
+    _, far_two = after((one, over_x(far_two)))
+    two = over_y(near_sum[256:], far_two)
     sent_two = two.astype(bf16)
     turn_two = across(sent_two)
     there = shift(sent_two, lambda x, y, z, c: (x, 3 - y if y in (1, 2) else y, z, 1 - c)).astype(f32)

time: 121 us -> 118 us (0.975)
  local copies, waits for them, and re-layouts: 5.61 us -> 2.03 us
  waiting for transfers between devices: 52.9 us -> 54.3 us
    unnamed x10 -> x6, local copies, waits for them, and re-layouts: 4.38 us -> 0.8 us
    ppermute x24, waiting for transfers between devices: 52.9 us -> 54.3 us  [shift(): return lax.ppermute(array, AXES, pairs)]
  transfers between devices with their start and end apart: 24 -> 24, of which waited for: 11 -> 10; matrix products, arithmetic and copies ran while one was open for 1% -> 2% of each run, Pallas kernels for 11% -> 12%
where the time goes in v5:
time: 118 us; the launch traced here: 117 us
  waiting for transfers between devices  54.3 us (46%)
  starting transfers between devices  35.3 us (30%)
  Pallas kernels  22.8 us (19%)
  other arithmetic  2.76 us (2%)
  local copies, waits for them, and re-layouts  2.03 us (2%)
    ppermute x24, waiting for transfers between devices, shift(): return lax.ppermute(array, AXES, pairs)  54.3 us
    ppermute x24, starting transfers between devices, shift(): return lax.ppermute(array, AXES, pairs)  35.3 us
    pallas_call x3, Pallas kernels, gram(): pl.pallas_call(functools.partial(gram_kernel, len(rows)), in_specs=[IN_SM...  13.8 us
    pallas_call x1, Pallas kernels, features(): pl.pallas_call(feature_kernel, grid_spec=pltpu.PrefetchScalarGridSpec(num...  8.93 us
  transfers between devices with their start and end apart: 24, of which 10 were waited for; matrix products, arithmetic and copies ran while one was open for 2% of the time, Pallas kernels for 12%

profile of v5, /device:TPU:104, one launch (start us, length us, event | category | flops | bytes accessed | tf_op | source)
XLA Modules:
  0.0 117.3 jit_solution(3706835868708670027)
XLA Ops:
  0.0 8.9 %features.1 = (bf16[32,256,128]{2,1,0:T(8,128)(2,1)S(1)}, bf16[8,256,128]{2,1,0:T(8,128)(2,1)S(1)}, bf16[8,256,128]{2,1,0:T(8,128)(2,1)S(1)}, bf16[8,256,128]{2,1,0:T(8,128)(2,1)S(1)}, bf16[8,256,128]{2,1,0:T(8,128)(2,1)}) custom-call(s32[1]{0:T(128)} %bitcast.7.s_ref, bf16[1,256,64,256]{3,2,1,0:T(8,128)(2,1)} %g_ref.1, bf16[1,256,64,256]{3,2,1,0:T(8,128)(2,1)} %i_ref.1), custom_call_target="tpu_custom_call" | custom-call | flops 1 | bytes 1 | tf_op jit(solution)/shard_map/features/pallas_call | solution.py:56
  8.9 2.3 %collective-permute-start.7 = (bf16[32,256,128]{2,1,0:T(8,128)(2,1)S(1)}, bf16[32,256,128]{2,1,0:T(8,128)(2,1)}, u32[]{:S(2)}, u32[]{:S(2)}) collective-permute-start(bf16[32,256,128]{2,1,0:T(8,128)(2,1)S(1)} %get-tuple-element.33.refs_0_.refs_2_.refs_1_), channel_id=1, source_target_pairs={{0,16},{8,24},{32,48},{40,56},{64,80},{72,88},{96,112},{104,120},{... | collective-permute-start | bytes 6291464 | tf_op jit(solution)/shard_map/ppermute | solution.py:133
  11.2 0.4 collective-permute-start.1
  11.6 0.1 collective-permute-start.2
  11.7 3.1 %collective-permute-start.3 = (bf16[8,256,128]{2,1,0:T(8,128)(2,1)S(1)}, bf16[8,256,128]{2,1,0:T(8,128)(2,1)}, u32[]{:S(2)}, u32[]{:S(2)}) collective-permute-start(bf16[8,256,128]{2,1,0:T(8,128)(2,1)S(1)} %get-tuple-element.36), channel_id=1, source_target_pairs={{0,32},{8,40},{32,64},{40,72},{64,96},{72,104},{96,0},{104,8},{1,3... | collective-permute-start | bytes 1572872 | tf_op jit(solution)/shard_map/ppermute | solution.py:133
  14.9 12.3 %collective-permute-done.1.refs_3_.refs_2_ = bf16[8,256,128]{2,1,0:T(8,128)(2,1)S(1)} collective-permute-done((bf16[8,256,128]{2,1,0:T(8,128)(2,1)S(1)}, bf16[8,256,128]{2,1,0:T(8,128)(2,1)S(1)}, u32[]{:S(2)}, u32[]{:S(2)}) %collective-permute-start.1) | collective-permute-done | bytes 524320 | tf_op jit(solution)/shard_map/ppermute | solution.py:133
  27.2 10.5 %collective-permute-done.2.refs_4_.refs_3_ = bf16[8,256,128]{2,1,0:T(8,128)(2,1)S(1)} collective-permute-done((bf16[8,256,128]{2,1,0:T(8,128)(2,1)S(1)}, bf16[8,256,128]{2,1,0:T(8,128)(2,1)S(1)}, u32[]{:S(2)}, u32[]{:S(2)}) %collective-permute-start.2) | collective-permute-done | bytes 524320 | tf_op jit(solution)/shard_map/ppermute | solution.py:133
  37.7 0.0 collective-permute-done.3.refs_5_.refs_4_
  37.7 3.2 %collective-permute-start.6 = (bf16[8,256,128]{2,1,0:T(8,128)(2,1)}, bf16[8,256,128]{2,1,0:T(8,128)(2,1)}, u32[]{:S(2)}, u32[]{:S(2)}) collective-permute-start(bf16[8,256,128]{2,1,0:T(8,128)(2,1)} %collective-permute-done.3.refs_5_.refs_4_), channel_id=1, source_target_pairs={{0,32},{8,40},{32,64},{40,72},{64,96},{72,104},{96,0},{104,8},{1,3... | collective-permute-start | bytes 1572872 | tf_op jit(solution)/shard_map/ppermute | solution.py:133
  41.0 0.1 and_select_fusion
  41.1 0.1 pad_add_fusion.s_ref
  41.1 0.0 collective-permute-done.4.refs_6_.refs_5_
  41.1 11.1 %collective-permute-done.5.refs_7_.refs_6_ = bf16[8,256,128]{2,1,0:T(8,128)(2,1)} collective-permute-done((bf16[8,256,128]{2,1,0:T(8,128)(2,1)S(1)}, bf16[8,256,128]{2,1,0:T(8,128)(2,1)}, u32[]{:S(2)}, u32[]{:S(2)}) %collective-permute-start.5) | collective-permute-done | bytes 524320 | tf_op jit(solution)/shard_map/ppermute | solution.py:133
  52.3 6.0 %gram.3 = (f32[512,256]{1,0:T(8,128)S(1)}, bf16[512,256]{1,0:T(8,128)(2,1)S(1)}, bf16[512,256]{1,0:T(8,128)(2,1)}, bf16[512,256]{1,0:T(8,128)(2,1)}) custom-call(s32[7]{0:T(128)S(1)} %pad_add_fusion.s_ref, bf16[32,256,128]{2,1,0:T(8,128)(2,1)S(1)} %get-tuple-element.33.refs_0_.refs_2_.refs_1_, bf16[32,256,128]{2,1,0:T(8,128)(2,1)} %collective-permute-done.refs_1_, ...), custom_call_target="tpu_custom_call" | custom-call | flops 1 | bytes 1 | tf_op jit(solution)/shard_map/gram/pallas_call | solution.py:106
  58.3 0.8 copy-done
  59.1 2.8 %collective-permute-start.10 = (bf16[512,256]{1,0:T(8,128)(2,1)}, bf16[512,256]{1,0:T(8,128)(2,1)}, u32[]{:S(2)}, u32[]{:S(2)}) collective-permute-start(bf16[512,256]{1,0:T(8,128)(2,1)} %get-tuple-element.45), channel_id=1, source_target_pairs={{0,6},{8,14},{32,38},{40,46},{64,70},{72,78},{96,102},{104,110},{1... | collective-permute-start | bytes 786440 | tf_op jit(solution)/shard_map/ppermute | solution.py:133
  61.9 0.8 collective-permute-start.9
  62.7 0.9 collective-permute-start.8
  63.6 3.8 %gram.4 = (f32[256,256]{1,0:T(8,128)S(1)}, bf16[256,256]{1,0:T(8,128)(2,1)S(1)}, bf16[256,256]{1,0:T(8,128)(2,1)S(1)}, bf16[256,256]{1,0:T(8,128)(2,1)S(1)}) custom-call(s32[7]{0:T(128)S(1)} %pad_add_fusion.s_ref, bf16[32,256,128]{2,1,0:T(8,128)(2,1)} %collective-permute-done.7.refs_0_, bf16[32,256,128]{2,1,0:T(8,128)(2,1)S(1)} %get-tuple-element.33.refs_0_.refs_2_.refs_1_, ...), custom_call_target="tpu_custom_call" | custom-call | flops 1 | bytes 1 | tf_op jit(solution)/shard_map/gram/pallas_call | solution.py:106
  67.4 2.4 %collective-permute-start.14 = (bf16[256,256]{1,0:T(8,128)(2,1)S(1)}, bf16[256,256]{1,0:T(8,128)(2,1)S(1)}, u32[]{:S(2)}, u32[]{:S(2)}) collective-permute-start(bf16[256,256]{1,0:T(8,128)(2,1)S(1)} %get-tuple-element.54), channel_id=1, source_target_pairs={{0,6},{8,14},{32,38},{40,46},{64,70},{72,78},{96,102},{104,110},{1... | collective-permute-start | bytes 393224 | tf_op jit(solution)/shard_map/ppermute | solution.py:133
  69.8 1.5 %collective-permute-start.13 = (bf16[256,256]{1,0:T(8,128)(2,1)S(1)}, bf16[256,256]{1,0:T(8,128)(2,1)S(1)}, u32[]{:S(2)}, u32[]{:S(2)}) collective-permute-start(bf16[256,256]{1,0:T(8,128)(2,1)S(1)} %get-tuple-element.53), channel_id=1, source_target_pairs={{0,4},{8,12},{32,36},{40,44},{64,68},{72,76},{96,100},{104,108},{1... | collective-permute-start | bytes 393224 | tf_op jit(solution)/shard_map/ppermute | solution.py:133
  71.4 2.9 %collective-permute-done.10 = bf16[512,256]{1,0:T(8,128)(2,1)} collective-permute-done((bf16[512,256]{1,0:T(8,128)(2,1)}, bf16[512,256]{1,0:T(8,128)(2,1)}, u32[]{:S(2)}, u32[]{:S(2)}) %collective-permute-start.10) | collective-permute-done | bytes 262176 | tf_op jit(solution)/shard_map/ppermute | solution.py:133
  74.3 4.1 %collective-permute-done.8 = bf16[512,256]{1,0:T(8,128)(2,1)} collective-permute-done((bf16[512,256]{1,0:T(8,128)(2,1)S(1)}, bf16[512,256]{1,0:T(8,128)(2,1)}, u32[]{:S(2)}, u32[]{:S(2)}) %collective-permute-start.8) | collective-permute-done | bytes 262176 | tf_op jit(solution)/shard_map/ppermute | solution.py:133
  78.4 1.2 %add_add_fusion = f32[512,256]{1,0:T(8,128)S(1)} fusion(bf16[512,256]{1,0:T(8,128)(2,1)} %collective-permute-done.10, bf16[512,256]{1,0:T(8,128)(2,1)} %collective-permute-done.9, f32[512,256]{1,0:T(8,128)S(1)} %copy-done.1, bf16[512,256]{1,0:T(8,128)(2,1)} %collective-permute-done.8), kind=kLoop, calls=%fused_computation.1 | loop fusion | flops 786432 | bytes 1835008 | tf_op jit(solution)/shard_map/add | solution.py:177
  79.6 0.0 copy-start.2
  79.6 4.0 %gram.5 = (f32[256,256]{1,0:T(8,128)S(1)}, bf16[256,256]{1,0:T(8,128)(2,1)S(1)}, bf16[256,256]{1,0:T(8,128)(2,1)S(1)}, bf16[256,256]{1,0:T(8,128)(2,1)S(1)}) custom-call(s32[7]{0:T(128)S(1)} %pad_add_fusion.s_ref, bf16[32,256,128]{2,1,0:T(8,128)(2,1)} %collective-permute-done.11.refs_0_, bf16[32,256,128]{2,1,0:T(8,128)(2,1)S(1)} %get-tuple-element.33.refs_0_.refs_2_.refs_1_, ...), custom_call_target="tpu_custom_call" | custom-call | flops 1 | bytes 1 | tf_op jit(solution)/shard_map/gram/pallas_call | solution.py:106
  83.6 0.7 collective-permute-start.20
  84.3 0.8 collective-permute-start.19
  85.1 1.2 collective-permute-start.18
  86.3 0.1 select_convert_fusion.1
  86.4 1.5 %collective-permute-start.15 = (bf16[256,256]{1,0:T(8,128)(2,1)S(1)}, bf16[256,256]{1,0:T(8,128)(2,1)S(1)}, u32[]{:S(2)}, u32[]{:S(2)}) collective-permute-start(bf16[256,256]{1,0:T(8,128)(2,1)S(1)} %select_convert_fusion.1), channel_id=1, source_target_pairs={{0,1},{8,9},{32,33},{40,41},{64,65},{72,73},{96,97},{104,105},{1,0... | collective-permute-start | bytes 393224 | tf_op jit(solution)/shard_map/ppermute | solution.py:133
  87.9 2.2 %collective-permute-done.20 = bf16[256,256]{1,0:T(8,128)(2,1)S(1)} collective-permute-done((bf16[256,256]{1,0:T(8,128)(2,1)S(1)}, bf16[256,256]{1,0:T(8,128)(2,1)S(1)}, u32[]{:S(2)}, u32[]{:S(2)}) %collective-permute-start.20) | collective-permute-done | bytes 131104 | tf_op jit(solution)/shard_map/ppermute | solution.py:133
  90.1 1.9 %collective-permute-done.19 = bf16[256,256]{1,0:T(8,128)(2,1)S(1)} collective-permute-done((bf16[256,256]{1,0:T(8,128)(2,1)S(1)}, bf16[256,256]{1,0:T(8,128)(2,1)S(1)}, u32[]{:S(2)}, u32[]{:S(2)}) %collective-permute-start.19) | collective-permute-done | bytes 131104 | tf_op jit(solution)/shard_map/ppermute | solution.py:133
  91.9 1.5 %collective-permute-done.18 = bf16[256,256]{1,0:T(8,128)(2,1)S(1)} collective-permute-done((bf16[256,256]{1,0:T(8,128)(2,1)S(1)}, bf16[256,256]{1,0:T(8,128)(2,1)S(1)}, u32[]{:S(2)}, u32[]{:S(2)}) %collective-permute-start.18) | collective-permute-done | bytes 131104 | tf_op jit(solution)/shard_map/ppermute | solution.py:133
  93.4 0.1 add_add_fusion.1
  93.5 0.1 fusion.3
  93.6 1.5 %collective-permute-start.21 = (bf16[256,256]{1,0:T(8,128)(2,1)S(1)}, bf16[256,256]{1,0:T(8,128)(2,1)S(1)}, u32[]{:S(2)}, u32[]{:S(2)}) collective-permute-start(bf16[256,256]{1,0:T(8,128)(2,1)S(1)} %select_convert_fusion), channel_id=1, source_target_pairs={{0,1},{8,9},{32,33},{40,41},{64,65},{72,73},{96,97},{104,105},{1,0... | collective-permute-start | bytes 393224 | tf_op jit(solution)/shard_map/ppermute | solution.py:133
  95.2 2.8 %collective-permute-start.16 = (bf16[256,256]{1,0:T(8,128)(2,1)S(1)}, bf16[256,256]{1,0:T(8,128)(2,1)S(1)}, u32[]{:S(2)}, u32[]{:S(2)}) collective-permute-start(bf16[256,256]{1,0:T(8,128)(2,1)S(1)} %get-tuple-element.61), channel_id=1, source_target_pairs={{1,16},{9,24},{33,48},{41,56},{65,80},{73,88},{97,112},{105,120},{... | collective-permute-start | bytes 393224 | tf_op jit(solution)/shard_map/ppermute | solution.py:133
  97.9 5.2 %collective-permute-start.17 = (bf16[256,256]{1,0:T(8,128)(2,1)S(1)}, bf16[256,256]{1,0:T(8,128)(2,1)S(1)}, u32[]{:S(2)}, u32[]{:S(2)}) collective-permute-start(bf16[256,256]{1,0:T(8,128)(2,1)S(1)} %get-tuple-element.61), channel_id=1, source_target_pairs={{32,2},{40,10},{64,4},{72,12},{96,6},{104,14},{33,3},{41,11},{65,5... | collective-permute-start | bytes 393224 | tf_op jit(solution)/shard_map/ppermute | solution.py:133
  103.1 1.0 add_convert_fusion
  104.1 4.0 %collective-permute-start.23 = (bf16[256,256]{1,0:T(8,128)(2,1)S(1)}, bf16[256,256]{1,0:T(8,128)(2,1)S(1)}, u32[]{:S(2)}, u32[]{:S(2)}) collective-permute-start(bf16[256,256]{1,0:T(8,128)(2,1)S(1)} %add_convert_fusion), channel_id=1, source_target_pairs={{32,2},{40,10},{64,4},{72,12},{96,6},{104,14},{33,3},{41,11},{65,5... | collective-permute-start | bytes 393224 | tf_op jit(solution)/shard_map/ppermute | solution.py:133
  108.1 0.1 copy.4
  108.2 0.1 collective-permute-start.22
  108.4 0.1 copy.3
  108.5 3.8 %collective-permute-done.17 = bf16[256,256]{1,0:T(8,128)(2,1)S(1)} collective-permute-done((bf16[256,256]{1,0:T(8,128)(2,1)S(1)}, bf16[256,256]{1,0:T(8,128)(2,1)S(1)}, u32[]{:S(2)}, u32[]{:S(2)}) %collective-permute-start.17) | collective-permute-done | bytes 131104 | tf_op jit(solution)/shard_map/ppermute | solution.py:133
  112.3 3.9 %collective-permute-done.23 = bf16[256,256]{1,0:T(8,128)(2,1)S(1)} collective-permute-done((bf16[256,256]{1,0:T(8,128)(2,1)S(1)}, bf16[256,256]{1,0:T(8,128)(2,1)S(1)}, u32[]{:S(2)}, u32[]{:S(2)}) %collective-permute-start.23) | collective-permute-done | bytes 131104 | tf_op jit(solution)/shard_map/ppermute | solution.py:133
  116.2 0.1 fusion.1
  116.3 1.0 copy.5
  (24 shorter events, 0.2 us)
Async XLA Ops:
  8.9 43.4 %collective-permute-start = (bf16[32,256,128]{2,1,0:T(8,128)(2,1)S(1)}, bf16[32,256,128]{2,1,0:T(8,128)(2,1)}, u32[]{:S(2)}, u32[]{:S(2)}) collective-permute-start(bf16[32,256,128]{2,1,0:T(8,128)(2,1)S(1)} %get-tuple-element.33.refs_0_.refs_2_.refs_1_), channel_id=1, source_target_pairs={{0,8},{8,0},{32,40},{40,32},{64,72},{72,64},{96,104},{104,96},{1,9... | collective-permute-start | bytes 6291464 | tf_op jit(solution)/shard_map/ppermute | solution.py:133
  8.9 50.2 %collective-permute-start.7 = (bf16[32,256,128]{2,1,0:T(8,128)(2,1)S(1)}, bf16[32,256,128]{2,1,0:T(8,128)(2,1)}, u32[]{:S(2)}, u32[]{:S(2)}) collective-permute-start(bf16[32,256,128]{2,1,0:T(8,128)(2,1)S(1)} %get-tuple-element.33.refs_0_.refs_2_.refs_1_), channel_id=1, source_target_pairs={{0,16},{8,24},{32,48},{40,56},{64,80},{72,88},{96,112},{104,120},{... | collective-permute-start | bytes 6291464 | tf_op jit(solution)/shard_map/ppermute | solution.py:133
  11.2 16.0 %collective-permute-start.1 = (bf16[8,256,128]{2,1,0:T(8,128)(2,1)S(1)}, bf16[8,256,128]{2,1,0:T(8,128)(2,1)S(1)}, u32[]{:S(2)}, u32[]{:S(2)}) collective-permute-start(bf16[8,256,128]{2,1,0:T(8,128)(2,1)S(1)} %get-tuple-element.34), channel_id=1, source_target_pairs={{0,96},{8,104},{32,0},{40,8},{64,32},{72,40},{96,64},{104,72},{1,9... | collective-permute-start | bytes 1572872 | tf_op jit(solution)/shard_map/ppermute | solution.py:133
  11.6 26.1 %collective-permute-start.2 = (bf16[8,256,128]{2,1,0:T(8,128)(2,1)S(1)}, bf16[8,256,128]{2,1,0:T(8,128)(2,1)S(1)}, u32[]{:S(2)}, u32[]{:S(2)}) collective-permute-start(bf16[8,256,128]{2,1,0:T(8,128)(2,1)S(1)} %get-tuple-element.35), channel_id=1, source_target_pairs={{0,96},{8,104},{32,0},{40,8},{64,32},{72,40},{96,64},{104,72},{1,9... | collective-permute-start | bytes 1572872 | tf_op jit(solution)/shard_map/ppermute | solution.py:133
  11.7 26.0 %collective-permute-start.3 = (bf16[8,256,128]{2,1,0:T(8,128)(2,1)S(1)}, bf16[8,256,128]{2,1,0:T(8,128)(2,1)}, u32[]{:S(2)}, u32[]{:S(2)}) collective-permute-start(bf16[8,256,128]{2,1,0:T(8,128)(2,1)S(1)} %get-tuple-element.36), channel_id=1, source_target_pairs={{0,32},{8,40},{32,64},{40,72},{64,96},{72,104},{96,0},{104,8},{1,3... | collective-permute-start | bytes 1572872 | tf_op jit(solution)/shard_map/ppermute | solution.py:133
  27.2 13.9 %collective-permute-start.4 = (bf16[8,256,128]{2,1,0:T(8,128)(2,1)}, bf16[8,256,128]{2,1,0:T(8,128)(2,1)}, u32[]{:S(2)}, u32[]{:S(2)}) collective-permute-start(bf16[8,256,128]{2,1,0:T(8,128)(2,1)} %get-tuple-element.37), channel_id=1, source_target_pairs={{0,32},{8,40},{32,64},{40,72},{64,96},{72,104},{96,0},{104,8},{1,3... | collective-permute-start | bytes 1572872 | tf_op jit(solution)/shard_map/ppermute | solution.py:133
  37.7 14.6 %collective-permute-start.5 = (bf16[8,256,128]{2,1,0:T(8,128)(2,1)S(1)}, bf16[8,256,128]{2,1,0:T(8,128)(2,1)}, u32[]{:S(2)}, u32[]{:S(2)}) collective-permute-start(bf16[8,256,128]{2,1,0:T(8,128)(2,1)S(1)} %collective-permute-done.1.refs_3_.refs_2_), channel_id=1, source_target_pairs={{0,96},{8,104},{32,0},{40,8},{64,32},{72,40},{96,64},{104,72},{1,9... | collective-permute-start | bytes 1572872 | tf_op jit(solution)/shard_map/ppermute | solution.py:133
  37.7 14.5 %collective-permute-start.6 = (bf16[8,256,128]{2,1,0:T(8,128)(2,1)}, bf16[8,256,128]{2,1,0:T(8,128)(2,1)}, u32[]{:S(2)}, u32[]{:S(2)}) collective-permute-start(bf16[8,256,128]{2,1,0:T(8,128)(2,1)} %collective-permute-done.3.refs_5_.refs_4_), channel_id=1, source_target_pairs={{0,32},{8,40},{32,64},{40,72},{64,96},{72,104},{96,0},{104,8},{1,3... | collective-permute-start | bytes 1572872 | tf_op jit(solution)/shard_map/ppermute | solution.py:133
  58.3 0.8 copy-start
  59.1 8.3 %collective-permute-start.11 = (bf16[32,256,128]{2,1,0:T(8,128)(2,1)}, bf16[32,256,128]{2,1,0:T(8,128)(2,1)}, u32[]{:S(2)}, u32[]{:S(2)}) collective-permute-start(bf16[32,256,128]{2,1,0:T(8,128)(2,1)} %collective-permute-done.7.refs_0_), channel_id=1, source_target_pairs={{0,8},{8,0},{32,40},{40,32},{64,72},{72,64},{96,104},{104,96},{1,9... | collective-permute-start | bytes 6291464 | tf_op jit(solution)/shard_map/ppermute | solution.py:133
  59.1 15.2 %collective-permute-start.10 = (bf16[512,256]{1,0:T(8,128)(2,1)}, bf16[512,256]{1,0:T(8,128)(2,1)}, u32[]{:S(2)}, u32[]{:S(2)}) collective-permute-start(bf16[512,256]{1,0:T(8,128)(2,1)} %get-tuple-element.45), channel_id=1, source_target_pairs={{0,6},{8,14},{32,38},{40,46},{64,70},{72,78},{96,102},{104,110},{1... | collective-permute-start | bytes 786440 | tf_op jit(solution)/shard_map/ppermute | solution.py:133
  61.9 12.4 %collective-permute-start.9 = (bf16[512,256]{1,0:T(8,128)(2,1)}, bf16[512,256]{1,0:T(8,128)(2,1)}, u32[]{:S(2)}, u32[]{:S(2)}) collective-permute-start(bf16[512,256]{1,0:T(8,128)(2,1)} %get-tuple-element.44), channel_id=1, source_target_pairs={{0,4},{8,12},{32,36},{40,44},{64,68},{72,76},{96,100},{104,108},{1... | collective-permute-start | bytes 786440 | tf_op jit(solution)/shard_map/ppermute | solution.py:133
  62.7 15.7 %collective-permute-start.8 = (bf16[512,256]{1,0:T(8,128)(2,1)S(1)}, bf16[512,256]{1,0:T(8,128)(2,1)}, u32[]{:S(2)}, u32[]{:S(2)}) collective-permute-start(bf16[512,256]{1,0:T(8,128)(2,1)S(1)} %get-tuple-element.43), channel_id=1, source_target_pairs={{0,2},{8,10},{32,34},{40,42},{64,66},{72,74},{96,98},{104,106},{1,... | collective-permute-start | bytes 786440 | tf_op jit(solution)/shard_map/ppermute | solution.py:133
  63.6 14.8 %copy-start.1 = (f32[512,256]{1,0:T(8,128)S(1)}, f32[512,256]{1,0:T(8,128)}, u32[]{:S(2)}) copy-start(f32[512,256]{1,0:T(8,128)} %copy-done) | copy-start | bytes 1572868
  67.4 17.7 %collective-permute-start.14 = (bf16[256,256]{1,0:T(8,128)(2,1)S(1)}, bf16[256,256]{1,0:T(8,128)(2,1)S(1)}, u32[]{:S(2)}, u32[]{:S(2)}) collective-permute-start(bf16[256,256]{1,0:T(8,128)(2,1)S(1)} %get-tuple-element.54), channel_id=1, source_target_pairs={{0,6},{8,14},{32,38},{40,46},{64,70},{72,78},{96,102},{104,110},{1... | collective-permute-start | bytes 393224 | tf_op jit(solution)/shard_map/ppermute | solution.py:133
  69.8 16.5 %collective-permute-start.13 = (bf16[256,256]{1,0:T(8,128)(2,1)S(1)}, bf16[256,256]{1,0:T(8,128)(2,1)S(1)}, u32[]{:S(2)}, u32[]{:S(2)}) collective-permute-start(bf16[256,256]{1,0:T(8,128)(2,1)S(1)} %get-tuple-element.53), channel_id=1, source_target_pairs={{0,4},{8,12},{32,36},{40,44},{64,68},{72,76},{96,100},{104,108},{1... | collective-permute-start | bytes 393224 | tf_op jit(solution)/shard_map/ppermute | solution.py:133
  74.3 12.0 %collective-permute-start.12 = (bf16[256,256]{1,0:T(8,128)(2,1)S(1)}, bf16[256,256]{1,0:T(8,128)(2,1)S(1)}, u32[]{:S(2)}, u32[]{:S(2)}) collective-permute-start(bf16[256,256]{1,0:T(8,128)(2,1)S(1)} %get-tuple-element.52), channel_id=1, source_target_pairs={{0,2},{8,10},{32,34},{40,42},{64,66},{72,74},{96,98},{104,106},{1,... | collective-permute-start | bytes 393224 | tf_op jit(solution)/shard_map/ppermute | solution.py:133
  79.6 14.0 %copy-start.2 = (f32[512,256]{1,0:T(8,128)}, f32[512,256]{1,0:T(8,128)S(1)}, u32[]{:S(2)}) copy-start(f32[512,256]{1,0:T(8,128)S(1)} %add_add_fusion) | copy-start | bytes 1572868
  83.6 6.4 %collective-permute-start.20 = (bf16[256,256]{1,0:T(8,128)(2,1)S(1)}, bf16[256,256]{1,0:T(8,128)(2,1)S(1)}, u32[]{:S(2)}, u32[]{:S(2)}) collective-permute-start(bf16[256,256]{1,0:T(8,128)(2,1)S(1)} %get-tuple-element.59), channel_id=1, source_target_pairs={{0,6},{8,14},{32,38},{40,46},{64,70},{72,78},{96,102},{104,110},{1... | collective-permute-start | bytes 393224 | tf_op jit(solution)/shard_map/ppermute | solution.py:133
  84.3 7.6 %collective-permute-start.19 = (bf16[256,256]{1,0:T(8,128)(2,1)S(1)}, bf16[256,256]{1,0:T(8,128)(2,1)S(1)}, u32[]{:S(2)}, u32[]{:S(2)}) collective-permute-start(bf16[256,256]{1,0:T(8,128)(2,1)S(1)} %get-tuple-element.58), channel_id=1, source_target_pairs={{0,4},{8,12},{32,36},{40,44},{64,68},{72,76},{96,100},{104,108},{1... | collective-permute-start | bytes 393224 | tf_op jit(solution)/shard_map/ppermute | solution.py:133
  85.1 8.3 %collective-permute-start.18 = (bf16[256,256]{1,0:T(8,128)(2,1)S(1)}, bf16[256,256]{1,0:T(8,128)(2,1)S(1)}, u32[]{:S(2)}, u32[]{:S(2)}) collective-permute-start(bf16[256,256]{1,0:T(8,128)(2,1)S(1)} %get-tuple-element.57), channel_id=1, source_target_pairs={{0,2},{8,10},{32,34},{40,42},{64,66},{72,74},{96,98},{104,106},{1,... | collective-permute-start | bytes 393224 | tf_op jit(solution)/shard_map/ppermute | solution.py:133
  86.4 7.1 %collective-permute-start.15 = (bf16[256,256]{1,0:T(8,128)(2,1)S(1)}, bf16[256,256]{1,0:T(8,128)(2,1)S(1)}, u32[]{:S(2)}, u32[]{:S(2)}) collective-permute-start(bf16[256,256]{1,0:T(8,128)(2,1)S(1)} %select_convert_fusion.1), channel_id=1, source_target_pairs={{0,1},{8,9},{32,33},{40,41},{64,65},{72,73},{96,97},{104,105},{1,0... | collective-permute-start | bytes 393224 | tf_op jit(solution)/shard_map/ppermute | solution.py:133
  93.6 9.5 %collective-permute-start.21 = (bf16[256,256]{1,0:T(8,128)(2,1)S(1)}, bf16[256,256]{1,0:T(8,128)(2,1)S(1)}, u32[]{:S(2)}, u32[]{:S(2)}) collective-permute-start(bf16[256,256]{1,0:T(8,128)(2,1)S(1)} %select_convert_fusion), channel_id=1, source_target_pairs={{0,1},{8,9},{32,33},{40,41},{64,65},{72,73},{96,97},{104,105},{1,0... | collective-permute-start | bytes 393224 | tf_op jit(solution)/shard_map/ppermute | solution.py:133
  95.2 13.2 %collective-permute-start.16 = (bf16[256,256]{1,0:T(8,128)(2,1)S(1)}, bf16[256,256]{1,0:T(8,128)(2,1)S(1)}, u32[]{:S(2)}, u32[]{:S(2)}) collective-permute-start(bf16[256,256]{1,0:T(8,128)(2,1)S(1)} %get-tuple-element.61), channel_id=1, source_target_pairs={{1,16},{9,24},{33,48},{41,56},{65,80},{73,88},{97,112},{105,120},{... | collective-permute-start | bytes 393224 | tf_op jit(solution)/shard_map/ppermute | solution.py:133
  97.9 14.4 %collective-permute-start.17 = (bf16[256,256]{1,0:T(8,128)(2,1)S(1)}, bf16[256,256]{1,0:T(8,128)(2,1)S(1)}, u32[]{:S(2)}, u32[]{:S(2)}) collective-permute-start(bf16[256,256]{1,0:T(8,128)(2,1)S(1)} %get-tuple-element.61), channel_id=1, source_target_pairs={{32,2},{40,10},{64,4},{72,12},{96,6},{104,14},{33,3},{41,11},{65,5... | collective-permute-start | bytes 393224 | tf_op jit(solution)/shard_map/ppermute | solution.py:133
  104.1 12.1 %collective-permute-start.23 = (bf16[256,256]{1,0:T(8,128)(2,1)S(1)}, bf16[256,256]{1,0:T(8,128)(2,1)S(1)}, u32[]{:S(2)}, u32[]{:S(2)}) collective-permute-start(bf16[256,256]{1,0:T(8,128)(2,1)S(1)} %add_convert_fusion), channel_id=1, source_target_pairs={{32,2},{40,10},{64,4},{72,12},{96,6},{104,14},{33,3},{41,11},{65,5... | collective-permute-start | bytes 393224 | tf_op jit(solution)/shard_map/ppermute | solution.py:133
  108.2 8.0 %collective-permute-start.22 = (bf16[256,256]{0,1:T(8,128)(2,1)S(1)}, bf16[256,256]{0,1:T(8,128)(2,1)S(1)}, u32[]{:S(2)}, u32[]{:S(2)}) collective-permute-start(bf16[256,256]{0,1:T(8,128)(2,1)S(1)} %copy.4), channel_id=1, source_target_pairs={{0,8},{8,0},{32,40},{40,32},{64,72},{72,64},{96,104},{104,96},{1,2... | collective-permute-start | bytes 393224 | tf_op jit(solution)/shard_map/ppermute | solution.py:133

commit v6 on v5

--- a/solution.py
+++ b/solution.py
@@ -168,21 +168,26 @@
     mate, far = shift(own, other_core), shift(own, other_half)
     columns = [own, up_a, up_b, down_a, down_b, shift(up_a, z_down), shift(down_a, z_up)]
 
-    def over_x(parts):
-        moved = (
+    def to_x(parts):
+        return [
             shift(parts[1], lambda x, y, z, c: (x + 1, y, z, c)),
             shift(parts[2], lambda x, y, z, c: (x + 2, y, z, c)),
             shift(parts[3], lambda x, y, z, c: (x - 1, y, z, c)),
-        )
+        ]
+
+    def over_x(parts, moved=None):
+        moved = to_x(parts) if moved is None else moved
         return (parts[0] + moved[0].astype(f32)) + (moved[1].astype(f32) + moved[2].astype(f32))
 
     near = gram(scalars, [own, mate], columns)
-    near, far = after((near, far))
-    near_sum = over_x(near)
+    moved = to_x(near)
+    far, _ = after((far, near[0]))
+    near_sum = over_x(near, moved)
     far_one = gram(scalars, [far], columns)
-    far_mate = shift(far, other_core)
-    far_one, far_mate = after((far_one, far_mate))
-    far_two = gram(scalars, [far_mate], columns)
+    far_then, _ = after((far, moved[0]))
+    far_mate = shift(far_then, other_core)
+    late, _ = after((scalars, far_one[0]))
+    far_two = gram(late, [far_mate], columns)
 
     edge = (y == 0) | (y == 3)
 

time: 118 us -> 126 us (1.068)
  waiting for transfers between devices: 54.3 us -> 61.7 us
  starting transfers between devices: 35.3 us -> 36.6 us
    ppermute x24, waiting for transfers between devices: 54.3 us -> 61.7 us  [shift(): return lax.ppermute(array, AXES, pairs)]
    ppermute x24, starting transfers between devices: 35.3 us -> 36.6 us  [shift(): return lax.ppermute(array, AXES, pairs)]
  transfers between devices with their start and end apart: 24 -> 24, of which waited for: 10 -> 13; matrix products, arithmetic and copies ran while one was open for 2% -> 2% of each run, Pallas kernels for 12% -> 11%
where the time goes in v6:
time: 126 us
  waiting for transfers between devices  61.7 us (49%)
  starting transfers between devices  36.6 us (29%)
  Pallas kernels  22.5 us (18%)
  other arithmetic  2.67 us (2%)
  local copies, waits for them, and re-layouts  2.03 us (2%)
    ppermute x24, waiting for transfers between devices, shift(): return lax.ppermute(array, AXES, pairs)  61.7 us
    ppermute x24, starting transfers between devices, shift(): return lax.ppermute(array, AXES, pairs)  36.6 us
    pallas_call x3, Pallas kernels, gram(): pl.pallas_call(functools.partial(gram_kernel, len(rows)), in_specs=[IN_SM...  13.6 us
    pallas_call x1, Pallas kernels, features(): pl.pallas_call(feature_kernel, grid_spec=pltpu.PrefetchScalarGridSpec(num...  8.93 us
  transfers between devices with their start and end apart: 24, of which 13 were waited for; matrix products, arithmetic and copies ran while one was open for 2% of the time, Pallas kernels for 11%

profile of v6, /device:TPU:104, one launch (start us, length us, event | category | flops | bytes accessed | tf_op | source)
XLA Modules:
  0.0 125.7 jit_solution(9277585168104273137)
XLA Ops:
  0.0 8.9 %features.1 = (bf16[32,256,128]{2,1,0:T(8,128)(2,1)S(1)}, bf16[8,256,128]{2,1,0:T(8,128)(2,1)S(1)}, bf16[8,256,128]{2,1,0:T(8,128)(2,1)S(1)}, bf16[8,256,128]{2,1,0:T(8,128)(2,1)S(1)}, bf16[8,256,128]{2,1,0:T(8,128)(2,1)}) custom-call(s32[1]{0:T(128)} %bitcast.7.s_ref, bf16[1,256,64,256]{3,2,1,0:T(8,128)(2,1)} %g_ref.1, bf16[1,256,64,256]{3,2,1,0:T(8,128)(2,1)} %i_ref.1), custom_call_target="tpu_custom_call" | custom-call | flops 1 | bytes 1 | tf_op jit(solution)/shard_map/features/pallas_call | solution.py:56
  8.9 2.3 %collective-permute-start.10 = (bf16[32,256,128]{2,1,0:T(8,128)(2,1)S(1)}, bf16[32,256,128]{2,1,0:T(8,128)(2,1)}, u32[]{:S(2)}, u32[]{:S(2)}) collective-permute-start(bf16[32,256,128]{2,1,0:T(8,128)(2,1)S(1)} %get-tuple-element.26.refs_0_.refs_2_.refs_1_), channel_id=1, source_target_pairs={{0,16},{8,24},{32,48},{40,56},{64,80},{72,88},{96,112},{104,120},{... | collective-permute-start | bytes 6291464 | tf_op jit(solution)/shard_map/ppermute | solution.py:133
  11.2 0.4 collective-permute-start.1
  11.6 0.1 collective-permute-start.2
  11.7 3.1 %collective-permute-start.3 = (bf16[8,256,128]{2,1,0:T(8,128)(2,1)S(1)}, bf16[8,256,128]{2,1,0:T(8,128)(2,1)}, u32[]{:S(2)}, u32[]{:S(2)}) collective-permute-start(bf16[8,256,128]{2,1,0:T(8,128)(2,1)S(1)} %get-tuple-element.29), channel_id=1, source_target_pairs={{0,32},{8,40},{32,64},{40,72},{64,96},{72,104},{96,0},{104,8},{1,3... | collective-permute-start | bytes 1572872 | tf_op jit(solution)/shard_map/ppermute | solution.py:133
  14.9 12.3 %collective-permute-done.1.refs_3_.refs_2_ = bf16[8,256,128]{2,1,0:T(8,128)(2,1)S(1)} collective-permute-done((bf16[8,256,128]{2,1,0:T(8,128)(2,1)S(1)}, bf16[8,256,128]{2,1,0:T(8,128)(2,1)S(1)}, u32[]{:S(2)}, u32[]{:S(2)}) %collective-permute-start.1) | collective-permute-done | bytes 524320 | tf_op jit(solution)/shard_map/ppermute | solution.py:133
  27.2 10.5 %collective-permute-done.2.refs_4_.refs_3_ = bf16[8,256,128]{2,1,0:T(8,128)(2,1)S(1)} collective-permute-done((bf16[8,256,128]{2,1,0:T(8,128)(2,1)S(1)}, bf16[8,256,128]{2,1,0:T(8,128)(2,1)S(1)}, u32[]{:S(2)}, u32[]{:S(2)}) %collective-permute-start.2) | collective-permute-done | bytes 524320 | tf_op jit(solution)/shard_map/ppermute | solution.py:133
  37.7 3.2 %collective-permute-start.6 = (bf16[8,256,128]{2,1,0:T(8,128)(2,1)}, bf16[8,256,128]{2,1,0:T(8,128)(2,1)}, u32[]{:S(2)}, u32[]{:S(2)}) collective-permute-start(bf16[8,256,128]{2,1,0:T(8,128)(2,1)} %collective-permute-done.3.refs_5_.refs_4_), channel_id=1, source_target_pairs={{0,32},{8,40},{32,64},{40,72},{64,96},{72,104},{96,0},{104,8},{1,3... | collective-permute-start | bytes 1572872 | tf_op jit(solution)/shard_map/ppermute | solution.py:133
  41.0 0.1 and_select_fusion
  41.1 0.1 pad_add_fusion.s_ref
  41.1 11.1 %collective-permute-done.5.refs_7_.refs_6_ = bf16[8,256,128]{2,1,0:T(8,128)(2,1)} collective-permute-done((bf16[8,256,128]{2,1,0:T(8,128)(2,1)S(1)}, bf16[8,256,128]{2,1,0:T(8,128)(2,1)}, u32[]{:S(2)}, u32[]{:S(2)}) %collective-permute-start.5) | collective-permute-done | bytes 524320 | tf_op jit(solution)/shard_map/ppermute | solution.py:133
  52.3 5.9 %gram.3 = (f32[512,256]{1,0:T(8,128)S(1)}, bf16[512,256]{1,0:T(8,128)(2,1)S(1)}, bf16[512,256]{1,0:T(8,128)(2,1)S(1)}, bf16[512,256]{1,0:T(8,128)(2,1)}) custom-call(s32[7]{0:T(128)S(1)} %pad_add_fusion.s_ref, bf16[32,256,128]{2,1,0:T(8,128)(2,1)S(1)} %get-tuple-element.26.refs_0_.refs_2_.refs_1_, bf16[32,256,128]{2,1,0:T(8,128)(2,1)} %collective-permute-done.refs_1_, ...), custom_call_target="tpu_custom_call" | custom-call | flops 1 | bytes 1 | tf_op jit(solution)/shard_map/gram/pallas_call | solution.py:106
  58.2 0.8 copy-done
  59.0 1.5 %collective-permute-start.7 = (bf16[512,256]{1,0:T(8,128)(2,1)S(1)}, bf16[512,256]{1,0:T(8,128)(2,1)S(1)}, u32[]{:S(2)}, u32[]{:S(2)}) collective-permute-start(bf16[512,256]{1,0:T(8,128)(2,1)S(1)} %get-tuple-element.32), channel_id=1, source_target_pairs={{0,2},{8,10},{32,34},{40,42},{64,66},{72,74},{96,98},{104,106},{1,... | collective-permute-start | bytes 786440 | tf_op jit(solution)/shard_map/ppermute | solution.py:133
  60.5 6.4 %collective-permute-done.7 = bf16[512,256]{1,0:T(8,128)(2,1)S(1)} collective-permute-done((bf16[512,256]{1,0:T(8,128)(2,1)S(1)}, bf16[512,256]{1,0:T(8,128)(2,1)S(1)}, u32[]{:S(2)}, u32[]{:S(2)}) %collective-permute-start.7) | collective-permute-done | bytes 262176 | tf_op jit(solution)/shard_map/ppermute | solution.py:133
  66.9 1.5 %collective-permute-start.9 = (bf16[512,256]{1,0:T(8,128)(2,1)}, bf16[512,256]{1,0:T(8,128)(2,1)}, u32[]{:S(2)}, u32[]{:S(2)}) collective-permute-start(bf16[512,256]{1,0:T(8,128)(2,1)} %get-tuple-element.34), channel_id=1, source_target_pairs={{0,6},{8,14},{32,38},{40,46},{64,70},{72,78},{96,102},{104,110},{1... | collective-permute-start | bytes 786440 | tf_op jit(solution)/shard_map/ppermute | solution.py:133
  68.5 1.0 collective-permute-start.8
  69.5 3.9 %gram.4 = (f32[256,256]{1,0:T(8,128)S(1)}, bf16[256,256]{1,0:T(8,128)(2,1)S(1)}, bf16[256,256]{1,0:T(8,128)(2,1)S(1)}, bf16[256,256]{1,0:T(8,128)(2,1)S(1)}) custom-call(s32[7]{0:T(128)S(1)} %pad_add_fusion.s_ref, bf16[32,256,128]{2,1,0:T(8,128)(2,1)} %collective-permute-done.10.refs_0_, bf16[32,256,128]{2,1,0:T(8,128)(2,1)S(1)} %get-tuple-element.26.refs_0_.refs_2_.refs_1_, ...), custom_call_target="tpu_custom_call" | custom-call | flops 1 | bytes 1 | tf_op jit(solution)/shard_map/gram/pallas_call | solution.py:106
  73.3 2.2 %collective-permute-start.13 = (bf16[256,256]{1,0:T(8,128)(2,1)S(1)}, bf16[256,256]{1,0:T(8,128)(2,1)S(1)}, u32[]{:S(2)}, u32[]{:S(2)}) collective-permute-start(bf16[256,256]{1,0:T(8,128)(2,1)S(1)} %get-tuple-element.39), channel_id=1, source_target_pairs={{0,6},{8,14},{32,38},{40,46},{64,70},{72,78},{96,102},{104,110},{1... | collective-permute-start | bytes 393224 | tf_op jit(solution)/shard_map/ppermute | solution.py:133
  75.6 0.6 collective-permute-start.12
  76.2 0.2 collective-permute-done.9
  76.4 1.0 collective-permute-start.11
  77.4 1.2 collective-permute-done.8
  78.5 1.1 add_add_fusion
  79.7 5.0 %collective-permute-done.13 = bf16[256,256]{1,0:T(8,128)(2,1)S(1)} collective-permute-done((bf16[256,256]{1,0:T(8,128)(2,1)S(1)}, bf16[256,256]{1,0:T(8,128)(2,1)S(1)}, u32[]{:S(2)}, u32[]{:S(2)}) %collective-permute-start.13) | collective-permute-done | bytes 131104 | tf_op jit(solution)/shard_map/ppermute | solution.py:133
  84.7 0.2 collective-permute-done.11
  85.0 0.1 select_convert_fusion.1
  85.0 1.6 %collective-permute-start.14 = (bf16[256,256]{1,0:T(8,128)(2,1)S(1)}, bf16[256,256]{1,0:T(8,128)(2,1)S(1)}, u32[]{:S(2)}, u32[]{:S(2)}) collective-permute-start(bf16[256,256]{1,0:T(8,128)(2,1)S(1)} %select_convert_fusion.1), channel_id=1, source_target_pairs={{0,1},{8,9},{32,33},{40,41},{64,65},{72,73},{96,97},{104,105},{1,0... | collective-permute-start | bytes 393224 | tf_op jit(solution)/shard_map/ppermute | solution.py:133
  86.7 3.8 %gram.5 = (f32[256,256]{1,0:T(8,128)S(1)}, bf16[256,256]{1,0:T(8,128)(2,1)S(1)}, bf16[256,256]{1,0:T(8,128)(2,1)S(1)}, bf16[256,256]{1,0:T(8,128)(2,1)S(1)}) custom-call(s32[7]{0:T(128)S(1)} %pad_add_fusion.s_ref, bf16[32,256,128]{2,1,0:T(8,128)(2,1)} %collective-permute-done.17.refs_0_, bf16[32,256,128]{2,1,0:T(8,128)(2,1)S(1)} %get-tuple-element.26.refs_0_.refs_2_.refs_1_, ...), custom_call_target="tpu_custom_call" | custom-call | flops 1 | bytes 1 | tf_op jit(solution)/shard_map/gram/pallas_call | solution.py:106
  90.5 5.0 %collective-permute-start.20 = (bf16[256,256]{1,0:T(8,128)(2,1)S(1)}, bf16[256,256]{1,0:T(8,128)(2,1)S(1)}, u32[]{:S(2)}, u32[]{:S(2)}) collective-permute-start(bf16[256,256]{1,0:T(8,128)(2,1)S(1)} %get-tuple-element.45), channel_id=1, source_target_pairs={{0,6},{8,14},{32,38},{40,46},{64,70},{72,78},{96,102},{104,110},{1... | collective-permute-start | bytes 393224 | tf_op jit(solution)/shard_map/ppermute | solution.py:133
  95.4 0.6 collective-permute-start.19
  96.0 0.4 collective-permute-start.18
  96.4 0.1 fusion.3
  96.5 4.1 %collective-permute-done.20 = bf16[256,256]{1,0:T(8,128)(2,1)S(1)} collective-permute-done((bf16[256,256]{1,0:T(8,128)(2,1)S(1)}, bf16[256,256]{1,0:T(8,128)(2,1)S(1)}, u32[]{:S(2)}, u32[]{:S(2)}) %collective-permute-start.20) | collective-permute-done | bytes 131104 | tf_op jit(solution)/shard_map/ppermute | solution.py:133
  100.6 2.4 %collective-permute-done.19 = bf16[256,256]{1,0:T(8,128)(2,1)S(1)} collective-permute-done((bf16[256,256]{1,0:T(8,128)(2,1)S(1)}, bf16[256,256]{1,0:T(8,128)(2,1)S(1)}, u32[]{:S(2)}, u32[]{:S(2)}) %collective-permute-start.19) | collective-permute-done | bytes 131104 | tf_op jit(solution)/shard_map/ppermute | solution.py:133
  102.9 1.3 %collective-permute-done.18 = bf16[256,256]{1,0:T(8,128)(2,1)S(1)} collective-permute-done((bf16[256,256]{1,0:T(8,128)(2,1)S(1)}, bf16[256,256]{1,0:T(8,128)(2,1)S(1)}, u32[]{:S(2)}, u32[]{:S(2)}) %collective-permute-start.18) | collective-permute-done | bytes 131104 | tf_op jit(solution)/shard_map/ppermute | solution.py:133
  104.4 0.6 collective-permute-start.21
  104.9 2.2 %collective-permute-start.15 = (bf16[256,256]{1,0:T(8,128)(2,1)S(1)}, bf16[256,256]{1,0:T(8,128)(2,1)S(1)}, u32[]{:S(2)}, u32[]{:S(2)}) collective-permute-start(bf16[256,256]{1,0:T(8,128)(2,1)S(1)} %get-tuple-element.47), channel_id=1, source_target_pairs={{1,16},{9,24},{33,48},{41,56},{65,80},{73,88},{97,112},{105,120},{... | collective-permute-start | bytes 393224 | tf_op jit(solution)/shard_map/ppermute | solution.py:133
  107.1 4.8 %collective-permute-start.16 = (bf16[256,256]{1,0:T(8,128)(2,1)S(1)}, bf16[256,256]{1,0:T(8,128)(2,1)S(1)}, u32[]{:S(2)}, u32[]{:S(2)}) collective-permute-start(bf16[256,256]{1,0:T(8,128)(2,1)S(1)} %get-tuple-element.47), channel_id=1, source_target_pairs={{32,2},{40,10},{64,4},{72,12},{96,6},{104,14},{33,3},{41,11},{65,5... | collective-permute-start | bytes 393224 | tf_op jit(solution)/shard_map/ppermute | solution.py:133
  112.0 1.0 add_convert_fusion
  113.0 4.4 %collective-permute-start.23 = (bf16[256,256]{1,0:T(8,128)(2,1)S(1)}, bf16[256,256]{1,0:T(8,128)(2,1)S(1)}, u32[]{:S(2)}, u32[]{:S(2)}) collective-permute-start(bf16[256,256]{1,0:T(8,128)(2,1)S(1)} %add_convert_fusion), channel_id=1, source_target_pairs={{32,2},{40,10},{64,4},{72,12},{96,6},{104,14},{33,3},{41,11},{65,5... | collective-permute-start | bytes 393224 | tf_op jit(solution)/shard_map/ppermute | solution.py:133
  117.3 0.1 copy.4
  117.4 0.1 collective-permute-start.22
  117.6 0.1 copy.3
  117.7 1.5 %collective-permute-done.16 = bf16[256,256]{1,0:T(8,128)(2,1)S(1)} collective-permute-done((bf16[256,256]{1,0:T(8,128)(2,1)S(1)}, bf16[256,256]{1,0:T(8,128)(2,1)S(1)}, u32[]{:S(2)}, u32[]{:S(2)}) %collective-permute-start.16) | collective-permute-done | bytes 131104 | tf_op jit(solution)/shard_map/ppermute | solution.py:133
  119.2 5.4 %collective-permute-done.23 = bf16[256,256]{1,0:T(8,128)(2,1)S(1)} collective-permute-done((bf16[256,256]{1,0:T(8,128)(2,1)S(1)}, bf16[256,256]{1,0:T(8,128)(2,1)S(1)}, u32[]{:S(2)}, u32[]{:S(2)}) %collective-permute-start.23) | collective-permute-done | bytes 131104 | tf_op jit(solution)/shard_map/ppermute | solution.py:133
  124.5 0.1 fusion.1
  124.7 1.0 copy.5
  (28 shorter events, 0.2 us)
Async XLA Ops:
  8.9 43.4 %collective-permute-start = (bf16[32,256,128]{2,1,0:T(8,128)(2,1)S(1)}, bf16[32,256,128]{2,1,0:T(8,128)(2,1)}, u32[]{:S(2)}, u32[]{:S(2)}) collective-permute-start(bf16[32,256,128]{2,1,0:T(8,128)(2,1)S(1)} %get-tuple-element.26.refs_0_.refs_2_.refs_1_), channel_id=1, source_target_pairs={{0,8},{8,0},{32,40},{40,32},{64,72},{72,64},{96,104},{104,96},{1,9... | collective-permute-start | bytes 6291464 | tf_op jit(solution)/shard_map/ppermute | solution.py:133
  8.9 51.6 %collective-permute-start.10 = (bf16[32,256,128]{2,1,0:T(8,128)(2,1)S(1)}, bf16[32,256,128]{2,1,0:T(8,128)(2,1)}, u32[]{:S(2)}, u32[]{:S(2)}) collective-permute-start(bf16[32,256,128]{2,1,0:T(8,128)(2,1)S(1)} %get-tuple-element.26.refs_0_.refs_2_.refs_1_), channel_id=1, source_target_pairs={{0,16},{8,24},{32,48},{40,56},{64,80},{72,88},{96,112},{104,120},{... | collective-permute-start | bytes 6291464 | tf_op jit(solution)/shard_map/ppermute | solution.py:133
  11.2 16.0 %collective-permute-start.1 = (bf16[8,256,128]{2,1,0:T(8,128)(2,1)S(1)}, bf16[8,256,128]{2,1,0:T(8,128)(2,1)S(1)}, u32[]{:S(2)}, u32[]{:S(2)}) collective-permute-start(bf16[8,256,128]{2,1,0:T(8,128)(2,1)S(1)} %get-tuple-element.27), channel_id=1, source_target_pairs={{0,96},{8,104},{32,0},{40,8},{64,32},{72,40},{96,64},{104,72},{1,9... | collective-permute-start | bytes 1572872 | tf_op jit(solution)/shard_map/ppermute | solution.py:133
  11.6 26.1 %collective-permute-start.2 = (bf16[8,256,128]{2,1,0:T(8,128)(2,1)S(1)}, bf16[8,256,128]{2,1,0:T(8,128)(2,1)S(1)}, u32[]{:S(2)}, u32[]{:S(2)}) collective-permute-start(bf16[8,256,128]{2,1,0:T(8,128)(2,1)S(1)} %get-tuple-element.28), channel_id=1, source_target_pairs={{0,96},{8,104},{32,0},{40,8},{64,32},{72,40},{96,64},{104,72},{1,9... | collective-permute-start | bytes 1572872 | tf_op jit(solution)/shard_map/ppermute | solution.py:133
  11.7 26.0 %collective-permute-start.3 = (bf16[8,256,128]{2,1,0:T(8,128)(2,1)S(1)}, bf16[8,256,128]{2,1,0:T(8,128)(2,1)}, u32[]{:S(2)}, u32[]{:S(2)}) collective-permute-start(bf16[8,256,128]{2,1,0:T(8,128)(2,1)S(1)} %get-tuple-element.29), channel_id=1, source_target_pairs={{0,32},{8,40},{32,64},{40,72},{64,96},{72,104},{96,0},{104,8},{1,3... | collective-permute-start | bytes 1572872 | tf_op jit(solution)/shard_map/ppermute | solution.py:133
  27.2 13.9 %collective-permute-start.4 = (bf16[8,256,128]{2,1,0:T(8,128)(2,1)}, bf16[8,256,128]{2,1,0:T(8,128)(2,1)}, u32[]{:S(2)}, u32[]{:S(2)}) collective-permute-start(bf16[8,256,128]{2,1,0:T(8,128)(2,1)} %get-tuple-element.30), channel_id=1, source_target_pairs={{0,32},{8,40},{32,64},{40,72},{64,96},{72,104},{96,0},{104,8},{1,3... | collective-permute-start | bytes 1572872 | tf_op jit(solution)/shard_map/ppermute | solution.py:133
  37.7 14.6 %collective-permute-start.5 = (bf16[8,256,128]{2,1,0:T(8,128)(2,1)S(1)}, bf16[8,256,128]{2,1,0:T(8,128)(2,1)}, u32[]{:S(2)}, u32[]{:S(2)}) collective-permute-start(bf16[8,256,128]{2,1,0:T(8,128)(2,1)S(1)} %collective-permute-done.1.refs_3_.refs_2_), channel_id=1, source_target_pairs={{0,96},{8,104},{32,0},{40,8},{64,32},{72,40},{96,64},{104,72},{1,9... | collective-permute-start | bytes 1572872 | tf_op jit(solution)/shard_map/ppermute | solution.py:133
  37.7 14.5 %collective-permute-start.6 = (bf16[8,256,128]{2,1,0:T(8,128)(2,1)}, bf16[8,256,128]{2,1,0:T(8,128)(2,1)}, u32[]{:S(2)}, u32[]{:S(2)}) collective-permute-start(bf16[8,256,128]{2,1,0:T(8,128)(2,1)} %collective-permute-done.3.refs_5_.refs_4_), channel_id=1, source_target_pairs={{0,32},{8,40},{32,64},{40,72},{64,96},{72,104},{96,0},{104,8},{1,3... | collective-permute-start | bytes 1572872 | tf_op jit(solution)/shard_map/ppermute | solution.py:133
  58.2 0.8 copy-start
  59.0 7.9 %collective-permute-start.7 = (bf16[512,256]{1,0:T(8,128)(2,1)S(1)}, bf16[512,256]{1,0:T(8,128)(2,1)S(1)}, u32[]{:S(2)}, u32[]{:S(2)}) collective-permute-start(bf16[512,256]{1,0:T(8,128)(2,1)S(1)} %get-tuple-element.32), channel_id=1, source_target_pairs={{0,2},{8,10},{32,34},{40,42},{64,66},{72,74},{96,98},{104,106},{1,... | collective-permute-start | bytes 786440 | tf_op jit(solution)/shard_map/ppermute | solution.py:133
  66.9 1.6 %copy-start.3 = (bf16[512,256]{1,0:T(8,128)(2,1)}, bf16[512,256]{1,0:T(8,128)(2,1)S(1)}, u32[]{:S(2)}) copy-start(bf16[512,256]{1,0:T(8,128)(2,1)S(1)} %collective-permute-done.7) | copy-start | bytes 786436
  66.9 19.7 %collective-permute-start.17 = (bf16[32,256,128]{2,1,0:T(8,128)(2,1)}, bf16[32,256,128]{2,1,0:T(8,128)(2,1)}, u32[]{:S(2)}, u32[]{:S(2)}) collective-permute-start(bf16[32,256,128]{2,1,0:T(8,128)(2,1)} %collective-permute-done.10.refs_0_), channel_id=1, source_target_pairs={{0,8},{8,0},{32,40},{40,32},{64,72},{72,64},{96,104},{104,96},{1,9... | collective-permute-start | bytes 6291464 | tf_op jit(solution)/shard_map/ppermute | solution.py:133
  66.9 9.4 %collective-permute-start.9 = (bf16[512,256]{1,0:T(8,128)(2,1)}, bf16[512,256]{1,0:T(8,128)(2,1)}, u32[]{:S(2)}, u32[]{:S(2)}) collective-permute-start(bf16[512,256]{1,0:T(8,128)(2,1)} %get-tuple-element.34), channel_id=1, source_target_pairs={{0,6},{8,14},{32,38},{40,46},{64,70},{72,78},{96,102},{104,110},{1... | collective-permute-start | bytes 786440 | tf_op jit(solution)/shard_map/ppermute | solution.py:133
  68.5 10.0 %collective-permute-start.8 = (bf16[512,256]{1,0:T(8,128)(2,1)S(1)}, bf16[512,256]{1,0:T(8,128)(2,1)}, u32[]{:S(2)}, u32[]{:S(2)}) collective-permute-start(bf16[512,256]{1,0:T(8,128)(2,1)S(1)} %get-tuple-element.33), channel_id=1, source_target_pairs={{0,4},{8,12},{32,36},{40,44},{64,68},{72,76},{96,100},{104,108},{1... | collective-permute-start | bytes 786440 | tf_op jit(solution)/shard_map/ppermute | solution.py:133
  69.5 9.1 %copy-start.1 = (f32[512,256]{1,0:T(8,128)S(1)}, f32[512,256]{1,0:T(8,128)}, u32[]{:S(2)}) copy-start(f32[512,256]{1,0:T(8,128)} %copy-done) | copy-start | bytes 1572868
  69.5 9.1 %copy-start.4 = (bf16[512,256]{1,0:T(8,128)(2,1)S(1)}, bf16[512,256]{1,0:T(8,128)(2,1)}, u32[]{:S(2)}) copy-start(bf16[512,256]{1,0:T(8,128)(2,1)} %copy-done.3) | copy-start | bytes 786436
  73.3 11.4 %collective-permute-start.13 = (bf16[256,256]{1,0:T(8,128)(2,1)S(1)}, bf16[256,256]{1,0:T(8,128)(2,1)S(1)}, u32[]{:S(2)}, u32[]{:S(2)}) collective-permute-start(bf16[256,256]{1,0:T(8,128)(2,1)S(1)} %get-tuple-element.39), channel_id=1, source_target_pairs={{0,6},{8,14},{32,38},{40,46},{64,70},{72,78},{96,102},{104,110},{1... | collective-permute-start | bytes 393224 | tf_op jit(solution)/shard_map/ppermute | solution.py:133
  75.6 9.2 %collective-permute-start.12 = (bf16[256,256]{1,0:T(8,128)(2,1)S(1)}, bf16[256,256]{1,0:T(8,128)(2,1)S(1)}, u32[]{:S(2)}, u32[]{:S(2)}) collective-permute-start(bf16[256,256]{1,0:T(8,128)(2,1)S(1)} %get-tuple-element.38), channel_id=1, source_target_pairs={{0,4},{8,12},{32,36},{40,44},{64,68},{72,76},{96,100},{104,108},{1... | collective-permute-start | bytes 393224 | tf_op jit(solution)/shard_map/ppermute | solution.py:133
  76.4 8.6 %collective-permute-start.11 = (bf16[256,256]{1,0:T(8,128)(2,1)S(1)}, bf16[256,256]{1,0:T(8,128)(2,1)S(1)}, u32[]{:S(2)}, u32[]{:S(2)}) collective-permute-start(bf16[256,256]{1,0:T(8,128)(2,1)S(1)} %get-tuple-element.37), channel_id=1, source_target_pairs={{0,2},{8,10},{32,34},{40,42},{64,66},{72,74},{96,98},{104,106},{1,... | collective-permute-start | bytes 393224 | tf_op jit(solution)/shard_map/ppermute | solution.py:133
  79.7 24.7 %copy-start.2 = (f32[512,256]{1,0:T(8,128)}, f32[512,256]{1,0:T(8,128)S(1)}, u32[]{:S(2)}) copy-start(f32[512,256]{1,0:T(8,128)S(1)} %add_add_fusion) | copy-start | bytes 1572868
  85.0 11.4 %collective-permute-start.14 = (bf16[256,256]{1,0:T(8,128)(2,1)S(1)}, bf16[256,256]{1,0:T(8,128)(2,1)S(1)}, u32[]{:S(2)}, u32[]{:S(2)}) collective-permute-start(bf16[256,256]{1,0:T(8,128)(2,1)S(1)} %select_convert_fusion.1), channel_id=1, source_target_pairs={{0,1},{8,9},{32,33},{40,41},{64,65},{72,73},{96,97},{104,105},{1,0... | collective-permute-start | bytes 393224 | tf_op jit(solution)/shard_map/ppermute | solution.py:133
  90.5 10.1 %collective-permute-start.20 = (bf16[256,256]{1,0:T(8,128)(2,1)S(1)}, bf16[256,256]{1,0:T(8,128)(2,1)S(1)}, u32[]{:S(2)}, u32[]{:S(2)}) collective-permute-start(bf16[256,256]{1,0:T(8,128)(2,1)S(1)} %get-tuple-element.45), channel_id=1, source_target_pairs={{0,6},{8,14},{32,38},{40,46},{64,70},{72,78},{96,102},{104,110},{1... | collective-permute-start | bytes 393224 | tf_op jit(solution)/shard_map/ppermute | solution.py:133
  95.4 7.5 %collective-permute-start.19 = (bf16[256,256]{1,0:T(8,128)(2,1)S(1)}, bf16[256,256]{1,0:T(8,128)(2,1)S(1)}, u32[]{:S(2)}, u32[]{:S(2)}) collective-permute-start(bf16[256,256]{1,0:T(8,128)(2,1)S(1)} %get-tuple-element.44), channel_id=1, source_target_pairs={{0,4},{8,12},{32,36},{40,44},{64,68},{72,76},{96,100},{104,108},{1... | collective-permute-start | bytes 393224 | tf_op jit(solution)/shard_map/ppermute | solution.py:133
  96.0 8.3 %collective-permute-start.18 = (bf16[256,256]{1,0:T(8,128)(2,1)S(1)}, bf16[256,256]{1,0:T(8,128)(2,1)S(1)}, u32[]{:S(2)}, u32[]{:S(2)}) collective-permute-start(bf16[256,256]{1,0:T(8,128)(2,1)S(1)} %get-tuple-element.43), channel_id=1, source_target_pairs={{0,2},{8,10},{32,34},{40,42},{64,66},{72,74},{96,98},{104,106},{1,... | collective-permute-start | bytes 393224 | tf_op jit(solution)/shard_map/ppermute | solution.py:133
  104.4 7.6 %collective-permute-start.21 = (bf16[256,256]{1,0:T(8,128)(2,1)S(1)}, bf16[256,256]{1,0:T(8,128)(2,1)S(1)}, u32[]{:S(2)}, u32[]{:S(2)}) collective-permute-start(bf16[256,256]{1,0:T(8,128)(2,1)S(1)} %select_convert_fusion), channel_id=1, source_target_pairs={{0,1},{8,9},{32,33},{40,41},{64,65},{72,73},{96,97},{104,105},{1,0... | collective-permute-start | bytes 393224 | tf_op jit(solution)/shard_map/ppermute | solution.py:133
  104.9 12.6 %collective-permute-start.15 = (bf16[256,256]{1,0:T(8,128)(2,1)S(1)}, bf16[256,256]{1,0:T(8,128)(2,1)S(1)}, u32[]{:S(2)}, u32[]{:S(2)}) collective-permute-start(bf16[256,256]{1,0:T(8,128)(2,1)S(1)} %get-tuple-element.47), channel_id=1, source_target_pairs={{1,16},{9,24},{33,48},{41,56},{65,80},{73,88},{97,112},{105,120},{... | collective-permute-start | bytes 393224 | tf_op jit(solution)/shard_map/ppermute | solution.py:133
  107.1 12.0 %collective-permute-start.16 = (bf16[256,256]{1,0:T(8,128)(2,1)S(1)}, bf16[256,256]{1,0:T(8,128)(2,1)S(1)}, u32[]{:S(2)}, u32[]{:S(2)}) collective-permute-start(bf16[256,256]{1,0:T(8,128)(2,1)S(1)} %get-tuple-element.47), channel_id=1, source_target_pairs={{32,2},{40,10},{64,4},{72,12},{96,6},{104,14},{33,3},{41,11},{65,5... | collective-permute-start | bytes 393224 | tf_op jit(solution)/shard_map/ppermute | solution.py:133
  113.0 11.6 %collective-permute-start.23 = (bf16[256,256]{1,0:T(8,128)(2,1)S(1)}, bf16[256,256]{1,0:T(8,128)(2,1)S(1)}, u32[]{:S(2)}, u32[]{:S(2)}) collective-permute-start(bf16[256,256]{1,0:T(8,128)(2,1)S(1)} %add_convert_fusion), channel_id=1, source_target_pairs={{32,2},{40,10},{64,4},{72,12},{96,6},{104,14},{33,3},{41,11},{65,5... | collective-permute-start | bytes 393224 | tf_op jit(solution)/shard_map/ppermute | solution.py:133
  117.4 7.1 %collective-permute-start.22 = (bf16[256,256]{0,1:T(8,128)(2,1)S(1)}, bf16[256,256]{0,1:T(8,128)(2,1)S(1)}, u32[]{:S(2)}, u32[]{:S(2)}) collective-permute-start(bf16[256,256]{0,1:T(8,128)(2,1)S(1)} %copy.4), channel_id=1, source_target_pairs={{0,8},{8,0},{32,40},{40,32},{64,72},{72,64},{96,104},{104,96},{1,2... | collective-permute-start | bytes 393224 | tf_op jit(solution)/shard_map/ppermute | solution.py:133
